TPU v7x, 32 devices: a whole 2x2x4 slice. The times are simulated.
32 devices in a mesh: frame: 4 (over x, core), clip: 8 (over z, y).
Axes of the slice: x: 2, y: 2, z: 4, core: 2. Of those that a mesh axis runs over, the one named last changes fastest.
Arguments:
- latents: float32 [8, 8, 256, 16], P('clip', 'frame'), may hold values from -6 to 6
- noise: float32 [8, 8, 256, 16], P('clip', 'frame'), may hold values from -6 to 6
- timesteps: int32 [8], P('clip'), may hold values from 0 to 999
- captions: bfloat16 [8, 120, 4096], P('clip'), may hold values from -6 to 6
- cap_lengths: int32 [8], P('clip'), may hold values from 30 to 120, as said below
- null_flags: int32 [8], P('clip'), may hold values 0 or 1
- sample_weight: float32 [8], P('clip'), may hold values from 0.8 to 6.25
- embed_w: float32 [16158720], P('clip'), may hold values from -3 to 3
- attend_w: float32 [15925248], P('clip'), may hold values from -3 to 3
- dense_w: float32 [10616832], P('clip'), may hold values from -3 to 3
- vector_w: float32 [38032], replicated, may hold values from -1 to 2
- embed_m: float32 [16158720], P('clip'), may hold values from -0.00390625 to 0.00390625
- attend_m: float32 [15925248], P('clip'), may hold values from -0.0009765625 to 0.0009765625
- dense_m: float32 [10616832], P('clip'), may hold values from -0.0009765625 to 0.0009765625
- vector_m: float32 [38032], replicated, may hold values from -0.009765625 to 0.009765625
- embed_v: float32 [16158720], P('clip'), may hold values from 7.019378e-07 to 2.8077511e-06
- attend_v: float32 [15925248], P('clip'), may hold values from 2.3397925e-08 to 9.35917e-08
- dense_v: float32 [10616832], P('clip'), may hold values from 2.3397925e-08 to 9.35917e-08
- vector_v: float32 [38032], replicated, may hold values from 2.3397924e-06 to 9.35917e-06
- embed_e: float32 [16158720], P('clip'), may hold values from -3 to 3
- attend_e: float32 [15925248], P('clip'), may hold values from -3 to 3
- dense_e: float32 [10616832], P('clip'), may hold values from -3 to 3
- vector_e: float32 [38032], replicated, may hold values from -1 to 2
Outputs:
- loss_sum: float32 [], replicated
- weight_total: float32 [], replicated
- grad_norm: float32 [], replicated
- embed_new: float32 [16158720], P('clip')
- attend_new: float32 [15925248], P('clip')
- dense_new: float32 [10616832], P('clip')
- vector_new: float32 [38032], replicated
- embed_first: float32 [16158720], P('clip')
- attend_first: float32 [15925248], P('clip')
- dense_first: float32 [10616832], P('clip')
- vector_first: float32 [38032], replicated
- embed_second: float32 [16158720], P('clip')
- attend_second: float32 [15925248], P('clip')
- dense_second: float32 [10616832], P('clip')
- vector_second: float32 [38032], replicated
- embed_average: float32 [16158720], P('clip')
- attend_average: float32 [15925248], P('clip')
- dense_average: float32 [10616832], P('clip')
- vector_average: float32 [38032], replicated
Inputs may be any that keep to these rules, and one draw needn't show every extreme that they name: `cap_lengths`: in every draw one clip has 120 valid caption tokens and another has 30.
All inputs are finite; a program needn't handle non-finite values. No bound on the sum of `null_flags` on one device may be relied on, other than what follows from the above.
Results may differ from a plain program's by a relative error of at most 0.0017.
The roundings to bfloat16 on the way count: a program that leaves them out, or rounds other values in their place, can miss the bound.
Values may be sent and summed in bfloat16 or wider, within the bound.
A program may use at most 960 MiB of HBM per device.

v0:
```python
import math

import jax
import jax.numpy as jnp
from jax import lax
from jax.sharding import PartitionSpec as P

D = 1152
HEADS = 16
MLP = 4608
CAPW = 4096
L_CAP = 120
TFREQ = 256
PATCH_VALUES = 16
PGRID = 16
STEP = 10


NORM_FLOOR = 1e-06
CLIP_LIMIT = 1.0
SNR_LIMIT = 5.0
BETA_FIRST = 0.5
BETA_SECOND = 0.5
LEARN_RATE = 0.02
WEIGHT_DECAY = 0.01
ADAM_FLOOR = 1e-08
AVERAGE_KEEP = 0.9999
MASKED_SCORE = -1e30


def embed_shapes():
    return [
        (PATCH_VALUES, D),
        (TFREQ, D),
        (D, D),
        (D, 6 * D),
        (CAPW, D),
        (D, D),
        (D, PATCH_VALUES),
        (L_CAP, CAPW),
    ]


def attend_shapes():
    return [(D, 3 * D), (D, D), (D, 3 * D), (D, D), (D, D), (D, 2 * D), (D, D)]


def dense_shapes():
    return [(D, MLP), (MLP, D)]


def vector_shapes():
    return [(D,)] * 3 + [(6 * D,)] + [(D,)] * 11 + [(MLP,), (D,), (PATCH_VALUES,), (6, D), (2, D)]


def split_flat(flat, shapes):
    pieces = []
    offset = 0
    for extent in shapes:
        length = math.prod(extent)
        pieces.append(flat[offset : offset + length].reshape(extent))
        offset += length
    return pieces


def flatten_all(pieces):
    return jnp.concatenate([piece.reshape(-1) for piece in pieces])


def reduce_group(grad):
    n_clip = lax.axis_size("clip")
    n_frame = lax.axis_size("frame")
    reorder = grad.reshape(n_clip, n_frame, -1).swapaxes(0, 1).reshape(-1)
    share = lax.psum_scatter(reorder, ("frame", "clip"), scatter_dimension=0, tiled=True)
    return lax.all_gather(share, "frame", axis=0, tiled=True)


def sincos(places, width):
    half = width // 2
    omega = jnp.exp(-math.log(10000.0) * jnp.arange(half, dtype=jnp.float32) / half)
    angle = places.astype(jnp.float32)[..., None] * omega
    return jnp.concatenate([jnp.sin(angle), jnp.cos(angle)], -1)


def modulate(hidden, shift, scale):
    center = hidden - jnp.mean(hidden, -1, keepdims=True)
    normed = center * lax.rsqrt(jnp.mean(center * center, -1, keepdims=True) + NORM_FLOOR)
    return normed * (1.0 + scale) + shift


def gelu_tanh(value):
    return jax.nn.gelu(value, approximate=True)


def matmul_low(left, right):
    return lax.dot_general(
        left, right, (((left.ndim - 1,), (0,)), ((), ())), preferred_element_type=jnp.float32
    )


def halves(value):
    upper = value.astype(jnp.bfloat16)
    return (upper, (value - upper.astype(jnp.float32)).astype(jnp.bfloat16))


def back_low(grads, weight):
    return lax.dot_general(
        grads, weight, (((grads.ndim - 1,), (1,)), ((), ())), preferred_element_type=jnp.float32
    )


def back_split(grads, weight):
    upper, lower = halves(grads)
    return back_low(upper, weight) + back_low(lower, weight)


def weight_grad(inputs, grads):
    left = inputs.reshape(-1, inputs.shape[-1])
    right = grads.reshape(-1, grads.shape[-1])
    return lax.dot_general(
        left, right, (((0,), (0,)), ((), ())), preferred_element_type=jnp.float32
    )


def weight_split(inputs, grads):
    upper, lower = halves(grads)
    return weight_grad(inputs, upper) + weight_grad(inputs, lower)


def bias_grad(grads):
    return jnp.sum(grads.astype(jnp.float32).reshape(-1, grads.shape[-1]), 0)


def heads_of(tensor, batch):
    return tensor.reshape(batch, -1, HEADS, tensor.shape[-1] // HEADS)


def split_qkv(merged, bias_q, bias_v):
    width = merged.shape[-1] // 3
    return (
        (merged[..., :width] + bias_q).astype(jnp.bfloat16),
        merged[..., width : 2 * width].astype(jnp.bfloat16),
        (merged[..., 2 * width :] + bias_v).astype(jnp.bfloat16),
    )


def attend_scores(queries, key_rows, mask):
    scores = jnp.einsum("bqhe,bkhe->bhqk", queries, key_rows, preferred_element_type=jnp.float32)
    scores = scores * queries.shape[-1] ** (-0.5)
    if mask is not None:
        scores = jnp.where(mask[:, None, None, :], scores, MASKED_SCORE)
    return scores


def attend_forward(queries, key_rows, values, mask):
    scores = attend_scores(queries, key_rows, mask)
    summit = jnp.max(scores, -1, keepdims=True)
    powers = jnp.exp(scores - summit)
    totals = jnp.sum(powers, -1, keepdims=True)
    probs = (powers / totals).astype(jnp.bfloat16)
    output = jnp.einsum("bhqk,bkhe->bqhe", probs, values, preferred_element_type=jnp.float32)
    return (output.astype(jnp.bfloat16), summit + jnp.log(totals))


def attend_backward(queries, key_rows, values, mask, log_total, grad_out):
    scale = queries.shape[-1] ** (-0.5)
    probs = jnp.exp(attend_scores(queries, key_rows, mask) - log_total)
    grad_probs = jnp.einsum("bqhe,bkhe->bhqk", grad_out, values, preferred_element_type=jnp.float32)
    grad_scores = (probs * (grad_probs - jnp.sum(probs * grad_probs, -1, keepdims=True))).astype(
        jnp.bfloat16
    )
    grad_query = (
        jnp.einsum("bhqk,bkhe->bqhe", grad_scores, key_rows, preferred_element_type=jnp.float32)
        * scale
    )
    grad_keys = (
        jnp.einsum("bhqk,bqhe->bkhe", grad_scores, queries, preferred_element_type=jnp.float32)
        * scale
    )
    grad_values = jnp.einsum(
        "bhqk,bqhe->bkhe", probs.astype(jnp.bfloat16), grad_out, preferred_element_type=jnp.float32
    )
    return (grad_query, grad_keys, grad_values)


def unpack_all(gathered):
    return (
        split_flat(gathered[0], embed_shapes()),
        split_flat(gathered[1], attend_shapes()),
        split_flat(gathered[2], dense_shapes()),
    )


def adam_step(master, grad, first, second, average, factor):
    keep = min(AVERAGE_KEEP, (1.0 + STEP) / (10.0 + STEP))
    grad = grad * factor
    first = BETA_FIRST * first + (1.0 - BETA_FIRST) * grad
    second = BETA_SECOND * second + (1.0 - BETA_SECOND) * grad * grad
    moved = (
        first
        / (1.0 - BETA_FIRST**STEP)
        / (jnp.sqrt(second / (1.0 - BETA_SECOND**STEP)) + ADAM_FLOOR)
    )
    master = master - LEARN_RATE * (moved + WEIGHT_DECAY * master)
    return (master, first, second, keep * average + (1.0 - keep) * master)


def shards(
    latents,
    noise,
    timesteps,
    captions,
    cap_lengths,
    null_flags,
    sample_weight,
    embed_w,
    attend_w,
    dense_w,
    vector_w,
    embed_m,
    attend_m,
    dense_m,
    vector_m,
    embed_v,
    attend_v,
    dense_v,
    vector_v,
    embed_e,
    attend_e,
    dense_e,
    vector_e,
):
    clip_dev, frame_dev, patches = (latents.shape[0], latents.shape[1], latents.shape[2])
    n_frame = lax.axis_size("frame")
    n_clip = lax.axis_size("clip")
    local_pos = patches // n_frame
    gathered = (
        lax.all_gather(embed_w.astype(jnp.bfloat16), "clip", axis=0, tiled=True),
        lax.all_gather(attend_w.astype(jnp.bfloat16), "clip", axis=0, tiled=True),
        lax.all_gather(dense_w.astype(jnp.bfloat16), "clip", axis=0, tiled=True),
    )
    embeds, attends, denses = unpack_all(gathered)
    patch_w, time_one, time_two, block_w, cap_one, cap_two, final_w, null_caption = embeds
    space_qkv, space_out, time_qkv, time_out, cross_q, cross_kv, cross_out = attends
    fc_in, fc_out = denses
    (
        patch_b,
        time_b1,
        time_b2,
        block_b,
        cap_b1,
        cap_b2,
        space_bq,
        space_bv,
        space_bo,
        time_bq,
        time_bv,
        time_bo,
        cross_bq,
        cross_bv,
        cross_bo,
        fc_in_b,
        fc_out_b,
        final_b,
        table,
        final_table,
    ) = split_flat(vector_w, vector_shapes())
    angle = (timesteps.astype(jnp.float32) / 1000.0 + 0.008) / 1.008 * (math.pi / 2)
    signal = jnp.cos(angle) ** 2
    ratio = signal / (1.0 - signal)
    loss_weight = sample_weight * jnp.minimum(ratio, SNR_LIMIT) / ratio
    weight_total = lax.psum(jnp.sum(loss_weight), "clip")
    keep_part = jnp.sqrt(signal)[:, None, None, None]
    fade_part = jnp.sqrt(1.0 - signal)[:, None, None, None]
    noisy = (keep_part * latents + fade_part * noise).astype(jnp.bfloat16)
    frame_ids = lax.axis_index("frame") * frame_dev + jnp.arange(frame_dev)
    patch_ids = jnp.arange(patches)
    place = jnp.concatenate(
        [sincos(patch_ids // PGRID, D // 2), sincos(patch_ids % PGRID, D // 2)], -1
    )[None, None]
    hidden_zero = matmul_low(noisy, patch_w) + patch_b + place + sincos(frame_ids, D)[None, :, None]
    freq_in = sincos(timesteps, TFREQ).astype(jnp.bfloat16)
    pre_one = matmul_low(freq_in, time_one) + time_b1
    act_one = jax.nn.silu(pre_one).astype(jnp.bfloat16)
    time_embed = matmul_low(act_one, time_two) + time_b2
    silu_time = jax.nn.silu(time_embed).astype(jnp.bfloat16)
    mods = table[None] + (matmul_low(silu_time, block_w) + block_b).reshape(clip_dev, 6, D)

    def mod_row(number):
        return mods[:, number][:, None, None, :]

    is_null = null_flags == 1
    cap_in = jnp.where(is_null[:, None, None], null_caption[None], captions)
    cap_pre = matmul_low(cap_in, cap_one) + cap_b1
    cap_act = gelu_tanh(cap_pre).astype(jnp.bfloat16)
    cap_rows = (matmul_low(cap_act, cap_two) + cap_b2).astype(jnp.bfloat16)
    live_len = jnp.where(is_null, L_CAP, cap_lengths)
    key_mask = jnp.arange(L_CAP)[None, :] < live_len[:, None]
    space_in = modulate(hidden_zero, mod_row(0), mod_row(1)).astype(jnp.bfloat16)
    space_q, space_k, space_v = (
        heads_of(piece, clip_dev * frame_dev)
        for piece in split_qkv(matmul_low(space_in, space_qkv), space_bq, space_bv)
    )
    space_o, space_lse = attend_forward(space_q, space_k, space_v, None)
    space_flat = space_o.reshape(clip_dev, frame_dev, patches, D)
    space_res = matmul_low(space_flat, space_out) + space_bo
    hidden_one = hidden_zero + mod_row(2) * space_res
    time_in = lax.all_to_all(
        hidden_one.astype(jnp.bfloat16), "frame", split_axis=2, concat_axis=1, tiled=True
    )
    time_in = jnp.swapaxes(time_in, 1, 2)
    frames = time_in.shape[2]
    time_q, time_k, time_v = (
        heads_of(piece, clip_dev * local_pos)
        for piece in split_qkv(matmul_low(time_in, time_qkv), time_bq, time_bv)
    )
    time_o, time_lse = attend_forward(time_q, time_k, time_v, None)
    time_back = jnp.swapaxes(time_o.reshape(clip_dev, local_pos, frames, D), 1, 2)
    time_flat = lax.all_to_all(time_back, "frame", split_axis=1, concat_axis=2, tiled=True)
    time_res = matmul_low(time_flat, time_out) + time_bo
    hidden_two = hidden_one + mod_row(2) * time_res
    cross_in = hidden_two.astype(jnp.bfloat16)
    cross_query = heads_of(
        (matmul_low(cross_in, cross_q) + cross_bq).astype(jnp.bfloat16), clip_dev
    )
    cross_merged = matmul_low(cap_rows, cross_kv)
    cross_k = heads_of(cross_merged[..., :D].astype(jnp.bfloat16), clip_dev)
    cross_v = heads_of((cross_merged[..., D:] + cross_bv).astype(jnp.bfloat16), clip_dev)
    cross_o, cross_lse = attend_forward(cross_query, cross_k, cross_v, key_mask)
    cross_flat = cross_o.reshape(clip_dev, frame_dev, patches, D)
    hidden_three = hidden_two + matmul_low(cross_flat, cross_out) + cross_bo
    dense_in = modulate(hidden_three, mod_row(3), mod_row(4)).astype(jnp.bfloat16)
    dense_pre = matmul_low(dense_in, fc_in) + fc_in_b
    dense_act = gelu_tanh(dense_pre).astype(jnp.bfloat16)
    dense_res = matmul_low(dense_act, fc_out) + fc_out_b
    hidden_four = hidden_three + mod_row(5) * dense_res
    final_mod = final_table[None] + time_embed[:, None, :]
    final_shift = final_mod[:, 0][:, None, None, :]
    final_scale = final_mod[:, 1][:, None, None, :]
    final_in = modulate(hidden_four, final_shift, final_scale).astype(jnp.bfloat16)
    predicted = matmul_low(final_in, final_w) + final_b
    miss = predicted - noise
    clip_error = jnp.sum(jnp.mean(miss * miss, -1), (1, 2))
    local_loss = jnp.sum(loss_weight * clip_error)
    grad_pred = (
        2.0 / miss.shape[-1] * (loss_weight / weight_total)[:, None, None, None] * miss
    ).astype(jnp.bfloat16)
    g_final_w = weight_grad(final_in, grad_pred)
    g_final_b = bias_grad(grad_pred)
    unused, pullback = jax.vjp(modulate, hidden_four, final_shift, final_scale)
    grad_hidden, grad_fshift, grad_fscale = pullback(back_low(grad_pred, final_w))
    grad_fmod = jnp.stack([grad_fshift.reshape(clip_dev, D), grad_fscale.reshape(clip_dev, D)], 1)
    g_final_table = jnp.sum(grad_fmod, 0)
    grad_time_embed = grad_fmod[:, 0] + grad_fmod[:, 1]
    grad_dense = (grad_hidden * mod_row(5)).astype(jnp.bfloat16)
    grad_gate_b = jnp.sum(grad_hidden * dense_res, (1, 2))
    g_fc_out = weight_grad(dense_act, grad_dense)
    g_fc_out_b = bias_grad(grad_dense)
    unused, pullback = jax.vjp(gelu_tanh, dense_pre)
    grad_pre = pullback(back_low(grad_dense, fc_out))[0].astype(jnp.bfloat16)
    g_fc_in = weight_grad(dense_in, grad_pre)
    g_fc_in_b = bias_grad(grad_pre)
    dense_owned = reduce_group(flatten_all([g_fc_in, g_fc_out]))
    unused, pullback = jax.vjp(modulate, hidden_three, mod_row(3), mod_row(4))
    grad_input, grad_shift_b, grad_scale_b = pullback(back_low(grad_pre, fc_in))
    grad_hidden = grad_hidden + grad_input
    grad_cross = grad_hidden.astype(jnp.bfloat16)
    g_cross_out = weight_grad(cross_flat, grad_cross)
    g_cross_bo = bias_grad(grad_cross)
    grad_cross_o = heads_of(back_low(grad_cross, cross_out).astype(jnp.bfloat16), clip_dev)
    grad_cq, grad_ck, grad_cv = attend_backward(
        cross_query, cross_k, cross_v, key_mask, cross_lse, grad_cross_o
    )
    grad_cq = grad_cq.astype(jnp.bfloat16).reshape(clip_dev, frame_dev, patches, D)
    g_cross_q = weight_grad(cross_in, grad_cq)
    g_cross_bq = bias_grad(grad_cq)
    grad_hidden = grad_hidden + back_low(grad_cq, cross_q)
    grad_cv = grad_cv.reshape(clip_dev, L_CAP, D)
    grad_ckv = jnp.concatenate([grad_ck.reshape(clip_dev, L_CAP, D), grad_cv], -1)
    g_cross_kv = weight_split(cap_rows, grad_ckv)
    g_cross_bv = bias_grad(grad_cv)
    grad_cap_rows = back_split(grad_ckv, cross_kv)
    grad_time = (grad_hidden * mod_row(2)).astype(jnp.bfloat16)
    g_time_out = weight_grad(time_flat, grad_time)
    g_time_bo = bias_grad(grad_time)
    grad_time_o = lax.all_to_all(
        back_low(grad_time, time_out).astype(jnp.bfloat16),
        "frame",
        split_axis=2,
        concat_axis=1,
        tiled=True,
    )
    grad_time_o = heads_of(jnp.swapaxes(grad_time_o, 1, 2), clip_dev * local_pos)
    grad_tq, grad_tk, grad_tv = attend_backward(time_q, time_k, time_v, None, time_lse, grad_time_o)
    grad_tqkv = jnp.concatenate(
        [
            piece.astype(jnp.bfloat16).reshape(clip_dev, local_pos, frames, D)
            for piece in (grad_tq, grad_tk, grad_tv)
        ],
        -1,
    )
    g_time_qkv = weight_grad(time_in, grad_tqkv)
    g_time_bq = bias_grad(grad_tqkv[..., :D])
    g_time_bv = bias_grad(grad_tqkv[..., 2 * D :])
    grad_tqkv = lax.all_to_all(
        jnp.swapaxes(grad_tqkv, 1, 2), "frame", split_axis=1, concat_axis=2, tiled=True
    )
    grad_gate_a = jnp.sum(grad_hidden * time_res, (1, 2))
    grad_hidden = grad_hidden + back_low(grad_tqkv, time_qkv)
    grad_gate_a = grad_gate_a + jnp.sum(grad_hidden * space_res, (1, 2))
    grad_space = (grad_hidden * mod_row(2)).astype(jnp.bfloat16)
    g_space_out = weight_grad(space_flat, grad_space)
    g_space_bo = bias_grad(grad_space)
    grad_space_o = heads_of(
        back_low(grad_space, space_out).astype(jnp.bfloat16), clip_dev * frame_dev
    )
    grad_sq, grad_sk, grad_sv = attend_backward(
        space_q, space_k, space_v, None, space_lse, grad_space_o
    )
    grad_sqkv = jnp.concatenate(
        [
            piece.astype(jnp.bfloat16).reshape(clip_dev, frame_dev, patches, D)
            for piece in (grad_sq, grad_sk, grad_sv)
        ],
        -1,
    )
    g_space_qkv = weight_grad(space_in, grad_sqkv)
    g_space_bq = bias_grad(grad_sqkv[..., :D])
    g_space_bv = bias_grad(grad_sqkv[..., 2 * D :])
    attend_owned = reduce_group(
        flatten_all(
            [g_space_qkv, g_space_out, g_time_qkv, g_time_out, g_cross_q, g_cross_kv, g_cross_out]
        )
    )
    unused, pullback = jax.vjp(modulate, hidden_zero, mod_row(0), mod_row(1))
    grad_input, grad_shift_a, grad_scale_a = pullback(back_low(grad_sqkv, space_qkv))
    grad_hidden = grad_hidden + grad_input
    g_patch_w = weight_split(noisy, grad_hidden)
    g_patch_b = bias_grad(grad_hidden)
    grad_mods = jnp.stack(
        [
            grad_shift_a.reshape(clip_dev, D),
            grad_scale_a.reshape(clip_dev, D),
            grad_gate_a,
            grad_shift_b.reshape(clip_dev, D),
            grad_scale_b.reshape(clip_dev, D),
            grad_gate_b,
        ],
        1,
    )
    g_table = jnp.sum(grad_mods, 0)
    grad_zero = grad_mods.reshape(clip_dev, 6 * D)
    g_block_b = jnp.sum(grad_zero, 0)
    g_block_w = weight_split(silu_time, grad_zero)
    unused, pullback = jax.vjp(jax.nn.silu, time_embed)
    grad_time_embed = grad_time_embed + pullback(back_split(grad_zero, block_w))[0]
    g_time_b2 = jnp.sum(grad_time_embed, 0)
    g_time_two = weight_split(act_one, grad_time_embed)
    unused, pullback = jax.vjp(jax.nn.silu, pre_one)
    grad_pre_one = pullback(back_split(grad_time_embed, time_two))[0]
    g_time_b1 = jnp.sum(grad_pre_one, 0)
    g_time_one = weight_split(freq_in, grad_pre_one)
    g_cap_b2 = bias_grad(grad_cap_rows)
    g_cap_two = weight_split(cap_act, grad_cap_rows)
    unused, pullback = jax.vjp(gelu_tanh, cap_pre)
    grad_cap_pre = pullback(back_split(grad_cap_rows, cap_two))[0]
    g_cap_b1 = bias_grad(grad_cap_pre)
    g_cap_one = weight_split(cap_in, grad_cap_pre)
    grad_cap_in = back_split(grad_cap_pre, cap_one)
    g_null = jnp.sum(jnp.where(is_null[:, None, None], grad_cap_in, 0.0), 0)
    embed_owned = reduce_group(
        flatten_all(
            [g_patch_w, g_time_one, g_time_two, g_block_w, g_cap_one, g_cap_two, g_final_w, g_null]
        )
    )
    vector_grad = flatten_all(
        [
            g_patch_b,
            g_time_b1,
            g_time_b2,
            g_block_b,
            g_cap_b1,
            g_cap_b2,
            g_space_bq,
            g_space_bv,
            g_space_bo,
            g_time_bq,
            g_time_bv,
            g_time_bo,
            g_cross_bq,
            g_cross_bv,
            g_cross_bo,
            g_fc_in_b,
            g_fc_out_b,
            g_final_b,
            g_table,
            g_final_table,
        ]
    )
    vector_sum, loss_sum = lax.psum((vector_grad, local_loss), ("frame", "clip"))
    owned = (embed_owned, attend_owned, dense_owned)
    local_square = (
        sum((jnp.sum(shard_piece * shard_piece) for shard_piece in owned))
        + jnp.sum(vector_sum * vector_sum) / n_clip
    )
    grad_norm = jnp.sqrt(lax.psum(local_square, "clip"))
    factor = jnp.minimum(1.0, CLIP_LIMIT / (grad_norm + NORM_FLOOR))
    embed_r = adam_step(embed_w, owned[0], embed_m, embed_v, embed_e, factor)
    attend_r = adam_step(attend_w, owned[1], attend_m, attend_v, attend_e, factor)
    dense_r = adam_step(dense_w, owned[2], dense_m, dense_v, dense_e, factor)
    vector_r = adam_step(vector_w, vector_sum, vector_m, vector_v, vector_e, factor)
    return (
        loss_sum,
        weight_total,
        grad_norm,
        embed_r[0],
        attend_r[0],
        dense_r[0],
        vector_r[0],
        embed_r[1],
        attend_r[1],
        dense_r[1],
        vector_r[1],
        embed_r[2],
        attend_r[2],
        dense_r[2],
        vector_r[2],
        embed_r[3],
        attend_r[3],
        dense_r[3],
        vector_r[3],
    )


def solution(mesh):
    in_specs = (
        P("clip", "frame", None, None),
        P("clip", "frame", None, None),
        P("clip"),
        P("clip", None, None),
        P("clip"),
        P("clip"),
        P("clip"),
        P("clip"),
        P("clip"),
        P("clip"),
        P(),
        P("clip"),
        P("clip"),
        P("clip"),
        P(),
        P("clip"),
        P("clip"),
        P("clip"),
        P(),
        P("clip"),
        P("clip"),
        P("clip"),
        P(),
    )
    out_specs = (
        P(),
        P(),
        P(),
        P("clip"),
        P("clip"),
        P("clip"),
        P(),
        P("clip"),
        P("clip"),
        P("clip"),
        P(),
        P("clip"),
        P("clip"),
        P("clip"),
        P(),
        P("clip"),
        P("clip"),
        P("clip"),
        P(),
    )
    return jax.shard_map(shards, mesh=mesh, in_specs=in_specs, out_specs=out_specs, check_vma=False)
```

profile of v0, /device:TPU:0, one launch (start us, length us, event | category | flops | bytes accessed | tf_op | source)
XLA Modules:
  0.0 6514.5 jit_solution(17155469229823764947)
XLA Ops:
  19.6 47.0 reshape.1638
  103.4 317.8 %all-gather.11.cloned.1.call-done = bf16[10616832]{0:T(1024)(128)(2,1)} async-done(((bf16[1327104]{0:T(1024)(128)(2,1)}), bf16[10616832]{0:T(1024)(128)(2,1)}) %all-gather.11.cloned.1.call-update) | async-done | bytes 21233680 | tf_op jit(solution)/shard_map/all_gather | solution.py:240
  476.0 553.1 %all-gather.9.cloned.1.call-done = bf16[15925248]{0:T(1024)(128)(2,1)} async-done(((bf16[1990656]{0:T(1024)(128)(2,1)}), bf16[15925248]{0:T(1024)(128)(2,1)}) %all-gather.9.cloned.1.call-update) | async-done | bytes 31850512 | tf_op jit(solution)/shard_map/all_gather | solution.py:239
  1117.7 1134.1 %all-gather.17.cloned.1.call-done = bf16[8,1,2019840]{2,1,0:T(2,128)(2,1)} async-done(((bf16[1,1,2019840]{2,1,0:T(2,128)(2,1)}), bf16[8,1,2019840]{2,1,0:T(2,128)(2,1)}) %all-gather.17.cloned.1.call-update) | async-done | bytes 32317456 | tf_op jit(solution)/shard_map/all_gather | solution.py:238
  2251.7 196.0 %reduce.75 = bf16[8,2019840]{1,0:T(8,128)(2,1)} reduce(bf16[8,1,2019840]{2,1,0:T(2,128)(2,1)} %all-gather.17.cloned.1.call-done, bf16[]{:T(256)} %constant.199), dimensions={1}, to_apply=%all-gather.reduce_sub_computation | reduce | bytes 64634880 | tf_op jit(solution)/shard_map/all_gather | solution.py:238
  2447.8 80.3 %reshape.1639 = bf16[16158720]{0:T(1024)(128)(2,1)} reshape(bf16[8,2019840]{1,0:T(8,128)(2,1)} %reduce.75) | data formatting | bytes 64634880
  2565.5 29.0 reshape.1578
  3007.6 29.3 concatenate.82
  3059.7 34.1 concatenate.81
  3143.3 34.9 copy.366
  3444.7 32.7 reshape.1612
  3549.9 80.9 %reshape.1632 = f32[8,4,497664]{2,1,0:T(4,128)} reshape(f32[15925248]{0:T(1024)} %constant_dynamic-update-slice_fusion.12) | data formatting | bytes 127401984 | tf_op jit(solution)/shard_map/reshape | solution.py:73
  3630.8 43.5 copy.409
  3674.2 42.8 copy.365
  3764.3 83.8 %reshape.1617 = f32[8,4,504960]{2,1,0:T(4,128)} reshape(f32[16158720]{0:T(1024)} %constant_dynamic-update-slice_fusion.5) | data formatting | bytes 129269760 | tf_op jit(solution)/shard_map/reshape | solution.py:73
  3848.0 45.2 copy.334
  3893.4 52.7 reshape.1618
  3947.3 688.7 %all-reduce.7.cloned.1.call-done = f32[15925248]{0:T(1024)} async-done(((f32[15925248]{0:T(1024)}), f32[15925248]{0:T(1024)}) %all-reduce.7.cloned.1.call-update) | async-done | bytes 63701008
  4639.0 1515.7 %all-reduce.9.cloned.1.call-done = (f32[16158720]{0:T(1024)}, f32[10616832]{0:T(1024)}, f32[38032]{0:T(1024)}) async-done(((f32[16158720]{0:T(1024)}, f32[10616832]{0:T(1024)}, f32[38032]{0:T(1024)}), (f32[16158720]{0:T(1024)}, f32[10616832]{0:T(1024)}, f32[38032]{0:T(1024)})) %all-reduce.9.cloned.1.call-update) | async-done | bytes 107254352
  6171.1 41.7 all-gather.13.cloned.1.call-done
  6219.1 36.7 all-gather.15.cloned.1.call-done
  6259.7 54.9 all-gather.19.cloned.1.call-done
  6334.9 40.0 psum.28
  6397.4 29.5 multiply_reduce_fusion.1
  (761 shorter events, 1244.4 us)
Async XLA Ops:
  7.2 414.0 %all-gather.11.cloned.1.call-start = ((), (), s32[]{:S(2)}) async-start(), calls=%async_computation.5 | async-start | bytes 23887872 | tf_op jit(solution)/shard_map/all_gather | solution.py:240
  11.0 1018.1 %all-gather.9.cloned.1.call-start = ((), (), s32[]{:S(2)}) async-start(), calls=%async_computation.4 | async-start | bytes 35831808 | tf_op jit(solution)/shard_map/all_gather | solution.py:239
  15.9 2235.8 %all-gather.17.cloned.1.call-start = ((), (), s32[]{:S(2)}) async-start(), calls=%async_computation.8 | async-start | bytes 72714240 | tf_op jit(solution)/shard_map/all_gather | solution.py:238
  103.3 2499.6 %copy-start.96 = (bf16[2,256,16]{1,2,0:T(8,128)(2,1)}, bf16[2,256,16]{1,2,0:T(8,128)(2,1)S(1)}, u32[]{:S(2)}) copy-start(bf16[2,256,16]{1,2,0:T(8,128)(2,1)S(1)} %fusion.101) | copy-start | bytes 49156
  2565.4 184.2 %copy-start.111 = (f32[1152]{0:T(1024)}, f32[1152]{0:T(1024)S(1)}, u32[]{:S(2)}) copy-start(f32[1152]{0:T(1024)S(1)} %get-tuple-element.69) | copy-start | bytes 13828
  2602.9 332.4 %copy-start.93 = (f32[1152]{0:T(1024)}, f32[1152]{0:T(1024)S(1)}, u32[]{:S(2)}) copy-start(f32[1152]{0:T(1024)S(1)} %get-tuple-element.33) | copy-start | bytes 13828
  2604.9 162.2 %copy-start.6 = (f32[2,256,1152]{2,1,0:T(8,128)}, f32[2,256,1152]{2,1,0:T(8,128)S(1)}, u32[]{:S(2)}) copy-start(f32[2,256,1152]{2,1,0:T(8,128)S(1)} %get-tuple-element.132) | copy-start | bytes 7077892
  2638.3 48.6 all-to-all-start
  2745.1 20.4 all-to-all-start.1
  2749.7 67.9 %copy-start.142 = (f32[1152]{0:T(1024)}, f32[1152]{0:T(1024)S(1)}, u32[]{:S(2)}) copy-start(f32[1152]{0:T(1024)S(1)} %get-tuple-element.35) | copy-start | bytes 13828
  2791.8 60.5 copy-start.19
  2791.8 60.5 copy-start.164
  2792.2 60.1 copy-start.172
  2869.1 56.9 copy-start.25
  2947.6 286.2 %all-to-all-start.2 = ((bf16[1,2,256,1152]{3,1,0,2:T(2,128)(2,1)}), bf16[1,2,256,1152]{3,1,0,2:T(2,128)(2,1)}, u32[]{:S(2)}, u32[]{:S(2)}) async-start(bf16[1,2,256,1152]{3,1,0,2:T(2,128)(2,1)} %copy.311), calls=%async_computation.2 | async-start | bytes 2359296 | tf_op jit(solution)/shard_map/all_to_all | solution.py:386
  3283.3 46.2 all-to-all-start.3
  3288.3 1347.7 %all-reduce.7.cloned.1.call-start = ((), (), s32[]{:S(2)}) async-start(), calls=%async_computation.10 | async-start | bytes 127401984
  3717.1 2437.6 %all-reduce.9.cloned.1.call-start = ((), (), s32[]{:S(2)}) async-start(), calls=%async_computation.11 | async-start | bytes 214515712
  3893.2 53.0 copy-start.92
  3893.3 53.0 copy-start.110
  3893.3 53.0 copy-start.123
  3947.2 2265.7 %all-gather.13.cloned.1.call-start = ((), (), s32[]{:S(2)}) async-start(), calls=%async_computation.6 | async-start | bytes 9953280 | tf_op jit(solution)/shard_map/all_gather | solution.py:75
  4639.0 1616.9 %all-gather.15.cloned.1.call-start = ((), (), s32[]{:S(2)}) async-start(), calls=%async_computation.7 | async-start | bytes 6635520 | tf_op jit(solution)/shard_map/all_gather | solution.py:75
  6157.2 157.4 %all-gather.19.cloned.1.call-start = ((), (), s32[]{:S(2)}) async-start(), calls=%async_computation.9 | async-start | bytes 10099200 | tf_op jit(solution)/shard_map/all_gather | solution.py:75
  (209 other events, 2766.2 us)
Sparse Core Ops, SparseCore 0:
  11.1 410.0 all-gather.10
  423.3 605.7 all-gather.8
  1031.2 1220.4 all-gather.16
  3717.2 918.7 all-reduce.6
  4642.8 1511.8 all-reduce.8
  6156.7 56.1 all-gather.12
  6215.0 40.7 all-gather.14
  6258.0 56.5 all-gather.18
where the time goes:
time: 6530 us; the launch traced here: 6510 us
  waiting for transfers between devices  4370 us (67%)
  local copies, waits for them, and re-layouts  1260 us (19%)
  other arithmetic  412 us (6%)
  matrix products  344 us (5%)
  blocking collectives  87.5 us (1%)
    unnamed x10, waiting for transfers between devices  2200 us
    all_gather x1, waiting for transfers between devices, shards(): lax.all_gather(embed_w.astype(jnp.bfloat16), 'clip', axis=0, tiled=True)  1130 us
    all_gather x1, waiting for transfers between devices, shards(): lax.all_gather(attend_w.astype(jnp.bfloat16), 'clip', axis=0, tiled=True)  553 us
    unnamed x465, local copies, waits for them, and re-layouts  336 us
    all_gather x1, waiting for transfers between devices, shards(): lax.all_gather(dense_w.astype(jnp.bfloat16), 'clip', axis=0, tiled=True)  318 us
    reshape x3, local copies, waits for them, and re-layouts, reduce_group(): reorder = grad.reshape(n_clip, n_frame, -1).swapaxes(0, 1).reshape(-1)  217 us
    all_gather x1, other arithmetic, shards(): lax.all_gather(embed_w.astype(jnp.bfloat16), 'clip', axis=0, tiled=True)  196 us
    slice x25, local copies, waits for them, and re-layouts, split_flat(): pieces.append(flat[offset:offset + length].reshape(extent))  170 us
  transfers between devices with their start and end apart: 12, of which 10 were waited for; matrix products, arithmetic and copies ran while one was open for 13% of the time, Pallas kernels for 0%

commit v1 on v0

--- a/solution.py
+++ b/solution.py
@@ -1,8 +1,12 @@
 import math
+from functools import partial
 
 import jax
 import jax.numpy as jnp
+import numpy as np
 from jax import lax
+from jax.experimental import pallas as pl
+from jax.experimental.pallas import tpu as pltpu
 from jax.sharding import PartitionSpec as P
 
 D = 1152
@@ -532,6 +536,1039 @@
     )
 
 
+AXES = ("frame", "clip")
+LANES = 128
+LANE_TILES = D // LANES
+EMB_PAD = 1792
+
+
+X_SIZE, CORES, Z_SIZE, Y_SIZE = 2, 2, 4, 2
+N_OWN = Z_SIZE * Y_SIZE
+RING = [(0, 0), (1, 0), (2, 0), (3, 0), (3, 1), (2, 1), (1, 1), (0, 1)]
+RING_CLIP = [z * Y_SIZE + y for z, y in RING]
+CLIP_RING = [RING_CLIP.index(c) for c in range(N_OWN)]
+
+
+def pairs(move):
+    out = []
+    for x in range(X_SIZE):
+        for core in range(CORES):
+            for z in range(Z_SIZE):
+                for y in range(Y_SIZE):
+                    to = move(x, core, z, y)
+                    if to is not None:
+                        rank = lambda a, b, c, d: (a * CORES + b) * N_OWN + c * Y_SIZE + d
+                        out.append((rank(x, core, z, y), rank(*to)))
+    return out
+
+
+SWAP_X = pairs(lambda x, c, z, y: (1 - x, c, z, y))
+SWAP_CORE = pairs(lambda x, c, z, y: (x, 1 - c, z, y))
+SWAP_Y = pairs(lambda x, c, z, y: (x, c, z, 1 - y))
+SWAP_Z1 = pairs(lambda x, c, z, y: (x, c, z ^ 1, y))
+SWAP_Z2 = pairs(lambda x, c, z, y: (x, c, z ^ 2, y))
+
+
+def hop_z(source, to):
+    return pairs(lambda x, c, z, y: (x, c, to, y) if z == source else None)
+
+
+def ring_move(step, keep, seen):
+    def move(x, c, z, y):
+        place = CLIP_RING[z * Y_SIZE + y]
+        origin = RING_CLIP[(place + seen) % N_OWN]
+        if origin not in keep:
+            return None
+        to = RING[(place + step) % N_OWN]
+        return (x, c) + to
+
+    return pairs(move)
+
+
+def swap_move(flip_x, flip_core, keep, seen):
+    def move(x, c, z, y):
+        place = CLIP_RING[z * Y_SIZE + y]
+        if RING_CLIP[(place + seen) % N_OWN] not in keep:
+            return None
+        return (x ^ flip_x, c ^ flip_core, z, y)
+
+    return pairs(move)
+
+
+def shift(value, perm):
+    return lax.ppermute(value, AXES, perm)
+
+
+def sum_clips(value):
+    for perm in (SWAP_Y, SWAP_Z1, SWAP_Z2):
+        value = value + shift(value, perm)
+    return value
+
+
+def sum_frames(value):
+    for perm in (SWAP_CORE, SWAP_X):
+        value = value + shift(value, perm)
+    return value
+
+
+def shard_segments(matrices, n_rows):
+    spans, offset = [], 0
+    for name, rows, wide in matrices:
+        spans.append((name, offset, rows, wide))
+        offset += rows * wide
+    out = []
+    for owner in range(N_OWN):
+        low, high = owner * n_rows, (owner + 1) * n_rows
+        mine = []
+        for name, start, rows, wide in spans:
+            begin, end = max(low, start), min(high, start + rows * wide)
+            if begin < end:
+                mine.append((name, (begin - start) // wide, (end - begin) // wide, wide))
+        out.append(mine)
+    return out
+
+
+ATTEND = [
+    ("space_qkv", D, 3),
+    ("space_out", D, 1),
+    ("time_qkv", D, 3),
+    ("time_out", D, 1),
+    ("cross_q", D, 1),
+    ("cross_kv", D, 2),
+    ("cross_out", D, 1),
+]
+DENSE = [("fc_in", D, 4), ("fc_out", MLP, 1)]
+ATTEND_ROWS = 13824 // N_OWN
+DENSE_ROWS = 9216 // N_OWN
+ATTEND_SEGS = shard_segments(ATTEND, ATTEND_ROWS)
+DENSE_SEGS = shard_segments(DENSE, DENSE_ROWS)
+
+
+def cast_table(segments, block):
+    out = []
+    for mine in segments:
+        rows, offset = [], 0
+        for name, first, count, wide in mine:
+            for start in range(0, count * wide, block):
+                rows.append((wide, offset + start // wide, count))
+            offset += count * wide
+        out.append(rows)
+    return np.array(out, np.int32)
+
+
+def step_table(segments, block, n_rows):
+    out = []
+    for mine in segments:
+        rows, offset = [], 0
+        for name, first, count, wide in mine:
+            half = count // 2
+            for start in range(0, count * wide, block):
+                core, inner = divmod(start // wide, half)
+                rows.append((wide, core * (n_rows // 2) + offset + inner, half))
+            offset += half * wide
+        out.append(rows)
+    return np.array(out, np.int32)
+
+
+CAST_BLOCK = 576
+STEP_BLOCK = 288
+
+
+def cast_kernel(widths, table, flat, out):
+    block = pl.program_id(0)
+    for wide in widths:
+        count = CAST_BLOCK // wide
+
+        @pl.when(table[block, 0] == wide)
+        def _():
+            for slab in range(wide):
+                row = pl.multiple_of(table[block, 1] + slab * table[block, 2], 16)
+                for tile in range(LANE_TILES):
+                    piece = flat[pl.ds(LANE_TILES * slab + tile, count, stride=LANE_TILES * wide), :]
+                    out[pl.ds(row, count), tile * LANES : (tile + 1) * LANES] = piece.astype(jnp.bfloat16)
+
+
+def cast_shard(flat, table, widths, n_rows):
+    units = CAST_BLOCK * LANE_TILES
+    return pl.pallas_call(
+        partial(cast_kernel, widths),
+        grid_spec=pltpu.PrefetchScalarGridSpec(
+            num_scalar_prefetch=1,
+            grid=(n_rows // CAST_BLOCK,),
+            in_specs=[pl.BlockSpec((units, LANES), lambda b, t: (b, 0))],
+            out_specs=pl.BlockSpec((n_rows, D), lambda b, t: (0, 0)),
+        ),
+        out_shape=jax.ShapeDtypeStruct((n_rows, D), jnp.bfloat16),
+        compiler_params=pltpu.CompilerParams(vmem_limit_bytes=40 * 1024 * 1024),
+    )(table, flat.reshape(-1, LANES))
+
+
+def rows_kernel(flat, out):
+    count = out.shape[0]
+    for tile in range(LANE_TILES):
+        piece = flat[pl.ds(tile, count, stride=LANE_TILES), :]
+        out[:, tile * LANES : (tile + 1) * LANES] = piece.astype(out.dtype)
+
+
+def flat_to_rows(flat, dtype):
+    rows = flat.shape[0] // LANE_TILES
+    block = rows // 8
+    return pl.pallas_call(
+        rows_kernel,
+        grid=(8,),
+        in_specs=[pl.BlockSpec((block * LANE_TILES, LANES), lambda b: (b, 0))],
+        out_specs=pl.BlockSpec((block, D), lambda b: (b, 0)),
+        out_shape=jax.ShapeDtypeStruct((rows, D), dtype),
+        compiler_params=pltpu.CompilerParams(vmem_limit_bytes=32 * 1024 * 1024),
+    )(flat)
+
+
+def flat_kernel(rows, out):
+    count = rows.shape[0]
+    for tile in range(LANE_TILES):
+        out[pl.ds(tile, count, stride=LANE_TILES), :] = rows[:, tile * LANES : (tile + 1) * LANES]
+
+
+def rows_to_flat(rows):
+    block = rows.shape[0] // 8
+    return pl.pallas_call(
+        flat_kernel,
+        grid=(8,),
+        in_specs=[pl.BlockSpec((block, D), lambda b: (b, 0))],
+        out_specs=pl.BlockSpec((block * LANE_TILES, LANES), lambda b: (b, 0)),
+        out_shape=jax.ShapeDtypeStruct((rows.shape[0] * LANE_TILES, LANES), rows.dtype),
+        compiler_params=pltpu.CompilerParams(vmem_limit_bytes=32 * 1024 * 1024),
+    )(rows)
+
+
+def place_kernel(n_pieces, keep, stores, slots, own, *refs):
+    pieces, outs, (held, sems, out_sem) = refs[:n_pieces], refs[n_pieces:-3], refs[-3:]
+    low = min(keep)
+
+    def copies():
+        yield slots[0, 0], pltpu.make_async_copy(own, held.at[slots[0, 0] - low], sems.at[n_pieces])
+        for number in range(n_pieces):
+            owner = slots[number + 1, 0]
+            yield owner, pltpu.make_async_copy(
+                pieces[number], held.at[owner - low, slots[number + 1, 1]], sems.at[number]
+            )
+
+    for action in ("start", "wait"):
+        for owner, copy in copies():
+            if len(keep) == N_OWN:
+                getattr(copy, action)()
+            else:
+
+                @pl.when(owner >= low)
+                def _():
+                    getattr(copy, action)()
+
+    rows = held.shape[1] * held.shape[2]
+    done = []
+    for number, (out, row, column, owner, first, count) in enumerate(stores):
+        quarter = rows // 4
+        while count > 0:
+            part, inner = divmod(first, quarter)
+            some = min(count, quarter - inner)
+            copy = pltpu.make_async_copy(
+                held.at[owner - low, part, pl.ds(inner, some)],
+                outs[out].at[pl.ds(row, some), pl.ds(column, D)],
+                out_sem.at[len(done)],
+            )
+            copy.start()
+            done.append(copy)
+            first, row, count = first + some, row + some, count - some
+    for copy in done:
+        copy.wait()
+
+
+def place_pieces(own, pieces, slots, keep, shapes, stores):
+    rows = own.shape[0]
+    spec = pl.BlockSpec(memory_space=pl.ANY)
+    return pl.pallas_call(
+        partial(place_kernel, len(pieces), keep, stores),
+        in_specs=[pl.BlockSpec(memory_space=pltpu.SMEM)] + [spec] * (len(pieces) + 1),
+        out_specs=[spec] * len(shapes),
+        out_shape=[jax.ShapeDtypeStruct(shape, own.dtype) for shape in shapes],
+        scratch_shapes=[
+            pltpu.VMEM((len(keep), 4, rows // 4, D), own.dtype),
+            pltpu.SemaphoreType.DMA((len(pieces) + 1,)),
+            pltpu.SemaphoreType.DMA((4 * len(stores),)),
+        ],
+        compiler_params=pltpu.CompilerParams(vmem_limit_bytes=48 * 1024 * 1024),
+    )(slots, own.reshape(4, rows // 4, D), *pieces)
+
+
+def gather_shards(own, clip_id, frame_id, keep, shapes, stores):
+    rows = own.shape[0]
+    quarter = lax.dynamic_slice_in_dim(own, frame_id * (rows // 4), rows // 4, 0)
+    place = jnp.asarray(CLIP_RING, jnp.int32)[clip_id]
+    ring_clip = jnp.asarray(RING_CLIP, jnp.int32)
+    pieces, slots = [], [jnp.stack([clip_id, 0 * clip_id])]
+    ahead, behind = quarter, quarter
+    arrived = []
+    for step in range(1, N_OWN // 2 + 1):
+        ahead = shift(ahead, ring_move(1, keep, 1 - step))
+        arrived.append((ahead, -step))
+        if step < N_OWN // 2:
+            behind = shift(behind, ring_move(-1, keep, step - 1))
+            arrived.append((behind, step))
+    for piece, seen in arrived:
+        source = ring_clip[(place + seen) % N_OWN]
+        over_x = shift(piece, swap_move(1, 0, keep, seen))
+        over_core = shift(piece, swap_move(0, 1, keep, seen))
+        both = shift(over_x, swap_move(0, 1, keep, seen))
+        for value, flip in ((piece, 0), (over_x, 2), (over_core, 1), (both, 3)):
+            pieces.append(value)
+            slots.append(jnp.stack([source, frame_id ^ flip]))
+    return place_pieces(own, pieces, jnp.stack(slots).astype(jnp.int32), keep, shapes, stores)
+
+
+def matrix_plan(matrices, segments):
+    shapes = [(rows, wide * D) for name, rows, wide in matrices]
+    names = [name for name, rows, wide in matrices]
+    stores = []
+    for owner in range(N_OWN):
+        offset = 0
+        for name, first, count, wide in segments[owner]:
+            for j in range(wide):
+                stores.append((names.index(name), first, j * D, owner, offset, count))
+                offset += count
+    return shapes, stores
+
+
+def half_rows(segments, name):
+    rows = [[], []]
+    for mine in segments:
+        for label, first, count, wide in mine:
+            if label == name:
+                for core in range(2):
+                    begin = first + core * (count // 2)
+                    rows[core].extend(range(begin, begin + count // 2))
+    return np.array(rows, np.int32)
+
+
+def pick_columns(values, rows, core):
+    wanted = jnp.asarray(rows)[core]
+    chooser = (jnp.arange(values.shape[1], dtype=jnp.int32)[:, None] == wanted[None]).astype(jnp.bfloat16)
+    return matmul_low(values, chooser).astype(jnp.bfloat16)
+
+
+def both_cores(value):
+    return jnp.concatenate([value, shift(value, SWAP_CORE)], 0)
+
+
+def reduce_pair(pair, owner_z, x_first, x_id, y_id):
+    def fold(value, axis, place, perm):
+        mine = lax.dynamic_index_in_dim(value, place, axis, keepdims=False)
+        other = lax.dynamic_index_in_dim(value, 1 - place, axis, keepdims=False)
+        return mine + shift(other, perm)
+
+    if x_first:
+        part = fold(fold(pair, 1, x_id, SWAP_X), 0, y_id, SWAP_Y)
+    else:
+        part = fold(fold(pair, 0, y_id, SWAP_Y), 0, x_id, SWAP_X)
+    for source in range(Z_SIZE - 1, owner_z, -1):
+        part = part + shift(part, hop_z(source, source - 1))
+    for source in range(owner_z):
+        part = part + shift(part, hop_z(source, source + 1))
+    return part
+
+
+def pair_chunks(grads, segments, owner_z):
+    chunks = []
+    for owner in (2 * owner_z, 2 * owner_z + 1):
+        parts = []
+        for label, first, count, wide in segments[owner]:
+            begin = sum(
+                seg[2] // 2 for mine in segments[:owner] for seg in mine if seg[0] == label
+            )
+            for j in range(wide):
+                parts.append(grads[label][j][begin : begin + count // 2])
+        chunks.append(jnp.concatenate(parts, 0) if len(parts) > 1 else parts[0])
+    pair = jnp.stack(chunks)
+    return pair.reshape(2, 2, pair.shape[1] // 2, D)
+
+
+def choose_z(parts, z_id):
+    out = parts[0]
+    for number in range(1, Z_SIZE):
+        out = jnp.where(z_id == number, parts[number], out)
+    return out
+
+
+def step_values(master, grad, first, second, average):
+    keep = min(AVERAGE_KEEP, (1.0 + STEP) / (10.0 + STEP))
+    first = BETA_FIRST * first + (1.0 - BETA_FIRST) * grad
+    second = BETA_SECOND * second + (1.0 - BETA_SECOND) * grad * grad
+    moved = (
+        first
+        / (1.0 - BETA_FIRST**STEP)
+        / (jnp.sqrt(second / (1.0 - BETA_SECOND**STEP)) + ADAM_FLOOR)
+    )
+    master = master - LEARN_RATE * (moved + WEIGHT_DECAY * master)
+    return (master, first, second, keep * average + (1.0 - keep) * master)
+
+
+STEP_ROWS = 144
+
+
+def step_kernel(widths, n_rows, table, places, factor, *refs):
+    quarters, olds, news = refs[:4], refs[4:8], refs[8:12]
+    shard, flat, sems = refs[12:]
+    block = pl.program_id(0)
+    per = n_rows // 4
+
+    @pl.when(block == 0)
+    def _():
+        copies = [
+            pltpu.make_async_copy(
+                quarters[k],
+                shard.at[pl.ds(pl.multiple_of(places[k] * per, 8), per)],
+                sems.at[k],
+            )
+            for k in range(4)
+        ]
+        for copy in copies:
+            copy.start()
+        for copy in copies:
+            copy.wait()
+
+    for wide in widths:
+        count = STEP_BLOCK // wide
+
+        @pl.when(table[block, 0] == wide)
+        def _():
+            for slab in range(wide):
+                row = pl.multiple_of(table[block, 1] + slab * table[block, 2], 8)
+                for tile in range(LANE_TILES):
+                    flat[pl.ds(LANE_TILES * slab + tile, count, stride=LANE_TILES * wide), :] = shard[
+                        pl.ds(row, count), tile * LANES : (tile + 1) * LANES
+                    ]
+
+    scale = factor[0]
+
+    def some_rows(number, carry):
+        at = pl.ds(pl.multiple_of(number * STEP_ROWS, 8), STEP_ROWS)
+        old = [ref[at, :] for ref in olds]
+        made = step_values(old[0], flat[at, :] * scale, old[1], old[2], old[3])
+        for ref, value in zip(news, made):
+            ref[at, :] = value
+        return carry
+
+    lax.fori_loop(0, STEP_BLOCK * LANE_TILES // STEP_ROWS, some_rows, 0)
+
+
+def step_shard(quarters, places, table, widths, n_rows, factor, olds):
+    units = STEP_BLOCK * LANE_TILES
+    block_spec = pl.BlockSpec((units, LANES), lambda b, t, p, f: (b, 0))
+    whole = pl.BlockSpec(memory_space=pl.ANY)
+    flat_shape = jax.ShapeDtypeStruct((n_rows * LANE_TILES, LANES), jnp.float32)
+    made = pl.pallas_call(
+        partial(step_kernel, widths, n_rows),
+        grid_spec=pltpu.PrefetchScalarGridSpec(
+            num_scalar_prefetch=3,
+            grid=(n_rows // STEP_BLOCK,),
+            in_specs=[whole] * 4 + [block_spec] * 4,
+            out_specs=[block_spec] * 4,
+            scratch_shapes=[
+                pltpu.VMEM((n_rows, D), jnp.float32),
+                pltpu.VMEM((units, LANES), jnp.float32),
+                pltpu.SemaphoreType.DMA((4,)),
+            ],
+        ),
+        out_shape=[flat_shape] * 4,
+        compiler_params=pltpu.CompilerParams(vmem_limit_bytes=50 * 1024 * 1024),
+    )(table, places, factor, *quarters, *[old.reshape(-1, LANES) for old in olds])
+    return [value.reshape(-1) for value in made]
+
+
+ROW_TIME_ONE = PATCH_VALUES
+ROW_TIME_TWO = ROW_TIME_ONE + TFREQ
+ROW_BLOCK = ROW_TIME_TWO + D
+ROW_CAP_ONE = ROW_BLOCK + 6 * D
+ROW_CAP_TWO = ROW_CAP_ONE + CAPW
+ROW_FINAL = ROW_CAP_TWO + D
+ROW_NULL = ROW_FINAL + PATCH_VALUES
+EMB_UNITS = 16158720 // LANES // N_OWN
+EMB_FIRST = [EMB_UNITS * c // LANE_TILES for c in range(N_OWN)]
+EMB_SHIFT = [EMB_UNITS * c % LANE_TILES for c in range(N_OWN)]
+
+
+def two_parts(product, value):
+    upper, lower = halves(value)
+    return product(upper) + product(lower)
+
+
+def shards_block(
+    latents,
+    noise,
+    timesteps,
+    captions,
+    cap_lengths,
+    null_flags,
+    sample_weight,
+    embed_w,
+    attend_w,
+    dense_w,
+    vector_w,
+    embed_m,
+    attend_m,
+    dense_m,
+    vector_m,
+    embed_v,
+    attend_v,
+    dense_v,
+    vector_v,
+    embed_e,
+    attend_e,
+    dense_e,
+    vector_e,
+):
+    clip_dev, frame_dev, patches = (latents.shape[0], latents.shape[1], latents.shape[2])
+    n_frame = lax.axis_size("frame")
+    n_clip = lax.axis_size("clip")
+    local_pos = patches // n_frame
+    tokens = frame_dev * patches
+    frame_id = lax.axis_index("frame")
+    clip_id = lax.axis_index("clip")
+    x_id, core_id = frame_id // CORES, frame_id % CORES
+    z_id, y_id = clip_id // Y_SIZE, clip_id % Y_SIZE
+
+    attend_cast = cast_shard(
+        attend_w, jnp.asarray(cast_table(ATTEND_SEGS, CAST_BLOCK))[clip_id], (1, 2, 3), ATTEND_ROWS
+    )
+    space_qkv, space_out, time_qkv, time_out, cross_q, cross_kv, cross_out = gather_shards(
+        attend_cast, clip_id, frame_id, range(N_OWN), *matrix_plan(ATTEND, ATTEND_SEGS)
+    )
+    emb_first = jnp.asarray(EMB_FIRST, jnp.int32)[clip_id]
+    emb_shift = jnp.asarray(EMB_SHIFT, jnp.int32)[clip_id]
+    emb_flat = lax.dynamic_update_slice(
+        jnp.zeros((EMB_PAD * LANE_TILES, LANES), jnp.float32),
+        embed_w.reshape(-1, LANES),
+        (emb_shift, 0 * emb_shift),
+    )
+    emb_rows = flat_to_rows(emb_flat, jnp.bfloat16)
+    cap_owners = range(4, N_OWN)
+    cap_weights = gather_shards(
+        emb_rows,
+        clip_id,
+        frame_id,
+        cap_owners,
+        [(EMB_PAD * len(cap_owners), D)],
+        [(0, EMB_PAD * k, 0, owner, 0, EMB_PAD) for k, owner in enumerate(cap_owners)],
+    )[0]
+    dense_cast = cast_shard(
+        dense_w, jnp.asarray(cast_table(DENSE_SEGS, CAST_BLOCK))[clip_id], (1, 4), DENSE_ROWS
+    )
+    fc_in, fc_out = gather_shards(
+        dense_cast, clip_id, frame_id, range(N_OWN), *matrix_plan(DENSE, DENSE_SEGS)
+    )
+
+    last = N_OWN - 1
+    cap_last = cap_weights[EMB_PAD * (len(cap_owners) - 1) :]
+    null_end = 16158720 - ROW_NULL * D
+    null_first, final_first = ROW_NULL - EMB_FIRST[last], ROW_FINAL - EMB_FIRST[last]
+    null_caption = (
+        cap_last[null_first : null_first - (-null_end // D)]
+        .reshape(-1)[:null_end]
+        .reshape(L_CAP, CAPW)
+    )
+    final_w = cap_last[final_first : final_first + PATCH_VALUES].reshape(D, PATCH_VALUES)
+    two_first = ROW_CAP_TWO - EMB_FIRST[last]
+
+    def to_cap_rows(value):
+        padded = jnp.pad(value, ((0, 0), (EMB_PAD, EMB_PAD)))
+        starts = [EMB_FIRST[owner] - ROW_CAP_ONE + EMB_PAD for owner in cap_owners]
+        return jnp.concatenate([padded[:, start : start + EMB_PAD] for start in starts], 1)
+
+    def from_cap_rows(value):
+        total = 0.0
+        for k, owner in enumerate(cap_owners):
+            start = EMB_FIRST[owner] - ROW_CAP_ONE
+            low, high = max(0, -start), min(EMB_PAD, CAPW - start)
+            part = value[:, EMB_PAD * k + low : EMB_PAD * k + high]
+            total = total + jnp.pad(part, ((0, 0), (start + low, CAPW - start - high)))
+        return total
+
+    (
+        patch_b,
+        time_b1,
+        time_b2,
+        block_b,
+        cap_b1,
+        cap_b2,
+        space_bq,
+        space_bv,
+        space_bo,
+        time_bq,
+        time_bv,
+        time_bo,
+        cross_bq,
+        cross_bv,
+        cross_bo,
+        fc_in_b,
+        fc_out_b,
+        final_b,
+        table,
+        final_table,
+    ) = split_flat(vector_w, vector_shapes())
+
+    own_clip = jnp.arange(n_clip) == clip_id
+    facts = jnp.stack([timesteps.astype(jnp.float32)[0], sample_weight[0]])
+    facts = sum_clips(jnp.where(own_clip[:, None], facts[None], 0.0))
+    all_steps = facts[:, 0]
+    angle = (all_steps / 1000.0 + 0.008) / 1.008 * (math.pi / 2)
+    signal = jnp.cos(angle) ** 2
+    ratio = signal / (1.0 - signal)
+    all_weights = facts[:, 1] * jnp.minimum(ratio, SNR_LIMIT) / ratio
+    weight_total = jnp.sum(all_weights)
+    signal = lax.dynamic_slice_in_dim(signal, clip_id, 1, 0)
+    loss_weight = lax.dynamic_slice_in_dim(all_weights, clip_id, 1, 0)
+
+    freq_in = sincos(all_steps, TFREQ).astype(jnp.bfloat16)
+    at_start = clip_id == 0
+    time_one = emb_rows[ROW_TIME_ONE:ROW_TIME_TWO]
+    time_two = emb_rows[ROW_TIME_TWO:ROW_BLOCK]
+    pre_one = matmul_low(freq_in, time_one) + time_b1
+    act_one = jax.nn.silu(pre_one).astype(jnp.bfloat16)
+    time_embed = matmul_low(act_one, time_two) + time_b2
+    early = jnp.concatenate(
+        [pre_one, time_embed, emb_rows[:ROW_TIME_ONE].astype(jnp.float32)], 0
+    )
+    early = sum_clips(jnp.where(at_start, early, 0.0))
+    pre_one, time_embed = early[:n_clip], early[n_clip : 2 * n_clip]
+    patch_w = early[2 * n_clip :].astype(jnp.bfloat16)
+    act_one = jax.nn.silu(pre_one).astype(jnp.bfloat16)
+    silu_time = jax.nn.silu(time_embed).astype(jnp.bfloat16)
+    local_row = emb_first + jnp.arange(EMB_PAD, dtype=jnp.int32)
+    block_row = local_row - ROW_BLOCK
+    in_block = (block_row >= 0) & (block_row < 6 * D)
+    block_part = jnp.where(in_block, block_row % 6, -1)
+    block_line = jnp.where(in_block, block_row // 6, -1)
+    chooser = jnp.arange(D, dtype=jnp.int32)[:, None] == block_line[None]
+    silu_rows = matmul_low(silu_time, chooser.astype(jnp.bfloat16)).astype(jnp.bfloat16)
+    part_mask = jnp.arange(6, dtype=jnp.int32)[:, None] == block_part[None]
+    block_left = jnp.where(part_mask[None], silu_rows[:, None], 0).reshape(n_clip * 6, EMB_PAD)
+    block_out = sum_clips(matmul_low(block_left, emb_rows)).reshape(n_clip, 6, D)
+    all_mods = table[None] + (block_out + block_b.reshape(6, D))
+    mods = lax.dynamic_slice_in_dim(all_mods, clip_id, 1, 0)
+    my_embed = lax.dynamic_slice_in_dim(time_embed, clip_id, 1, 0)
+
+    keep_part = jnp.sqrt(signal)[:, None, None, None]
+    fade_part = jnp.sqrt(1.0 - signal)[:, None, None, None]
+    noisy = (keep_part * latents + fade_part * noise).astype(jnp.bfloat16)
+    frame_ids = frame_id * frame_dev + jnp.arange(frame_dev)
+    patch_ids = jnp.arange(patches)
+    place = jnp.concatenate(
+        [sincos(patch_ids // PGRID, D // 2), sincos(patch_ids % PGRID, D // 2)], -1
+    )[None, None]
+    hidden_zero = matmul_low(noisy, patch_w) + patch_b + place + sincos(frame_ids, D)[None, :, None]
+
+    def mod_row(number):
+        return mods[:, number][:, None, None, :]
+
+    is_null = null_flags == 1
+    cap_in = jnp.where(is_null[:, None, None], null_caption[None], captions)
+    cap_pre = (matmul_low(to_cap_rows(cap_in[0]), cap_weights) + cap_b1)[None]
+    cap_act = gelu_tanh(cap_pre).astype(jnp.bfloat16)
+    act_rows = jnp.pad(cap_act[0], ((0, 0), (two_first, EMB_PAD - two_first - D)))
+    cap_rows = (matmul_low(act_rows, cap_last) + cap_b2).astype(jnp.bfloat16)[None]
+    live_len = jnp.where(is_null, L_CAP, cap_lengths)
+    key_mask = jnp.arange(L_CAP)[None, :] < live_len[:, None]
+    cap_wide = jnp.concatenate([cap_in[0], cap_act[0]], -1)
+    cap_wide = jnp.pad(cap_wide, ((0, 0), (EMB_PAD, EMB_PAD)))
+    wanted = []
+    for owner in range(n_clip):
+        start = EMB_FIRST[owner] - ROW_CAP_ONE + EMB_PAD
+        if start + EMB_PAD <= EMB_PAD:
+            wanted.append(jnp.zeros((L_CAP, EMB_PAD // 4), jnp.bfloat16))
+        else:
+            wanted.append(
+                lax.dynamic_slice_in_dim(cap_wide, start + frame_id * (EMB_PAD // 4), EMB_PAD // 4, 1)
+            )
+    cap_left = lax.all_to_all(jnp.stack(wanted), "clip", split_axis=0, concat_axis=0, tiled=True)
+    cap_left = cap_left.reshape(n_clip * L_CAP, EMB_PAD // 4)
+
+    def flat2(value):
+        return value.reshape(-1, value.shape[-1])
+
+    space_in = modulate(hidden_zero, mod_row(0), mod_row(1)).astype(jnp.bfloat16)
+    space_q, space_k, space_v = (
+        heads_of(piece, clip_dev * frame_dev)
+        for piece in split_qkv(matmul_low(space_in, space_qkv), space_bq, space_bv)
+    )
+    space_o, space_lse = attend_forward(space_q, space_k, space_v, None)
+    space_flat = space_o.reshape(clip_dev, frame_dev, patches, D)
+    space_res = matmul_low(space_flat, space_out) + space_bo
+    hidden_one = hidden_zero + mod_row(2) * space_res
+    time_in = lax.all_to_all(
+        hidden_one.astype(jnp.bfloat16), "frame", split_axis=2, concat_axis=1, tiled=True
+    )
+    time_in = jnp.swapaxes(time_in, 1, 2)
+    frames = time_in.shape[2]
+    time_q, time_k, time_v = (
+        heads_of(piece, clip_dev * local_pos)
+        for piece in split_qkv(matmul_low(time_in, time_qkv), time_bq, time_bv)
+    )
+    time_o, time_lse = attend_forward(time_q, time_k, time_v, None)
+    time_back = jnp.swapaxes(time_o.reshape(clip_dev, local_pos, frames, D), 1, 2)
+    time_flat = lax.all_to_all(time_back, "frame", split_axis=1, concat_axis=2, tiled=True)
+    time_res = matmul_low(time_flat, time_out) + time_bo
+    hidden_two = hidden_one + mod_row(2) * time_res
+    cross_in = hidden_two.astype(jnp.bfloat16)
+    cross_query = heads_of(
+        (matmul_low(cross_in, cross_q) + cross_bq).astype(jnp.bfloat16), clip_dev
+    )
+    cross_merged = matmul_low(cap_rows, cross_kv)
+    cross_k = heads_of(cross_merged[..., :D].astype(jnp.bfloat16), clip_dev)
+    cross_v = heads_of((cross_merged[..., D:] + cross_bv).astype(jnp.bfloat16), clip_dev)
+    cross_o, cross_lse = attend_forward(cross_query, cross_k, cross_v, key_mask)
+    cross_flat = cross_o.reshape(clip_dev, frame_dev, patches, D)
+    hidden_three = hidden_two + matmul_low(cross_flat, cross_out) + cross_bo
+    dense_in = modulate(hidden_three, mod_row(3), mod_row(4)).astype(jnp.bfloat16)
+    dense_pre = matmul_low(dense_in, fc_in) + fc_in_b
+    dense_act = gelu_tanh(dense_pre).astype(jnp.bfloat16)
+    dense_res = matmul_low(dense_act, fc_out) + fc_out_b
+    hidden_four = hidden_three + mod_row(5) * dense_res
+    final_mod = final_table[None] + my_embed[:, None, :]
+    final_shift = final_mod[:, 0][:, None, None, :]
+    final_scale = final_mod[:, 1][:, None, None, :]
+    final_in = modulate(hidden_four, final_shift, final_scale).astype(jnp.bfloat16)
+    predicted = matmul_low(final_in, final_w) + final_b
+    miss = predicted - noise
+    clip_error = jnp.sum(jnp.mean(miss * miss, -1), (1, 2))
+    local_loss = jnp.sum(loss_weight * clip_error)
+
+    inputs = {}
+    for label, value in (
+        ("space_qkv", space_in),
+        ("space_out", space_flat),
+        ("time_qkv", time_in),
+        ("time_out", time_flat),
+        ("cross_q", cross_in),
+        ("cross_out", cross_flat),
+        ("fc_in", dense_in),
+    ):
+        segments = DENSE_SEGS if label == "fc_in" else ATTEND_SEGS
+        inputs[label] = pick_columns(both_cores(flat2(value)), half_rows(segments, label), core_id)
+    act_both = both_cores(flat2(dense_act))
+    half = half_rows([[("square", 0, D, 1)]], "square")
+    for block in range(MLP // D):
+        inputs["fc_out", block] = pick_columns(act_both[:, block * D : (block + 1) * D], half, core_id)
+
+    def core_grad(left, outs):
+        return [weight_grad(left, both_cores(flat2(out))) for out in outs]
+
+    def columns(value):
+        return [value[..., j * D : (j + 1) * D] for j in range(value.shape[-1] // D)]
+
+    grad_pred = (
+        2.0 / miss.shape[-1] * (loss_weight / weight_total)[:, None, None, None] * miss
+    ).astype(jnp.bfloat16)
+    g_final_w = weight_grad(final_in, grad_pred)
+    g_final_b = bias_grad(grad_pred)
+    unused, pullback = jax.vjp(modulate, hidden_four, final_shift, final_scale)
+    grad_hidden, grad_fshift, grad_fscale = pullback(back_low(grad_pred, final_w))
+    grad_fmod = jnp.concatenate([grad_fshift.reshape(1, D), grad_fscale.reshape(1, D)], 0)
+    grad_dense = (grad_hidden * mod_row(5)).astype(jnp.bfloat16)
+    grad_gate_b = jnp.sum(grad_hidden * dense_res, (1, 2))
+    grads = {}
+    dense_both = both_cores(flat2(grad_dense))
+    g_fc_out = [weight_grad(inputs["fc_out", block], dense_both) for block in range(MLP // D)]
+    grads["fc_out"] = [jnp.concatenate(g_fc_out, 0)]
+    g_fc_out_b = bias_grad(grad_dense)
+    unused, pullback = jax.vjp(gelu_tanh, dense_pre)
+    grad_pre = pullback(back_low(grad_dense, fc_out))[0].astype(jnp.bfloat16)
+    grads["fc_in"] = core_grad(inputs["fc_in"], columns(grad_pre))
+    g_fc_in_b = bias_grad(grad_pre)
+    dense_parts = [
+        reduce_pair(pair_chunks(grads, DENSE_SEGS, z), z, z % 2 == 1, x_id, y_id)
+        for z in (3, 2, 1, 0)
+    ][::-1]
+    unused, pullback = jax.vjp(modulate, hidden_three, mod_row(3), mod_row(4))
+    grad_input, grad_shift_b, grad_scale_b = pullback(back_low(grad_pre, fc_in))
+    grad_hidden = grad_hidden + grad_input
+    grad_cross = grad_hidden.astype(jnp.bfloat16)
+    grads["cross_out"] = core_grad(inputs["cross_out"], [grad_cross])
+    g_cross_bo = bias_grad(grad_cross)
+    grad_cross_o = heads_of(back_low(grad_cross, cross_out).astype(jnp.bfloat16), clip_dev)
+    grad_cq, grad_ck, grad_cv = attend_backward(
+        cross_query, cross_k, cross_v, key_mask, cross_lse, grad_cross_o
+    )
+    grad_cq = grad_cq.astype(jnp.bfloat16).reshape(clip_dev, frame_dev, patches, D)
+    grads["cross_q"] = core_grad(inputs["cross_q"], [grad_cq])
+    g_cross_bq = bias_grad(grad_cq)
+    grad_hidden = grad_hidden + back_low(grad_cq, cross_q)
+    grad_cv = grad_cv.reshape(clip_dev, L_CAP, D)
+    grad_ckv = jnp.concatenate([grad_ck.reshape(clip_dev, L_CAP, D), grad_cv], -1)[0]
+    g_cross_bv = bias_grad(grad_cv)
+    grad_ckv = grad_ckv + shift(grad_ckv, SWAP_CORE)
+    cap_half = pick_columns(cap_rows[0], half_rows(ATTEND_SEGS, "cross_kv"), core_id)
+    grads["cross_kv"] = [weight_split(cap_half, part) for part in columns(grad_ckv)]
+    grad_ckv = grad_ckv + shift(grad_ckv, SWAP_X)
+    grad_cap_rows = back_split(grad_ckv, cross_kv)
+
+    def reduce_attend(z, x_first):
+        return reduce_pair(pair_chunks(grads, ATTEND_SEGS, z), z, x_first, x_id, y_id)
+
+    attend_parts = [None] * Z_SIZE
+    attend_parts[3] = reduce_attend(3, True)
+    grad_time = (grad_hidden * mod_row(2)).astype(jnp.bfloat16)
+    grads["time_out"] = core_grad(inputs["time_out"], [grad_time])
+    g_time_bo = bias_grad(grad_time)
+    grad_time_o = lax.all_to_all(
+        back_low(grad_time, time_out).astype(jnp.bfloat16),
+        "frame",
+        split_axis=2,
+        concat_axis=1,
+        tiled=True,
+    )
+    grad_time_o = heads_of(jnp.swapaxes(grad_time_o, 1, 2), clip_dev * local_pos)
+    grad_tq, grad_tk, grad_tv = attend_backward(time_q, time_k, time_v, None, time_lse, grad_time_o)
+    grad_tqkv = [
+        piece.astype(jnp.bfloat16).reshape(clip_dev, local_pos, frames, D)
+        for piece in (grad_tq, grad_tk, grad_tv)
+    ]
+    grads["time_qkv"] = core_grad(inputs["time_qkv"], grad_tqkv)
+    g_time_bq = bias_grad(grad_tqkv[0])
+    g_time_bv = bias_grad(grad_tqkv[2])
+    grad_tqkv = lax.all_to_all(
+        jnp.swapaxes(jnp.concatenate(grad_tqkv, -1), 1, 2), "frame", split_axis=1, concat_axis=2, tiled=True
+    )
+    attend_parts[2] = reduce_attend(2, False)
+    grad_gate_a = jnp.sum(grad_hidden * time_res, (1, 2))
+    grad_hidden = grad_hidden + back_low(grad_tqkv, time_qkv)
+    grad_gate_a = grad_gate_a + jnp.sum(grad_hidden * space_res, (1, 2))
+    grad_space = (grad_hidden * mod_row(2)).astype(jnp.bfloat16)
+    grads["space_out"] = core_grad(inputs["space_out"], [grad_space])
+    g_space_bo = bias_grad(grad_space)
+    attend_parts[1] = reduce_attend(1, True)
+    grad_space_o = heads_of(
+        back_low(grad_space, space_out).astype(jnp.bfloat16), clip_dev * frame_dev
+    )
+    grad_sqkv = [
+        piece.astype(jnp.bfloat16).reshape(clip_dev, frame_dev, patches, D)
+        for piece in attend_backward(space_q, space_k, space_v, None, space_lse, grad_space_o)
+    ]
+    grads["space_qkv"] = core_grad(inputs["space_qkv"], grad_sqkv)
+    attend_parts[0] = reduce_attend(0, False)
+    g_space_bq = bias_grad(grad_sqkv[0])
+    g_space_bv = bias_grad(grad_sqkv[2])
+    grad_sqkv = jnp.concatenate(grad_sqkv, -1)
+    unused, pullback = jax.vjp(modulate, hidden_zero, mod_row(0), mod_row(1))
+    grad_input, grad_shift_a, grad_scale_a = pullback(back_low(grad_sqkv, space_qkv))
+    grad_hidden = grad_hidden + grad_input
+    g_patch_w = weight_split(noisy, grad_hidden)
+    g_patch_b = bias_grad(grad_hidden)
+    grad_mods = jnp.concatenate(
+        [
+            grad_shift_a.reshape(clip_dev, D),
+            grad_scale_a.reshape(clip_dev, D),
+            grad_gate_a,
+            grad_shift_b.reshape(clip_dev, D),
+            grad_scale_b.reshape(clip_dev, D),
+            grad_gate_b,
+            grad_fmod,
+        ],
+        0,
+    )
+
+    unused, pullback = jax.vjp(gelu_tanh, cap_pre[0])
+    grad_cap_pre = pullback(back_split(grad_cap_rows, cap_last)[:, two_first : two_first + D])[0]
+    cap_right = lax.all_gather(
+        jnp.stack([grad_cap_pre, grad_cap_rows]), "clip", axis=1, tiled=True
+    )
+    null_sum = jnp.where(is_null[0], grad_cap_pre, 0.0)
+    g_cap_b1 = bias_grad(grad_cap_pre)
+    g_cap_b2 = bias_grad(grad_cap_rows)
+
+    once = frame_id == 0
+    gathered_mods = jnp.where(own_clip[:, None, None], grad_mods[None], 0.0)
+    zero_d = jnp.zeros((D,), jnp.float32)
+    vector_grad = flatten_all(
+        [
+            g_patch_b,
+            jnp.where(once, g_cap_b1, 0.0),
+            jnp.where(once, g_cap_b2, 0.0),
+            g_space_bq,
+            g_space_bv,
+            g_space_bo,
+            g_time_bq,
+            g_time_bv,
+            g_time_bo,
+            g_cross_bq,
+            g_cross_bv,
+            g_cross_bo,
+            g_fc_in_b,
+            g_fc_out_b,
+            g_final_b,
+        ]
+    )
+    vector_grad, gathered_mods, g_patch_w, g_final_w, loss_sum, null_sum = lax.psum(
+        (
+            vector_grad,
+            gathered_mods,
+            g_patch_w,
+            g_final_w,
+            local_loss,
+            jnp.where(once, null_sum, 0.0),
+        ),
+        AXES,
+    )
+
+    grad_zero = gathered_mods[:, :6]
+    grad_final = gathered_mods[:, 6:]
+    zero_rows = grad_zero.reshape(n_clip * 6, D)
+    back_rows = two_parts(lambda part: back_low(part, emb_rows), zero_rows)
+    back_rows = jnp.sum(jnp.where(part_mask[None], back_rows.reshape(n_clip, 6, EMB_PAD), 0.0), 1)
+    grad_silu = lax.dot_general(
+        back_rows,
+        chooser.astype(jnp.float32),
+        (((1,), (1,)), ((), ())),
+        precision=lax.Precision.HIGHEST,
+        preferred_element_type=jnp.float32,
+    )
+    grad_silu = sum_clips(grad_silu)
+    unused, pullback = jax.vjp(jax.nn.silu, time_embed)
+    grad_embed = grad_final[:, 0] + grad_final[:, 1] + pullback(grad_silu)[0]
+    grad_act = two_parts(lambda part: back_low(part, time_two), grad_embed)
+    grad_act = sum_clips(jnp.where(at_start, grad_act, 0.0))
+    unused, pullback = jax.vjp(jax.nn.silu, pre_one)
+    grad_one = pullback(grad_act)[0]
+    g_table = jnp.sum(grad_zero, 0)
+    vector_sum = flatten_all(
+        [
+            vector_grad[:D],
+            jnp.sum(grad_one, 0),
+            jnp.sum(grad_embed, 0),
+            g_table,
+            vector_grad[D:],
+            g_table,
+            jnp.sum(grad_final, 0),
+        ]
+    )
+
+    per = EMB_PAD // 4
+    quarter_row = emb_first + frame_id * per + jnp.arange(per, dtype=jnp.int32)
+    time_left = jnp.concatenate(
+        [
+            jnp.pad(freq_in, ((0, 0), (ROW_TIME_ONE, EMB_PAD - ROW_TIME_TWO))),
+            jnp.pad(act_one, ((0, 0), (ROW_TIME_TWO, EMB_PAD - ROW_BLOCK))),
+        ],
+        0,
+    )
+    time_left = jnp.where(at_start, time_left, jnp.zeros_like(time_left))
+    small_left = lax.dynamic_slice_in_dim(
+        jnp.concatenate([time_left, block_left], 0), frame_id * per, per, 1
+    )
+    small_right = jnp.concatenate([grad_one, grad_embed, zero_rows], 0)
+    first_kind = (quarter_row < ROW_CAP_TWO)[None]
+    no_left = jnp.zeros_like(cap_left)
+    emb_left = jnp.concatenate(
+        [
+            small_left,
+            jnp.where(first_kind, cap_left, no_left),
+            jnp.where(first_kind, no_left, cap_left),
+        ],
+        0,
+    )
+    emb_right = jnp.concatenate([small_right, cap_right[0], cap_right[1]], 0)
+    emb_grad = two_parts(lambda part: weight_grad(emb_left, part), emb_right)
+    g_null = from_cap_rows(two_parts(lambda part: back_low(part, cap_weights), null_sum))
+    null_rows = jnp.pad(g_null.reshape(-1), (0, (EMB_PAD - (ROW_NULL - EMB_FIRST[last])) * D - null_end))
+    tail_rows = jnp.concatenate(
+        [
+            jnp.zeros((ROW_FINAL - EMB_FIRST[last], D), jnp.float32),
+            g_final_w.reshape(PATCH_VALUES, D),
+            null_rows.reshape(-1, D),
+        ],
+        0,
+    )
+    head_rows = jnp.pad(g_patch_w, ((0, EMB_PAD - PATCH_VALUES), (0, 0)))
+    extra = jnp.where(clip_id == last, tail_rows, jnp.where(at_start, head_rows, 0.0))
+    emb_grad = emb_grad + lax.dynamic_slice_in_dim(extra, frame_id * per, per, 0)
+    unit = (
+        LANE_TILES * (frame_id * per + jnp.arange(per, dtype=jnp.int32))[:, None]
+        + jnp.arange(D, dtype=jnp.int32)[None] // LANES
+        - emb_shift
+    )
+    emb_grad = jnp.where((unit >= 0) & (unit < EMB_UNITS), emb_grad, 0.0)
+
+    attend_part = choose_z(attend_parts, z_id).reshape(-1, D)
+    dense_part = choose_z(dense_parts, z_id).reshape(-1, D)
+    local_square = sum(jnp.sum(part * part) for part in (attend_part, dense_part, emb_grad))
+    grad_norm = jnp.sqrt(lax.psum(local_square, AXES) + jnp.sum(vector_sum * vector_sum))
+    factor = jnp.minimum(1.0, CLIP_LIMIT / (grad_norm + NORM_FLOOR))
+
+    def four_parts(part):
+        over_x = shift(part, SWAP_X)
+        return [part, over_x, shift(part, SWAP_CORE), shift(over_x, SWAP_CORE)]
+
+    spots = jnp.stack(
+        [
+            core_id * 2 + x_id,
+            core_id * 2 + 1 - x_id,
+            (1 - core_id) * 2 + x_id,
+            (1 - core_id) * 2 + 1 - x_id,
+        ]
+    ).astype(jnp.int32)
+    scale = factor.reshape(1)
+    dense_r = step_shard(
+        four_parts(dense_part),
+        spots,
+        jnp.asarray(step_table(DENSE_SEGS, STEP_BLOCK, DENSE_ROWS))[clip_id],
+        (1, 4),
+        DENSE_ROWS,
+        scale,
+        (dense_w, dense_m, dense_v, dense_e),
+    )
+    attend_r = step_shard(
+        four_parts(attend_part),
+        spots,
+        jnp.asarray(step_table(ATTEND_SEGS, STEP_BLOCK, ATTEND_ROWS))[clip_id],
+        (1, 2, 3),
+        ATTEND_ROWS,
+        scale,
+        (attend_w, attend_m, attend_v, attend_e),
+    )
+    emb_parts = four_parts(emb_grad)
+    emb_whole = jnp.zeros((4, per, D), jnp.float32)
+    for part, flip in zip(emb_parts, (0, 2, 1, 3)):
+        emb_whole = lax.dynamic_update_index_in_dim(emb_whole, part, frame_id ^ flip, 0)
+    emb_flat = rows_to_flat(emb_whole.reshape(EMB_PAD, D))
+    emb_owned = lax.dynamic_slice_in_dim(emb_flat, emb_shift, EMB_UNITS, 0).reshape(-1)
+    embed_r = adam_step(embed_w, emb_owned, embed_m, embed_v, embed_e, factor)
+    vector_r = adam_step(vector_w, vector_sum, vector_m, vector_v, vector_e, factor)
+    return (
+        loss_sum,
+        weight_total,
+        grad_norm,
+        embed_r[0],
+        attend_r[0],
+        dense_r[0],
+        vector_r[0],
+        embed_r[1],
+        attend_r[1],
+        dense_r[1],
+        vector_r[1],
+        embed_r[2],
+        attend_r[2],
+        dense_r[2],
+        vector_r[2],
+        embed_r[3],
+        attend_r[3],
+        dense_r[3],
+        vector_r[3],
+    )
+
+
+def pick_plan(mesh):
+    if mesh.shape["frame"] == X_SIZE * CORES and mesh.shape["clip"] == N_OWN:
+        return shards_block
+    return shards
+
+
 def solution(mesh):
     in_specs = (
         P("clip", "frame", None, None),
@@ -579,4 +1616,4 @@
         P("clip"),
         P(),
     )
-    return jax.shard_map(shards, mesh=mesh, in_specs=in_specs, out_specs=out_specs, check_vma=False)
+    return jax.shard_map(pick_plan(mesh), mesh=mesh, in_specs=in_specs, out_specs=out_specs, check_vma=False)

time: 6530 us -> 2600 us (0.40)
  waiting for transfers between devices: 4370 us -> 862 us
  local copies, waits for them, and re-layouts: 1260 us -> 350 us
  starting transfers between devices: 18.7 us -> 571 us
  other arithmetic: 412 us -> 247 us
  Pallas kernels: 0 us -> 102 us
    unnamed x10 -> x2, waiting for transfers between devices: 2200 us -> 0.03 us
    all_gather x6 -> x1, waiting for transfers between devices: 2140 us -> 0.01 us  [shards_block(): lax.all_gather(jnp.stack([grad_cap_pre, grad_cap_rows]), 'clip', axis=1,...]
    ppermute x0 -> x173, waiting for transfers between devices: none -> 641 us  [shift(): return lax.ppermute(value, AXES, perm)]
    ppermute x0 -> x173, starting transfers between devices: none -> 546 us  [shift(): return lax.ppermute(value, AXES, perm)]
    reshape x18 -> x17, local copies, waits for them, and re-layouts: 297 us -> 33.1 us  [the longest x3 10.3 us: shards_block(): piece.astype(jnp.bfloat16).reshape(clip_dev, local_pos, frames, D)]
    unnamed x465 -> x643, local copies, waits for them, and re-layouts: 336 us -> 88.2 us
    psum x0 -> x1, waiting for transfers between devices: none -> 210 us  [shards_block(): lax.psum((vector_grad, gathered_mods, g_patch_w, g_final_w, local_loss, j...]
    all_gather x1 -> x0, other arithmetic: 196 us -> none  [shards(): lax.all_gather(embed_w.astype(jnp.bfloat16), 'clip', axis=0, tiled=True)]
  transfers between devices with their start and end apart: 12 -> 180, of which waited for: 10 -> 40; matrix products, arithmetic and copies ran while one was open for 13% -> 32% of each run, Pallas kernels for 0% -> 4%
where the time goes in v1:
time: 2600 us; the launch traced here: 2580 us
  waiting for transfers between devices  862 us (33%)
  starting transfers between devices  571 us (22%)
  matrix products  369 us (14%)
  local copies, waits for them, and re-layouts  350 us (13%)
  other arithmetic  247 us (10%)
  Pallas kernels  102 us (4%)
  between operations  38.7 us (1%)
  blocking collectives  37.8 us (1%)
    ppermute x173, waiting for transfers between devices, shift(): return lax.ppermute(value, AXES, perm)  641 us
    ppermute x173, starting transfers between devices, shift(): return lax.ppermute(value, AXES, perm)  546 us
    psum x1, waiting for transfers between devices, shards_block(): lax.psum((vector_grad, gathered_mods, g_patch_w, g_final_w, local_loss, j...  210 us
    dot_general x27, matrix products, weight_grad(): lax.dot_general(left, right, (((0,), (0,)), ((), ())), preferred_element_...  112 us
    dot_general x19, matrix products, back_low(): lax.dot_general(grads, weight, (((grads.ndim - 1,), (1,)), ((), ())), pre...  108 us
    dot_general x21, matrix products, matmul_low(): lax.dot_general(left, right, (((left.ndim - 1,), (0,)), ((), ())), prefer...  93.2 us
    unnamed x643, local copies, waits for them, and re-layouts  88.2 us
  transfers between devices with their start and end apart: 180, of which 40 were waited for; matrix products, arithmetic and copies ran while one was open for 32% of the time, Pallas kernels for 4%

profile of v1, /device:TPU:0, one launch (start us, length us, event | category | flops | bytes accessed | tf_op | source)
XLA Modules:
  0.0 2577.8 jit_solution(11059458583399707745)
XLA Ops:
  19.4 20.8 dynamic_update_slice.16.flat
  137.7 27.1 %collective-permute-done.7 = f32[48,1152]{1,0:T(8,128)S(1)} collective-permute-done((f32[48,1152]{1,0:T(8,128)S(1)}, f32[48,1152]{1,0:T(8,128)S(1)}, u32[]{:S(2)}, u32[]{:S(2)}) %collective-permute-start.7) | collective-permute-done | bytes 221216 | tf_op jit(solution)/shard_map/ppermute | solution.py:599
  166.5 24.6 collective-permute-start.8
  325.5 20.0 collective-permute-done.49.refs_12_
  368.3 20.2 collective-permute-done.18.refs_9_
  463.6 20.8 collective-permute-done.30.refs_21_
  484.4 20.9 collective-permute-done.34.refs_25_
  553.0 22.2 shard_map.557
  685.7 18.8 collective-permute-done.62.refs_25_
  1276.8 210.4 %all-reduce.15.cloned.1.call-done = (f32[8,8,1152]{2,0,1:T(8,128)}, f32[16,1152]{1,0:T(8,128)}, f32[16,1152]{1,0:T(8,128)}, f32[120,1152]{1,0:T(8,128)}, f32[19600]{0:T(1024)}) async-done(((f32[8,8,1152]{2,0,1:T(8,128)}, f32[16,1152]{1,0:T(8,128)}, f32[16,1152]{1,0:T(8,128)}, f32[120,1152]{1,0:T(8,128)}, f32[19600]{0:T(1024)}), (f32[8,8,1152]{2,0,1:T(8,128)}, f32[16,1152]{1,0:T(8,128)}, ...) | async-done | bytes 1073744 | tf_op jit(solution)/shard_map/psum | solution.py:1408
  1589.9 18.2 collective-permute-done.96
  1617.1 18.6 collective-permute-done.153
  1657.3 76.2 %collective-permute-done.125 = f32[2,432,1152]{2,1,0:T(8,128)} collective-permute-done((f32[2,432,1152]{2,1,0:T(8,128)}, f32[2,432,1152]{2,1,0:T(8,128)}, u32[]{:S(2)}, u32[]{:S(2)}) %collective-permute-start.125) | collective-permute-done | bytes 3981344 | tf_op jit(solution)/shard_map/ppermute | solution.py:599
  1738.4 95.0 %collective-permute-done.97 = f32[432,1152]{1,0:T(8,128)} collective-permute-done((f32[432,1152]{1,0:T(8,128)}, f32[432,1152]{1,0:T(8,128)}, u32[]{:S(2)}, u32[]{:S(2)}) %collective-permute-start.97) | collective-permute-done | bytes 1990688 | tf_op jit(solution)/shard_map/ppermute | solution.py:599
  1848.7 31.2 %collective-permute-done.126 = f32[432,1152]{1,0:T(8,128)} collective-permute-done((f32[432,1152]{1,0:T(8,128)}, f32[432,1152]{1,0:T(8,128)}, u32[]{:S(2)}, u32[]{:S(2)}) %collective-permute-start.126) | collective-permute-done | bytes 1990688 | tf_op jit(solution)/shard_map/ppermute | solution.py:599
  1889.4 46.0 %collective-permute-done.132 = f32[2,288,1152]{2,1,0:T(8,128)S(1)} collective-permute-done((f32[2,288,1152]{2,1,0:T(8,128)}, f32[2,288,1152]{2,1,0:T(8,128)S(1)}, u32[]{:S(2)}, u32[]{:S(2)}) %collective-permute-start.132) | collective-permute-done | bytes 2654240 | tf_op jit(solution)/shard_map/ppermute | solution.py:599
  1975.3 116.5 %collective-permute-start.112 = (f32[432,1152]{1,0:T(8,128)}, f32[432,1152]{1,0:T(8,128)}, u32[]{:S(2)}, u32[]{:S(2)}) collective-permute-start(f32[432,1152]{1,0:T(8,128)} %add.1431), channel_id=1, source_target_pairs={{0,2},{1,3},{8,10},{9,11},{16,18},{17,19},{24,26},{25,27}} | collective-permute-start | bytes 5971976 | tf_op jit(solution)/shard_map/ppermute | solution.py:599
  2193.6 47.1 %collective-permute-start.120 = (f32[432,1152]{1,0:T(8,128)}, f32[432,1152]{1,0:T(8,128)}, u32[]{:S(2)}, u32[]{:S(2)}) collective-permute-start(f32[432,1152]{1,0:T(8,128)} %add.1438), channel_id=1, source_target_pairs={{0,2},{1,3},{8,10},{9,11},{16,18},{17,19},{24,26},{25,27}} | collective-permute-start | bytes 5971976 | tf_op jit(solution)/shard_map/ppermute | solution.py:599
  2268.2 21.6 concatenate.214
  2367.4 72.9 %collective-permute-done.170.refs_1_ = f32[288,1152]{1,0:T(8,128)} collective-permute-done((f32[288,1152]{1,0:T(8,128)}, f32[288,1152]{1,0:T(8,128)}, u32[]{:S(2)}, u32[]{:S(2)}) %collective-permute-start.170) | collective-permute-done | bytes 1327136 | tf_op jit(solution)/shard_map/ppermute | solution.py:599
  2444.5 37.8 %all-reduce.11 = (f32[]{:T(128)}, f32[]{:T(128)}) all-reduce(f32[]{:T(128)} %bitcast.93, f32[]{:T(128)S(6)} %add.1504), channel_id=1, replica_groups=mesh['frame'=4,'clip'=8] {'frame','clip'}, use_global_device_ids=true, to_apply=%region_14.15 | all-reduce | flops 2 | bytes 16 | tf_op jit(solution)/shard_map/psum | solution.py:1408
  2485.4 19.5 shard_map.563
  2509.1 27.4 %shard_map.562 = (f32[15552,128]{1,0:T(8,128)}, f32[15552,128]{1,0:T(8,128)}, f32[15552,128]{1,0:T(8,128)}, f32[15552,128]{1,0:T(8,128)}) custom-call(s32[6,3]{1,0:T(8,128)S(1)} %copy.453.table, s32[4]{0:T(128)S(1)} %pad_add_fusion.places, f32[1]{0:T(128)} %bitcast.222.factor, f32[432,1152]{1,0:T(8,128)S(1)} %get-tuple-element.106.refs_0_, ...), custom_call_target="tpu_custom_call" | custom-call | tf_op jit(solution)/shard_map/pallas_call | solution.py:967
  2542.2 26.7 %multiply_add_fusion.1 = (f32[2019840]{0:T(1024)}, f32[2019840]{0:T(1024)}, f32[2019840]{0:T(1024)}, f32[2019840]{0:T(1024)}) fusion(f32[2019840]{0:T(1024)} %param.63, f32[2019840]{0:T(1024)} %param.51, f32[]{:T(128)} %min.7, f32[16128,128]{1,0:T(8,128)} %copy-done.4, s32[]{:T(128)S(6)} %select_n.501, f32[2019840]{0:T(1024)} %param.55, f32[2019840]{0:T(1024)} %param.59), kind=kLoop, calls=%fused_computation.55 | loop fusion | flops 36357120 | bytes 72714248 | tf_op jit(solution)/shard_map/add | solution.py:209
  (1433 shorter events, 1478.5 us)
Async XLA Ops:
  814.8 171.4 %collective-permute-start.101 = (bf16[512,1152]{1,0:T(8,128)(2,1)}, bf16[512,1152]{1,0:T(8,128)(2,1)}, u32[]{:S(2)}, u32[]{:S(2)}) collective-permute-start(bf16[512,1152]{1,0:T(8,128)(2,1)} %bitcast.701), channel_id=1, source_target_pairs={{0,8},{1,9},{2,10},{3,11},{4,12},{5,13},{6,14},{7,15},{8,0},{9,1},... | collective-permute-start | bytes 3538952 | tf_op jit(solution)/shard_map/ppermute | solution.py:599
  1041.8 131.0 %all-to-all-start.3 = ((bf16[1,8,64,3456]{3,2,0,1:T(8,128)(2,1)}), bf16[1,8,64,3456]{3,2,0,1:T(8,128)(2,1)}, u32[]{:S(2)}, u32[]{:S(2)}) async-start(bf16[1,8,64,3456]{3,2,0,1:T(8,128)(2,1)} %copy.433), calls=%async_computation.3 | async-start | bytes 7077888 | tf_op jit(solution)/shard_map/all_to_all | solution.py:1336
  1046.7 440.5 %all-reduce.15.cloned.1.call-start = ((), (), s32[]{:S(2)}) async-start(), calls=%async_computation.6 | async-start | bytes 2154496 | tf_op jit(solution)/shard_map/psum | solution.py:1408
  1069.8 460.8 %collective-permute-start.114 = (bf16[512,1152]{0,1:T(8,128)(2,1)}, bf16[512,1152]{0,1:T(8,128)(2,1)}, u32[]{:S(2)}, u32[]{:S(2)}) collective-permute-start(bf16[512,1152]{0,1:T(8,128)(2,1)} %bitcast.269), channel_id=1, source_target_pairs={{0,8},{1,9},{2,10},{3,11},{4,12},{5,13},{6,14},{7,15},{8,0},{9,1},... | collective-permute-start | bytes 3538952 | tf_op jit(solution)/shard_map/ppermute | solution.py:599
  1095.4 450.3 %collective-permute-start.130 = (bf16[512,4608]{1,0:T(8,128)(2,1)}, bf16[512,4608]{1,0:T(8,128)(2,1)}, u32[]{:S(2)}, u32[]{:S(2)}) collective-permute-start(bf16[512,4608]{1,0:T(8,128)(2,1)} %bitcast.162), channel_id=1, source_target_pairs={{0,8},{1,9},{2,10},{3,11},{4,12},{5,13},{6,14},{7,15},{8,0},{9,1},... | collective-permute-start | bytes 14155784 | tf_op jit(solution)/shard_map/ppermute | solution.py:599
  1138.9 133.3 %collective-permute-start.152 = (f32[2,288,1152]{2,1,0:T(8,128)}, f32[2,288,1152]{2,1,0:T(8,128)}, u32[]{:S(2)}, u32[]{:S(2)}) collective-permute-start(f32[2,288,1152]{2,1,0:T(8,128)} %fusion.110), channel_id=1, source_target_pairs={{0,1},{1,0},{2,3},{3,2},{4,5},{5,4},{6,7},{7,6},{8,9},{9,8},{10,11... | collective-permute-start | bytes 7962632 | tf_op jit(solution)/shard_map/ppermute | solution.py:599
  1143.9 353.8 %collective-permute-start.147 = (f32[2,288,1152]{2,1,0:T(8,128)}, f32[2,288,1152]{2,1,0:T(8,128)}, u32[]{:S(2)}, u32[]{:S(2)}) collective-permute-start(f32[2,288,1152]{2,1,0:T(8,128)} %fusion.115), channel_id=1, source_target_pairs={{0,16},{1,17},{2,18},{3,19},{4,20},{5,21},{6,22},{7,23},{8,24},{9,... | collective-permute-start | bytes 7962632 | tf_op jit(solution)/shard_map/ppermute | solution.py:599
  1258.8 1069.2 %all-gather.2.cloned.1.call-start = ((), (), s32[]{:S(2)}) async-start(), calls=%async_computation.5 | async-start | bytes 9953280 | tf_op jit(solution)/shard_map/all_gather | solution.py:1379
  1267.2 247.3 %collective-permute-start.124 = (bf16[512,1152]{0,1:T(8,128)(2,1)}, bf16[512,1152]{0,1:T(8,128)(2,1)}, u32[]{:S(2)}, u32[]{:S(2)}) collective-permute-start(bf16[512,1152]{0,1:T(8,128)(2,1)} %bitcast.287), channel_id=1, source_target_pairs={{0,8},{1,9},{2,10},{3,11},{4,12},{5,13},{6,14},{7,15},{8,0},{9,1},... | collective-permute-start | bytes 3538952 | tf_op jit(solution)/shard_map/ppermute | solution.py:599
  1272.2 246.7 %collective-permute-start.123 = (bf16[512,1152]{0,1:T(8,128)(2,1)}, bf16[512,1152]{0,1:T(8,128)(2,1)}, u32[]{:S(2)}, u32[]{:S(2)}) collective-permute-start(bf16[512,1152]{0,1:T(8,128)(2,1)} %bitcast.282), channel_id=1, source_target_pairs={{0,8},{1,9},{2,10},{3,11},{4,12},{5,13},{6,14},{7,15},{8,0},{9,1},... | collective-permute-start | bytes 3538952 | tf_op jit(solution)/shard_map/ppermute | solution.py:599
  1545.7 187.8 %collective-permute-start.125 = (f32[2,432,1152]{2,1,0:T(8,128)}, f32[2,432,1152]{2,1,0:T(8,128)}, u32[]{:S(2)}, u32[]{:S(2)}) collective-permute-start(f32[2,432,1152]{2,1,0:T(8,128)} %fusion.48), channel_id=1, source_target_pairs={{0,1},{1,0},{2,3},{3,2},{4,5},{5,4},{6,7},{7,6},{8,9},{9,8},{10,11... | collective-permute-start | bytes 11943944 | tf_op jit(solution)/shard_map/ppermute | solution.py:599
  1608.2 236.0 %collective-permute-start.160 = (f32[8,1152]{1,0:T(8,128)S(1)}, f32[8,1152]{1,0:T(8,128)S(1)}, u32[]{:S(2)}, u32[]{:S(2)}) collective-permute-start(f32[8,1152]{1,0:T(8,128)S(1)} %copy-done.201), channel_id=1, source_target_pairs={{0,1},{1,0},{2,3},{3,2},{4,5},{5,4},{6,7},{7,6},{8,9},{9,8},{10,11... | collective-permute-start | bytes 110600 | tf_op jit(solution)/shard_map/ppermute | solution.py:599
  1635.7 200.1 %collective-permute-start.116 = (f32[2,432,1152]{2,1,0:T(8,128)}, f32[2,432,1152]{2,1,0:T(8,128)}, u32[]{:S(2)}, u32[]{:S(2)}) collective-permute-start(f32[2,432,1152]{2,1,0:T(8,128)} %fusion.53), channel_id=1, source_target_pairs={{0,16},{1,17},{2,18},{3,19},{4,20},{5,21},{6,22},{7,23},{8,24},{9,... | collective-permute-start | bytes 11943944 | tf_op jit(solution)/shard_map/ppermute | solution.py:599
  1648.1 235.7 %collective-permute-start.137 = (f32[2,288,1152]{2,1,0:T(8,128)}, f32[2,288,1152]{2,1,0:T(8,128)}, u32[]{:S(2)}, u32[]{:S(2)}) collective-permute-start(f32[2,288,1152]{2,1,0:T(8,128)} %fusion.120), channel_id=1, source_target_pairs={{0,1},{1,0},{2,3},{3,2},{4,5},{5,4},{6,7},{7,6},{8,9},{9,8},{10,11... | collective-permute-start | bytes 7962632 | tf_op jit(solution)/shard_map/ppermute | solution.py:599
  1651.6 181.7 %collective-permute-start.97 = (f32[432,1152]{1,0:T(8,128)}, f32[432,1152]{1,0:T(8,128)}, u32[]{:S(2)}, u32[]{:S(2)}) collective-permute-start(f32[432,1152]{1,0:T(8,128)} %dynamic-slice_bitcast_fusion.3), channel_id=1, source_target_pairs={{0,1},{1,0},{2,3},{3,2},{4,5},{5,4},{6,7},{7,6},{8,9},{9,8},{10,11... | collective-permute-start | bytes 5971976 | tf_op jit(solution)/shard_map/ppermute | solution.py:599
  1941.6 150.1 %collective-permute-start.149 = (f32[288,1152]{1,0:T(8,128)}, f32[288,1152]{1,0:T(8,128)}, u32[]{:S(2)}, u32[]{:S(2)}) collective-permute-start(f32[288,1152]{1,0:T(8,128)} %bitcast_add_fusion.5), channel_id=1, source_target_pairs={{6,4},{7,5},{14,12},{15,13},{22,20},{23,21},{30,28},{31,29}} | collective-permute-start | bytes 3981320 | tf_op jit(solution)/shard_map/ppermute | solution.py:599
  1945.0 149.9 %collective-permute-start.138 = (f32[288,1152]{1,0:T(8,128)}, f32[288,1152]{1,0:T(8,128)}, u32[]{:S(2)}, u32[]{:S(2)}) collective-permute-start(f32[288,1152]{1,0:T(8,128)} %dynamic-slice_bitcast_fusion.6), channel_id=1, source_target_pairs={{0,16},{1,17},{2,18},{3,19},{4,20},{5,21},{6,22},{7,23},{8,24},{9,... | collective-permute-start | bytes 3981320 | tf_op jit(solution)/shard_map/ppermute | solution.py:599
  1946.9 150.8 %collective-permute-start.118 = (f32[432,1152]{1,0:T(8,128)}, f32[432,1152]{1,0:T(8,128)}, u32[]{:S(2)}, u32[]{:S(2)}) collective-permute-start(f32[432,1152]{1,0:T(8,128)} %bitcast_add_fusion.1), channel_id=1, source_target_pairs={{6,4},{7,5},{14,12},{15,13},{22,20},{23,21},{30,28},{31,29}} | collective-permute-start | bytes 5971976 | tf_op jit(solution)/shard_map/ppermute | solution.py:599
  1950.2 150.4 %all-to-all-start.4 = ((bf16[8,120,448]{1,2,0:T(8,128)(2,1)}), bf16[8,120,448]{1,2,0:T(8,128)(2,1)}, u32[]{:S(2)}, u32[]{:S(2)}) async-start(bf16[8,120,448]{1,2,0:T(8,128)(2,1)} %bitcast_dynamic-update-slice_fusion.4), calls=%async_computation.4 | async-start | bytes 1835008 | tf_op jit(solution)/shard_map/all_to_all | solution.py:1190
  1973.3 155.0 %collective-permute-start.99 = (f32[432,1152]{1,0:T(8,128)S(1)}, f32[432,1152]{1,0:T(8,128)}, u32[]{:S(2)}, u32[]{:S(2)}) collective-permute-start(f32[432,1152]{1,0:T(8,128)S(1)} %add.1424), channel_id=1, source_target_pairs={{2,4},{3,5},{10,12},{11,13},{18,20},{19,21},{26,28},{27,29}} | collective-permute-start | bytes 5971976 | tf_op jit(solution)/shard_map/ppermute | solution.py:599
  1975.3 155.1 %collective-permute-start.112 = (f32[432,1152]{1,0:T(8,128)}, f32[432,1152]{1,0:T(8,128)}, u32[]{:S(2)}, u32[]{:S(2)}) collective-permute-start(f32[432,1152]{1,0:T(8,128)} %add.1431), channel_id=1, source_target_pairs={{0,2},{1,3},{8,10},{9,11},{16,18},{17,19},{24,26},{25,27}} | collective-permute-start | bytes 5971976 | tf_op jit(solution)/shard_map/ppermute | solution.py:599
  2193.6 127.1 %collective-permute-start.120 = (f32[432,1152]{1,0:T(8,128)}, f32[432,1152]{1,0:T(8,128)}, u32[]{:S(2)}, u32[]{:S(2)}) collective-permute-start(f32[432,1152]{1,0:T(8,128)} %add.1438), channel_id=1, source_target_pairs={{0,2},{1,3},{8,10},{9,11},{16,18},{17,19},{24,26},{25,27}} | collective-permute-start | bytes 5971976 | tf_op jit(solution)/shard_map/ppermute | solution.py:599
  2327.6 156.2 %collective-permute-start.167 = (f32[432,1152]{1,0:T(8,128)S(1)}, f32[432,1152]{1,0:T(8,128)}, u32[]{:S(2)}, u32[]{:S(2)}) collective-permute-start(f32[432,1152]{1,0:T(8,128)S(1)} %get-tuple-element.106.refs_0_), channel_id=1, source_target_pairs={{0,16},{1,17},{2,18},{3,19},{4,20},{5,21},{6,22},{7,23},{8,24},{9,... | collective-permute-start | bytes 5971976 | tf_op jit(solution)/shard_map/ppermute | solution.py:599
  2355.7 128.6 %collective-permute-start.164 = (f32[448,1152]{1,0:T(8,128)}, f32[448,1152]{1,0:T(8,128)}, u32[]{:S(2)}, u32[]{:S(2)}) collective-permute-start(f32[448,1152]{1,0:T(8,128)} %get-tuple-element.248), channel_id=1, source_target_pairs={{0,16},{1,17},{2,18},{3,19},{4,20},{5,21},{6,22},{7,23},{8,24},{9,... | collective-permute-start | bytes 6193160 | tf_op jit(solution)/shard_map/ppermute | solution.py:599
  (473 other events, 13657.8 us)
Sparse Core Ops, SparseCore 0:
  1258.9 228.1 all-reduce.14
Sparse Core Ops, SparseCore 1:
  1264.7 132.8 all-gather.1

commit v2 on v1

--- a/solution.py
+++ b/solution.py
@@ -103,7 +103,7 @@
 
 
 def halves(value):
-    upper = value.astype(jnp.bfloat16)
+    upper = lax.optimization_barrier(value.astype(jnp.bfloat16))
     return (upper, (value - upper.astype(jnp.float32)).astype(jnp.bfloat16))
 
 
@@ -539,7 +539,7 @@
 AXES = ("frame", "clip")
 LANES = 128
 LANE_TILES = D // LANES
-EMB_PAD = 1792
+EMB_PAD = 1856
 
 
 X_SIZE, CORES, Z_SIZE, Y_SIZE = 2, 2, 4, 2
@@ -567,32 +567,6 @@
 SWAP_Y = pairs(lambda x, c, z, y: (x, c, z, 1 - y))
 SWAP_Z1 = pairs(lambda x, c, z, y: (x, c, z ^ 1, y))
 SWAP_Z2 = pairs(lambda x, c, z, y: (x, c, z ^ 2, y))
-
-
-def hop_z(source, to):
-    return pairs(lambda x, c, z, y: (x, c, to, y) if z == source else None)
-
-
-def ring_move(step, keep, seen):
-    def move(x, c, z, y):
-        place = CLIP_RING[z * Y_SIZE + y]
-        origin = RING_CLIP[(place + seen) % N_OWN]
-        if origin not in keep:
-            return None
-        to = RING[(place + step) % N_OWN]
-        return (x, c) + to
-
-    return pairs(move)
-
-
-def swap_move(flip_x, flip_core, keep, seen):
-    def move(x, c, z, y):
-        place = CLIP_RING[z * Y_SIZE + y]
-        if RING_CLIP[(place + seen) % N_OWN] not in keep:
-            return None
-        return (x ^ flip_x, c ^ flip_core, z, y)
-
-    return pairs(move)
 
 
 def shift(value, perm):
@@ -703,24 +677,45 @@
     )(table, flat.reshape(-1, LANES))
 
 
-def rows_kernel(flat, out):
-    count = out.shape[0]
+ROWS_AHEAD = 16
+
+
+def rows_kernel(shift_ref, flat, out, held, sem):
+    units, count = flat.shape[0], out.shape[0]
+    block = pl.program_id(0)
+
+    @pl.when(block == 0)
+    def _():
+        end = (ROWS_AHEAD + units) // 8 * 8
+        held[pl.ds(0, ROWS_AHEAD), :] = jnp.zeros((ROWS_AHEAD, LANES), jnp.float32)
+        held[pl.ds(end, held.shape[0] - end), :] = jnp.zeros((held.shape[0] - end, LANES), jnp.float32)
+        copy = pltpu.make_async_copy(flat, held.at[pl.ds(ROWS_AHEAD, units)], sem)
+        copy.start()
+        copy.wait()
+
+    begin = ROWS_AHEAD + block * (count * LANE_TILES) - shift_ref[0]
     for tile in range(LANE_TILES):
-        piece = flat[pl.ds(tile, count, stride=LANE_TILES), :]
+        piece = held[pl.ds(begin + tile, count, stride=LANE_TILES), :]
         out[:, tile * LANES : (tile + 1) * LANES] = piece.astype(out.dtype)
 
 
-def flat_to_rows(flat, dtype):
-    rows = flat.shape[0] // LANE_TILES
-    block = rows // 8
+def flat_to_rows(flat, rows, shift, dtype):
+    block = rows // 4
     return pl.pallas_call(
         rows_kernel,
-        grid=(8,),
-        in_specs=[pl.BlockSpec((block * LANE_TILES, LANES), lambda b: (b, 0))],
-        out_specs=pl.BlockSpec((block, D), lambda b: (b, 0)),
+        grid_spec=pltpu.PrefetchScalarGridSpec(
+            num_scalar_prefetch=1,
+            grid=(4,),
+            in_specs=[pl.BlockSpec(memory_space=pl.ANY)],
+            out_specs=pl.BlockSpec((block, D), lambda b, t: (b, 0)),
+            scratch_shapes=[
+                pltpu.VMEM((ROWS_AHEAD + rows * LANE_TILES + 8, LANES), jnp.float32),
+                pltpu.SemaphoreType.DMA,
+            ],
+        ),
         out_shape=jax.ShapeDtypeStruct((rows, D), dtype),
         compiler_params=pltpu.CompilerParams(vmem_limit_bytes=32 * 1024 * 1024),
-    )(flat)
+    )(shift.reshape(1), flat)
 
 
 def flat_kernel(rows, out):
@@ -730,10 +725,10 @@
 
 
 def rows_to_flat(rows):
-    block = rows.shape[0] // 8
+    block = rows.shape[0] // 4
     return pl.pallas_call(
         flat_kernel,
-        grid=(8,),
+        grid=(4,),
         in_specs=[pl.BlockSpec((block, D), lambda b: (b, 0))],
         out_specs=pl.BlockSpec((block * LANE_TILES, LANES), lambda b: (b, 0)),
         out_shape=jax.ShapeDtypeStruct((rows.shape[0] * LANE_TILES, LANES), rows.dtype),
@@ -741,87 +736,535 @@
     )(rows)
 
 
-def place_kernel(n_pieces, keep, stores, slots, own, *refs):
-    pieces, outs, (held, sems, out_sem) = refs[:n_pieces], refs[n_pieces:-3], refs[-3:]
-    low = min(keep)
-
-    def copies():
-        yield slots[0, 0], pltpu.make_async_copy(own, held.at[slots[0, 0] - low], sems.at[n_pieces])
-        for number in range(n_pieces):
-            owner = slots[number + 1, 0]
-            yield owner, pltpu.make_async_copy(
-                pieces[number], held.at[owner - low, slots[number + 1, 1]], sems.at[number]
-            )
-
-    for action in ("start", "wait"):
-        for owner, copy in copies():
-            if len(keep) == N_OWN:
-                getattr(copy, action)()
+def ring_place(clip):
+    return jnp.where(clip % 2 == 0, clip // 2, N_OWN - 1 - clip // 2)
+
+
+def clip_at(place):
+    return jnp.where(place < N_OWN // 2, 2 * place, 2 * N_OWN - 1 - 2 * place)
+
+
+def partners(frame, clip):
+    place = ring_place(clip)
+    x, core = frame // CORES, frame % CORES
+    return (
+        {"clip": clip_at((place + 1) % N_OWN)},
+        {"clip": clip_at((place + N_OWN - 1) % N_OWN)},
+        {"frame": (1 - x) * CORES + core},
+        {"frame": x * CORES + 1 - core},
+    )
+
+
+def greet(devices):
+    barrier = pltpu.get_barrier_semaphore()
+    for device in devices:
+        pl.semaphore_signal(barrier, inc=1, device_id=device, device_id_type=pl.DeviceIdType.MESH)
+    pl.semaphore_wait(barrier, len(devices))
+
+
+def spread_kernel(groups, modes, *refs):
+    n, m = len(groups), len(modes)
+    counts = [len(shapes) for keep, shapes, stores, common in groups]
+    refs = list(refs)
+    take = lambda number: [refs.pop(0) for _ in range(number)]
+    owns, given, outs, given_outs = take(n), take(m), take(sum(counts)), take(m)
+    helds, sources, landings = take(n), take(m), take(m)
+    load_sem, send_sem, recv_sem, out_sem, peer_sem, peer_send, peer_recv = refs
+    frame, clip = lax.axis_index("frame"), lax.axis_index("clip")
+    x, core = frame // CORES, frame % CORES
+    place = ring_place(clip)
+    right, left, over_x, other = partners(frame, clip)
+    half = N_OWN // 2
+    owners = [clip_at((place + N_OWN - k) % N_OWN) for k in range(half + 1)]
+    owners += [clip_at((place + k) % N_OWN) for k in range(1, half)]
+    flip_x = (1 - x) * CORES + core
+    mine = [core, frame, flip_x]
+    theirs = [1 - core, x * CORES + 1 - core, (1 - x) * CORES + 1 - core]
+    landing = mine + theirs
+
+    def block_of(group, kinds, kind):
+        return kinds[kind] + (2 if groups[group][3] and kind % 3 else 0)
+
+    def held_at(group, slot):
+        return helds[group].at[owners[slot] - min(groups[group][0])]
+
+    def where_kept(group, slot, action):
+        keep = groups[group][0]
+        if len(keep) == N_OWN:
+            action()
+        else:
+            pl.when(owners[slot] >= min(keep))(action)
+
+    def load(group):
+        return pltpu.make_async_copy(owns[group], held_at(group, 0), load_sem.at[group])
+
+    def copy_of(group, slot, block, device, to_slot, kind):
+        return pltpu.make_async_remote_copy(
+            src_ref=held_at(group, slot).at[block],
+            dst_ref=held_at(group, slot).at[block],
+            send_sem=send_sem.at[group, to_slot, kind],
+            recv_sem=recv_sem.at[group, to_slot, kind],
+            device_id=device,
+            device_id_type=pl.DeviceIdType.MESH,
+        )
+
+    sent = []
+
+    def send(group, slot, from_kind, device, to_slot, kind):
+        if from_kind == 0 and not groups[group][3]:
+            return
+        args = (group, slot, block_of(group, mine, from_kind), device, to_slot, kind)
+        where_kept(group, slot, lambda: copy_of(*args).start())
+        sent.append(args)
+
+    def arrive(group, slot, kind):
+        if kind % 3 == 0 and not groups[group][3]:
+            return
+        block = block_of(group, landing, kind)
+        where_kept(group, slot, lambda: copy_of(group, slot, block, other, slot, kind).wait_recv())
+
+    def onward(group, slot, kind):
+        if slot < half:
+            send(group, slot, kind, right, slot + 1, kind)
+        if slot == 0:
+            send(group, slot, kind, left, half + 1, kind)
+        elif half < slot < N_OWN - 1:
+            send(group, slot, kind, left, slot + 1, kind)
+
+    def peer_load(item):
+        return pltpu.make_async_copy(given[item], sources[item], peer_sem.at[item, 0])
+
+    def peer_own(item):
+        source = sources[item].at[clip] if modes[item] == "swap" else sources[item]
+        return pltpu.make_async_copy(source, landings[item].at[clip], peer_sem.at[item, 1])
+
+    def peer_copy(item, k):
+        to = (clip + k) % N_OWN
+        return pltpu.make_async_remote_copy(
+            src_ref=sources[item].at[to] if modes[item] == "swap" else sources[item],
+            dst_ref=landings[item].at[clip],
+            send_sem=peer_send.at[item, k - 1],
+            recv_sem=peer_recv.at[item, k - 1],
+            device_id={"clip": to},
+            device_id_type=pl.DeviceIdType.MESH,
+        )
+
+    def peers(item, arriving, action):
+        for k in range(1, N_OWN):
+            if modes[item] != "first":
+                action(k)
             else:
-
-                @pl.when(owner >= low)
-                def _():
-                    getattr(copy, action)()
-
-    rows = held.shape[1] * held.shape[2]
-    done = []
-    for number, (out, row, column, owner, first, count) in enumerate(stores):
-        quarter = rows // 4
-        while count > 0:
-            part, inner = divmod(first, quarter)
-            some = min(count, quarter - inner)
-            copy = pltpu.make_async_copy(
-                held.at[owner - low, part, pl.ds(inner, some)],
-                outs[out].at[pl.ds(row, some), pl.ds(column, D)],
-                out_sem.at[len(done)],
-            )
-            copy.start()
-            done.append(copy)
-            first, row, count = first + some, row + some, count - some
+                pl.when(clip == (k if arriving else 0))(lambda: action(k))
+
+    for group in range(n):
+        where_kept(group, 0, lambda: load(group).start())
+    for item in range(m):
+        peer_load(item).start()
+    everyone = tuple({"clip": (clip + k) % N_OWN} for k in range(1, N_OWN)) if m else ()
+    greet((right, left, over_x, other) + everyone)
+    for group in range(n):
+        where_kept(group, 0, lambda: load(group).wait())
+        onward(group, 0, 1)
+        onward(group, 0, 0)
+    for item in range(m):
+        peer_load(item).wait()
+        peer_own(item).start()
+        peers(item, False, lambda k: peer_copy(item, k).start())
+    waiting = []
+    for step in range(1, half + 1):
+        slots = [step] + ([half + step] if step < half else [])
+        pairs_now = [(group, slot) for group in range(n) for slot in slots]
+        for group, slot in pairs_now:
+            arrive(group, slot, 1)
+            onward(group, slot, 1)
+            send(group, slot, 1, over_x, slot, 2)
+            send(group, slot, 1, other, slot, 4)
+            arrive(group, slot, 0)
+            onward(group, slot, 0)
+            send(group, slot, 0, other, slot, 3)
+        for group, slot in waiting:
+            arrive(group, slot, 2)
+            send(group, slot, 2, other, slot, 5)
+        waiting = pairs_now
+    for group, slot in waiting:
+        arrive(group, slot, 2)
+        send(group, slot, 2, other, slot, 5)
+    for group in range(n):
+        for slot in range(1, N_OWN):
+            for kind in (3, 4, 5):
+                arrive(group, slot, kind)
+    done, base = [], 0
+    for group, (keep, shapes, stores, common) in enumerate(groups):
+        held = helds[group]
+        rows = held.shape[2]
+        for out, row, column, owner, first, count in stores:
+            while count > 0:
+                part, inner = divmod(first, rows)
+                some = min(count, rows - inner)
+                copy = pltpu.make_async_copy(
+                    held.at[owner - min(keep), part, pl.ds(inner, some)],
+                    outs[base + out].at[pl.ds(row, some), pl.ds(column, D)],
+                    out_sem.at[len(done)],
+                )
+                copy.start()
+                done.append(copy)
+                first, row, count = first + some, row + some, count - some
+        base += counts[group]
+    for item in range(m):
+        peer_own(item).wait()
+        peers(item, True, lambda k: peer_copy(item, k).wait_recv())
+        copy = pltpu.make_async_copy(landings[item], given_outs[item], peer_sem.at[item, 2])
+        copy.start()
+        done.append(copy)
+    for item in range(m):
+        peers(item, False, lambda k: peer_copy(item, k).wait_send())
+    for args in sent:
+        where_kept(args[0], args[1], lambda: copy_of(*args).wait_send())
     for copy in done:
         copy.wait()
 
 
-def place_pieces(own, pieces, slots, keep, shapes, stores):
-    rows = own.shape[0]
+def spread_shards(owns, groups, collective, given=()):
     spec = pl.BlockSpec(memory_space=pl.ANY)
+    shapes = [shape for keep, some, stores, common in groups for shape in some]
+    n_stores = sum(6 * len(stores) for keep, some, stores, common in groups)
+    blocks = [6 if group[3] else 4 for group in groups]
+    modes = [mode for value, mode in given]
+    values = [value for value, mode in given]
+    landed = [
+        value.shape if mode == "swap" else (N_OWN,) + value.shape for value, mode in given
+    ]
+    many = max(len(given), 1)
     return pl.pallas_call(
-        partial(place_kernel, len(pieces), keep, stores),
-        in_specs=[pl.BlockSpec(memory_space=pltpu.SMEM)] + [spec] * (len(pieces) + 1),
-        out_specs=[spec] * len(shapes),
-        out_shape=[jax.ShapeDtypeStruct(shape, own.dtype) for shape in shapes],
+        partial(spread_kernel, groups, modes),
+        in_specs=[spec] * (len(owns) + len(given)),
+        out_specs=[spec] * (len(shapes) + len(given)),
+        out_shape=[jax.ShapeDtypeStruct(shape, jnp.bfloat16) for shape in shapes]
+        + [jax.ShapeDtypeStruct(shape, value.dtype) for shape, value in zip(landed, values)],
         scratch_shapes=[
-            pltpu.VMEM((len(keep), 4, rows // 4, D), own.dtype),
-            pltpu.SemaphoreType.DMA((len(pieces) + 1,)),
-            pltpu.SemaphoreType.DMA((4 * len(stores),)),
+            pltpu.VMEM((len(group[0]), count, own.shape[0] // count, D), jnp.bfloat16)
+            for own, group, count in zip(owns, groups, blocks)
+        ]
+        + [pltpu.VMEM(value.shape, value.dtype) for value in values]
+        + [pltpu.VMEM(shape, value.dtype) for shape, value in zip(landed, values)]
+        + [
+            pltpu.SemaphoreType.DMA((len(owns),)),
+            pltpu.SemaphoreType.DMA((len(owns), N_OWN, 6)),
+            pltpu.SemaphoreType.DMA((len(owns), N_OWN, 6)),
+            pltpu.SemaphoreType.DMA((n_stores,)),
+            pltpu.SemaphoreType.DMA((many, 3)),
+            pltpu.SemaphoreType.DMA((many, N_OWN - 1)),
+            pltpu.SemaphoreType.DMA((many, N_OWN - 1)),
         ],
-        compiler_params=pltpu.CompilerParams(vmem_limit_bytes=48 * 1024 * 1024),
-    )(slots, own.reshape(4, rows // 4, D), *pieces)
-
-
-def gather_shards(own, clip_id, frame_id, keep, shapes, stores):
-    rows = own.shape[0]
-    quarter = lax.dynamic_slice_in_dim(own, frame_id * (rows // 4), rows // 4, 0)
-    place = jnp.asarray(CLIP_RING, jnp.int32)[clip_id]
-    ring_clip = jnp.asarray(RING_CLIP, jnp.int32)
-    pieces, slots = [], [jnp.stack([clip_id, 0 * clip_id])]
-    ahead, behind = quarter, quarter
-    arrived = []
-    for step in range(1, N_OWN // 2 + 1):
-        ahead = shift(ahead, ring_move(1, keep, 1 - step))
-        arrived.append((ahead, -step))
-        if step < N_OWN // 2:
-            behind = shift(behind, ring_move(-1, keep, step - 1))
-            arrived.append((behind, step))
-    for piece, seen in arrived:
-        source = ring_clip[(place + seen) % N_OWN]
-        over_x = shift(piece, swap_move(1, 0, keep, seen))
-        over_core = shift(piece, swap_move(0, 1, keep, seen))
-        both = shift(over_x, swap_move(0, 1, keep, seen))
-        for value, flip in ((piece, 0), (over_x, 2), (over_core, 1), (both, 3)):
-            pieces.append(value)
-            slots.append(jnp.stack([source, frame_id ^ flip]))
-    return place_pieces(own, pieces, jnp.stack(slots).astype(jnp.int32), keep, shapes, stores)
+        compiler_params=pltpu.CompilerParams(
+            collective_id=collective, has_side_effects=True, vmem_limit_bytes=50 * 1024 * 1024
+        ),
+        cost_estimate=pl.CostEstimate(
+            flops=0, bytes_accessed=200 * 1000 * 1000, transcendentals=0
+        ),
+    )(*[own.reshape(count, own.shape[0] // count, D) for own, count in zip(owns, blocks)], *values)
+
+
+LAG = 5
+
+
+def collect_kernel(first, last, chunks, small, part, out, small_out, part_out, scratch):
+    bufs, extra, locals_, finals, result = scratch[:2], scratch[2], scratch[3:5], scratch[5:7], scratch[7]
+    ring_send, ring_recv, x_send, x_recv, end_send, end_recv, load_sem, own_sem = scratch[8:16]
+    if small is not None:
+        sums, arrived, small_send, small_recv = scratch[16:]
+    if part is not None:
+        frames, part_send, part_recv = scratch[16:]
+    frame, clip = lax.axis_index("frame"), lax.axis_index("clip")
+    x, core = frame // CORES, frame % CORES
+    place = ring_place(clip)
+    right, left, over_x, other = partners(frame, clip)
+    swaps = [
+        other,
+        over_x,
+        {"clip": clip + 1 - 2 * (clip % 2)},
+        {"clip": clip + 2 - 4 * (clip // 2 % 2)},
+        {"clip": clip + 4 - 8 * (clip // 4)},
+    ]
+    greet((right, left) + (tuple(swaps) if small is not None else (over_x, other)))
+    f, l = first // 2, last // 2
+    toward = (right, left)
+
+    def owner(way, step):
+        moved = N_OWN - 1 - step if way == 0 else 1 + step
+        return clip_at((place + moved) % N_OWN)
+
+    def f_rows(side, way):
+        return pl.ds(pl.multiple_of(side * first + way * f, 8), f)
+
+    def l_rows(way):
+        return pl.ds(2 * first + way * l, l)
+
+    def remote(src, dst, send_sem, recv_sem, device):
+        return pltpu.make_async_remote_copy(
+            src_ref=src,
+            dst_ref=dst,
+            send_sem=send_sem,
+            recv_sem=recv_sem,
+            device_id=device,
+            device_id_type=pl.DeviceIdType.MESH,
+        )
+
+    def x_copy(way, step):
+        return remote(
+            chunks.at[owner(way, step), f_rows(1 - x, way)],
+            extra.at[way, step],
+            x_send.at[way, step],
+            x_recv.at[way, step],
+            over_x,
+        )
+
+    def load(kind, way, step):
+        to = bufs[kind].at[way, 0] if step == 0 else locals_[kind].at[way, step % 2]
+        rows = l_rows(way) if kind == 0 else f_rows(x, way)
+        return pltpu.make_async_copy(
+            chunks.at[owner(way, step), rows], to, load_sem.at[kind, way, step % 2]
+        )
+
+    def ring_copy(kind, way, step):
+        return remote(
+            bufs[kind].at[way, step],
+            bufs[kind].at[way, step + 1],
+            ring_send.at[kind, way, step],
+            ring_recv.at[kind, way, step],
+            toward[way],
+        )
+
+    def final_copy(kind, way):
+        return remote(
+            bufs[kind].at[way, N_OWN - 1],
+            finals[kind].at[way],
+            end_send.at[kind, way],
+            end_recv.at[kind, way],
+            over_x,
+        )
+
+    def small_copy(stage):
+        return remote(
+            sums.at[stage], arrived.at[stage], small_send.at[stage], small_recv.at[stage], swaps[stage]
+        )
+
+    flip_x = (1 - x) * CORES + core
+
+    def part_copy(number, block=None):
+        block = (frame, frame, flip_x)[number] if block is None else block
+        return remote(
+            frames.at[block],
+            frames.at[block],
+            part_send.at[number],
+            part_recv.at[number],
+            (over_x, other, other)[number],
+        )
+
+    def over_rows(start, count, work):
+        def body(number, carry):
+            work(pl.multiple_of(start + number * 8, 8))
+            return carry
+
+        lax.fori_loop(0, count // 8, body, 0)
+
+    def small_load():
+        return pltpu.make_async_copy(small, sums.at[0], own_sem.at[7])
+
+    def part_load():
+        return pltpu.make_async_copy(part, frames.at[frame], own_sem.at[7])
+
+    for kind in range(2):
+        for way in range(2):
+            load(kind, way, 0).start()
+    for way in range(2):
+        x_copy(way, 0).start()
+    if small is not None:
+        small_load().start()
+    if part is not None:
+        part_load().start()
+
+    def ring_step(kind, way, step):
+        load(kind, way, step).wait()
+        if step + 1 < N_OWN:
+            load(kind, way, step + 1).start()
+        if kind == 1:
+            x_copy(way, step).wait_recv()
+        if step > 0:
+            ring_copy(kind, way, step - 1).wait_recv()
+        buf, local = bufs[kind], locals_[kind]
+
+        def add(row):
+            at = pl.ds(row, 8)
+            total = buf[way, step, at]
+            if kind == 1:
+                total = total + extra[way, step, at]
+            if step > 0:
+                total = total + local[way, step % 2, at]
+            buf[way, step, at] = total
+
+        if kind == 1 or step > 0:
+            over_rows(0, f if kind == 1 else l, add)
+        if step + 1 < N_OWN:
+            ring_copy(kind, way, step).start()
+        else:
+            final_copy(kind, way).start()
+
+    def own_half(kind):
+        return pl.ds(2 * first, last) if kind == 0 else pl.ds(0, 2 * first)
+
+    def core_swap(kind, to):
+        return remote(
+            result.at[own_half(kind)],
+            out.at[to, own_half(kind)],
+            own_sem.at[kind],
+            own_sem.at[2 + kind],
+            other,
+        )
+
+    def own_store(kind):
+        return pltpu.make_async_copy(
+            result.at[own_half(kind)], out.at[core, own_half(kind)], own_sem.at[4 + kind]
+        )
+
+    def finish(kind):
+        for way in range(2):
+            final_copy(kind, way).wait_recv()
+            buf, final = bufs[kind], finals[kind]
+
+            def put(row):
+                at = pl.ds(row, 8)
+                if kind == 0:
+                    to = pl.multiple_of(2 * first + way * l + row, 8)
+                    result[pl.ds(to, 8)] = buf[way, N_OWN - 1, at] + final[way, at]
+                else:
+                    to = pl.multiple_of(x * first + way * f + row, 8)
+                    back = pl.multiple_of((1 - x) * first + way * f + row, 8)
+                    result[pl.ds(to, 8)] = buf[way, N_OWN - 1, at]
+                    result[pl.ds(back, 8)] = final[way, at]
+
+            over_rows(0, l if kind == 0 else f, put)
+        core_swap(kind, core).start()
+        own_store(kind).start()
+
+    for tick in range(N_OWN + LAG):
+        if small is not None and tick < len(swaps) + 1:
+            if tick == 0:
+                small_load().wait()
+            else:
+                small_copy(tick - 1).wait_recv()
+
+                def add_small(row):
+                    at = pl.ds(row, 8)
+                    sums[tick, at] = sums[tick - 1, at] + arrived[tick - 1, at]
+
+                over_rows(0, small.shape[0], add_small)
+            if tick < len(swaps):
+                small_copy(tick).start()
+        if 0 < tick < N_OWN:
+            for way in range(2):
+                x_copy(way, tick).start()
+        if part is not None and tick == N_OWN - 1:
+            part_load().wait()
+            part_copy(0).start()
+            part_copy(1).start()
+        for way in range(2):
+            if tick < N_OWN:
+                ring_step(0, way, tick)
+            if tick >= LAG:
+                ring_step(1, way, tick - LAG)
+    if small is not None:
+        small_store = pltpu.make_async_copy(sums.at[len(swaps)], small_out, own_sem.at[6])
+        small_store.start()
+    finish(0)
+    if part is not None:
+        part_copy(0, flip_x).wait_recv()
+        part_copy(2).start()
+    finish(1)
+    if part is not None:
+        part_copy(1, x * CORES + 1 - core).wait_recv()
+        part_copy(2, (1 - x) * CORES + 1 - core).wait_recv()
+        part_store = pltpu.make_async_copy(frames, part_out, own_sem.at[6])
+        part_store.start()
+        part_store.wait()
+        for number in range(3):
+            part_copy(number).wait_send()
+    if small is not None:
+        small_store.wait()
+        for stage in range(len(swaps)):
+            small_copy(stage).wait_send()
+    for way in range(2):
+        for step in range(N_OWN):
+            x_copy(way, step).wait_send()
+    for kind in range(2):
+        for way in range(2):
+            for step in range(N_OWN - 1):
+                ring_copy(kind, way, step).wait_send()
+            final_copy(kind, way).wait_send()
+        core_swap(kind, 1 - core).wait_recv()
+        core_swap(kind, core).wait_send()
+        own_store(kind).wait()
+
+
+def collect_shard(chunks, first, collective, small=None, part=None):
+    rows = chunks.shape[1]
+    last = rows - 2 * first
+    spec = pl.BlockSpec(memory_space=pl.ANY)
+    out_shape = [jax.ShapeDtypeStruct((2, rows, D), jnp.float32)]
+    beside = small if part is None else part
+    if part is None:
+        out_shape.append(jax.ShapeDtypeStruct(small.shape, jnp.float32))
+        more = [
+            pltpu.VMEM((6,) + small.shape, jnp.float32),
+            pltpu.VMEM((5,) + small.shape, jnp.float32),
+            pltpu.SemaphoreType.DMA((5,)),
+            pltpu.SemaphoreType.DMA((5,)),
+        ]
+    else:
+        out_shape.append(jax.ShapeDtypeStruct((4,) + part.shape, jnp.float32))
+        more = [
+            pltpu.VMEM((4,) + part.shape, jnp.float32),
+            pltpu.SemaphoreType.DMA((3,)),
+            pltpu.SemaphoreType.DMA((3,)),
+        ]
+
+    def kernel(chunks, beside, out, beside_out, *scratch):
+        if part is None:
+            collect_kernel(first, last, chunks, beside, None, out, beside_out, None, scratch)
+        else:
+            collect_kernel(first, last, chunks, None, beside, out, None, beside_out, scratch)
+
+    return pl.pallas_call(
+        kernel,
+        in_specs=[spec] * 2,
+        out_specs=[spec] * 2,
+        out_shape=out_shape,
+        scratch_shapes=[
+            pltpu.VMEM((2, N_OWN, last // 2, D), jnp.float32),
+            pltpu.VMEM((2, N_OWN, first // 2, D), jnp.float32),
+            pltpu.VMEM((2, N_OWN, first // 2, D), jnp.float32),
+            pltpu.VMEM((2, 2, last // 2, D), jnp.float32),
+            pltpu.VMEM((2, 2, first // 2, D), jnp.float32),
+            pltpu.VMEM((2, last // 2, D), jnp.float32),
+            pltpu.VMEM((2, first // 2, D), jnp.float32),
+            pltpu.VMEM((rows, D), jnp.float32),
+            pltpu.SemaphoreType.DMA((2, 2, N_OWN)),
+            pltpu.SemaphoreType.DMA((2, 2, N_OWN)),
+            pltpu.SemaphoreType.DMA((2, N_OWN)),
+            pltpu.SemaphoreType.DMA((2, N_OWN)),
+            pltpu.SemaphoreType.DMA((2, 2)),
+            pltpu.SemaphoreType.DMA((2, 2)),
+            pltpu.SemaphoreType.DMA((2, 2, 2)),
+            pltpu.SemaphoreType.DMA((8,)),
+        ]
+        + more,
+        compiler_params=pltpu.CompilerParams(
+            collective_id=collective, has_side_effects=True, vmem_limit_bytes=58 * 1024 * 1024
+        ),
+        cost_estimate=pl.CostEstimate(
+            flops=0, bytes_accessed=800 * 1000 * 1000, transcendentals=0
+        ),
+    )(chunks, beside)
 
 
 def matrix_plan(matrices, segments):
@@ -858,43 +1301,13 @@
     return jnp.concatenate([value, shift(value, SWAP_CORE)], 0)
 
 
-def reduce_pair(pair, owner_z, x_first, x_id, y_id):
-    def fold(value, axis, place, perm):
-        mine = lax.dynamic_index_in_dim(value, place, axis, keepdims=False)
-        other = lax.dynamic_index_in_dim(value, 1 - place, axis, keepdims=False)
-        return mine + shift(other, perm)
-
-    if x_first:
-        part = fold(fold(pair, 1, x_id, SWAP_X), 0, y_id, SWAP_Y)
-    else:
-        part = fold(fold(pair, 0, y_id, SWAP_Y), 0, x_id, SWAP_X)
-    for source in range(Z_SIZE - 1, owner_z, -1):
-        part = part + shift(part, hop_z(source, source - 1))
-    for source in range(owner_z):
-        part = part + shift(part, hop_z(source, source + 1))
-    return part
-
-
-def pair_chunks(grads, segments, owner_z):
-    chunks = []
-    for owner in (2 * owner_z, 2 * owner_z + 1):
-        parts = []
-        for label, first, count, wide in segments[owner]:
-            begin = sum(
-                seg[2] // 2 for mine in segments[:owner] for seg in mine if seg[0] == label
-            )
-            for j in range(wide):
-                parts.append(grads[label][j][begin : begin + count // 2])
-        chunks.append(jnp.concatenate(parts, 0) if len(parts) > 1 else parts[0])
-    pair = jnp.stack(chunks)
-    return pair.reshape(2, 2, pair.shape[1] // 2, D)
-
-
-def choose_z(parts, z_id):
-    out = parts[0]
-    for number in range(1, Z_SIZE):
-        out = jnp.where(z_id == number, parts[number], out)
-    return out
+def owner_chunk(grads, segments, owner):
+    parts = []
+    for label, first, count, wide in segments[owner]:
+        begin = sum(seg[2] // 2 for mine in segments[:owner] for seg in mine if seg[0] == label)
+        for j in range(wide):
+            parts.append(grads[label][j][begin : begin + count // 2])
+    return jnp.concatenate(parts, 0) if len(parts) > 1 else parts[0]
 
 
 def step_values(master, grad, first, second, average):
@@ -913,26 +1326,15 @@
 STEP_ROWS = 144
 
 
-def step_kernel(widths, n_rows, table, places, factor, *refs):
-    quarters, olds, news = refs[:4], refs[4:8], refs[8:12]
-    shard, flat, sems = refs[12:]
+def step_kernel(widths, table, factor, grad, *refs):
+    olds, news, (shard, flat, sem) = refs[:4], refs[4:8], refs[8:]
     block = pl.program_id(0)
-    per = n_rows // 4
 
     @pl.when(block == 0)
     def _():
-        copies = [
-            pltpu.make_async_copy(
-                quarters[k],
-                shard.at[pl.ds(pl.multiple_of(places[k] * per, 8), per)],
-                sems.at[k],
-            )
-            for k in range(4)
-        ]
-        for copy in copies:
-            copy.start()
-        for copy in copies:
-            copy.wait()
+        copy = pltpu.make_async_copy(grad, shard, sem)
+        copy.start()
+        copy.wait()
 
     for wide in widths:
         count = STEP_BLOCK // wide
@@ -959,27 +1361,26 @@
     lax.fori_loop(0, STEP_BLOCK * LANE_TILES // STEP_ROWS, some_rows, 0)
 
 
-def step_shard(quarters, places, table, widths, n_rows, factor, olds):
+def step_shard(grad, table, widths, n_rows, factor, olds):
     units = STEP_BLOCK * LANE_TILES
-    block_spec = pl.BlockSpec((units, LANES), lambda b, t, p, f: (b, 0))
-    whole = pl.BlockSpec(memory_space=pl.ANY)
+    block_spec = pl.BlockSpec((units, LANES), lambda b, t, f: (b, 0))
     flat_shape = jax.ShapeDtypeStruct((n_rows * LANE_TILES, LANES), jnp.float32)
     made = pl.pallas_call(
-        partial(step_kernel, widths, n_rows),
+        partial(step_kernel, widths),
         grid_spec=pltpu.PrefetchScalarGridSpec(
-            num_scalar_prefetch=3,
+            num_scalar_prefetch=2,
             grid=(n_rows // STEP_BLOCK,),
-            in_specs=[whole] * 4 + [block_spec] * 4,
+            in_specs=[pl.BlockSpec(memory_space=pl.ANY)] + [block_spec] * 4,
             out_specs=[block_spec] * 4,
             scratch_shapes=[
                 pltpu.VMEM((n_rows, D), jnp.float32),
                 pltpu.VMEM((units, LANES), jnp.float32),
-                pltpu.SemaphoreType.DMA((4,)),
+                pltpu.SemaphoreType.DMA,
             ],
         ),
         out_shape=[flat_shape] * 4,
         compiler_params=pltpu.CompilerParams(vmem_limit_bytes=50 * 1024 * 1024),
-    )(table, places, factor, *quarters, *[old.reshape(-1, LANES) for old in olds])
+    )(table, factor, grad, *[old.reshape(-1, LANES) for old in olds])
     return [value.reshape(-1) for value in made]
 
 
@@ -996,8 +1397,12 @@
 
 
 def two_parts(product, value):
-    upper, lower = halves(value)
-    return product(upper) + product(lower)
+    both = product(jnp.concatenate(halves(value), 0))
+    return both[: value.shape[0]] + both[value.shape[0] :]
+
+
+def grad_two_parts(left, value):
+    return weight_grad(jnp.concatenate([left, left], 0), jnp.concatenate(halves(value), 0))
 
 
 def shards_block(
@@ -1035,36 +1440,27 @@
     x_id, core_id = frame_id // CORES, frame_id % CORES
     z_id, y_id = clip_id // Y_SIZE, clip_id % Y_SIZE
 
-    attend_cast = cast_shard(
-        attend_w, jnp.asarray(cast_table(ATTEND_SEGS, CAST_BLOCK))[clip_id], (1, 2, 3), ATTEND_ROWS
-    )
-    space_qkv, space_out, time_qkv, time_out, cross_q, cross_kv, cross_out = gather_shards(
-        attend_cast, clip_id, frame_id, range(N_OWN), *matrix_plan(ATTEND, ATTEND_SEGS)
-    )
     emb_first = jnp.asarray(EMB_FIRST, jnp.int32)[clip_id]
     emb_shift = jnp.asarray(EMB_SHIFT, jnp.int32)[clip_id]
-    emb_flat = lax.dynamic_update_slice(
-        jnp.zeros((EMB_PAD * LANE_TILES, LANES), jnp.float32),
-        embed_w.reshape(-1, LANES),
-        (emb_shift, 0 * emb_shift),
-    )
-    emb_rows = flat_to_rows(emb_flat, jnp.bfloat16)
+    emb_rows = flat_to_rows(embed_w.reshape(-1, LANES), EMB_PAD, emb_shift, jnp.bfloat16)
+    dense_cast = cast_shard(
+        dense_w, jnp.asarray(cast_table(DENSE_SEGS, CAST_BLOCK))[clip_id], (1, 4), DENSE_ROWS
+    )
     cap_owners = range(4, N_OWN)
-    cap_weights = gather_shards(
-        emb_rows,
-        clip_id,
-        frame_id,
-        cap_owners,
+    cap_plan = (
         [(EMB_PAD * len(cap_owners), D)],
         [(0, EMB_PAD * k, 0, owner, 0, EMB_PAD) for k, owner in enumerate(cap_owners)],
-    )[0]
-    dense_cast = cast_shard(
-        dense_w, jnp.asarray(cast_table(DENSE_SEGS, CAST_BLOCK))[clip_id], (1, 4), DENSE_ROWS
-    )
-    fc_in, fc_out = gather_shards(
-        dense_cast, clip_id, frame_id, range(N_OWN), *matrix_plan(DENSE, DENSE_SEGS)
-    )
-
+    )
+    own_clip = jnp.arange(n_clip) == clip_id
+    facts = jnp.stack([timesteps.astype(jnp.float32)[0], sample_weight[0], null_flags.astype(jnp.float32)[0]])
+    facts = jnp.broadcast_to(jnp.pad(facts, (0, LANES - 3))[None], (8, LANES))
+    cap_weights, fc_in, fc_out, facts = spread_shards(
+        [emb_rows, dense_cast],
+        [(cap_owners,) + cap_plan + (False,), (range(N_OWN),) + matrix_plan(DENSE, DENSE_SEGS) + (True,)],
+        2,
+        given=[(facts, "gather")],
+    )
+    facts = facts[:, 0, :3]
     last = N_OWN - 1
     cap_last = cap_weights[EMB_PAD * (len(cap_owners) - 1) :]
     null_end = 16158720 - ROW_NULL * D
@@ -1114,10 +1510,7 @@
         final_table,
     ) = split_flat(vector_w, vector_shapes())
 
-    own_clip = jnp.arange(n_clip) == clip_id
-    facts = jnp.stack([timesteps.astype(jnp.float32)[0], sample_weight[0]])
-    facts = sum_clips(jnp.where(own_clip[:, None], facts[None], 0.0))
-    all_steps = facts[:, 0]
+    all_steps, all_null = facts[:, 0], facts[:, 2] == 1.0
     angle = (all_steps / 1000.0 + 0.008) / 1.008 * (math.pi / 2)
     signal = jnp.cos(angle) ** 2
     ratio = signal / (1.0 - signal)
@@ -1136,38 +1529,6 @@
     early = jnp.concatenate(
         [pre_one, time_embed, emb_rows[:ROW_TIME_ONE].astype(jnp.float32)], 0
     )
-    early = sum_clips(jnp.where(at_start, early, 0.0))
-    pre_one, time_embed = early[:n_clip], early[n_clip : 2 * n_clip]
-    patch_w = early[2 * n_clip :].astype(jnp.bfloat16)
-    act_one = jax.nn.silu(pre_one).astype(jnp.bfloat16)
-    silu_time = jax.nn.silu(time_embed).astype(jnp.bfloat16)
-    local_row = emb_first + jnp.arange(EMB_PAD, dtype=jnp.int32)
-    block_row = local_row - ROW_BLOCK
-    in_block = (block_row >= 0) & (block_row < 6 * D)
-    block_part = jnp.where(in_block, block_row % 6, -1)
-    block_line = jnp.where(in_block, block_row // 6, -1)
-    chooser = jnp.arange(D, dtype=jnp.int32)[:, None] == block_line[None]
-    silu_rows = matmul_low(silu_time, chooser.astype(jnp.bfloat16)).astype(jnp.bfloat16)
-    part_mask = jnp.arange(6, dtype=jnp.int32)[:, None] == block_part[None]
-    block_left = jnp.where(part_mask[None], silu_rows[:, None], 0).reshape(n_clip * 6, EMB_PAD)
-    block_out = sum_clips(matmul_low(block_left, emb_rows)).reshape(n_clip, 6, D)
-    all_mods = table[None] + (block_out + block_b.reshape(6, D))
-    mods = lax.dynamic_slice_in_dim(all_mods, clip_id, 1, 0)
-    my_embed = lax.dynamic_slice_in_dim(time_embed, clip_id, 1, 0)
-
-    keep_part = jnp.sqrt(signal)[:, None, None, None]
-    fade_part = jnp.sqrt(1.0 - signal)[:, None, None, None]
-    noisy = (keep_part * latents + fade_part * noise).astype(jnp.bfloat16)
-    frame_ids = frame_id * frame_dev + jnp.arange(frame_dev)
-    patch_ids = jnp.arange(patches)
-    place = jnp.concatenate(
-        [sincos(patch_ids // PGRID, D // 2), sincos(patch_ids % PGRID, D // 2)], -1
-    )[None, None]
-    hidden_zero = matmul_low(noisy, patch_w) + patch_b + place + sincos(frame_ids, D)[None, :, None]
-
-    def mod_row(number):
-        return mods[:, number][:, None, None, :]
-
     is_null = null_flags == 1
     cap_in = jnp.where(is_null[:, None, None], null_caption[None], captions)
     cap_pre = (matmul_low(to_cap_rows(cap_in[0]), cap_weights) + cap_b1)[None]
@@ -1187,8 +1548,47 @@
             wanted.append(
                 lax.dynamic_slice_in_dim(cap_wide, start + frame_id * (EMB_PAD // 4), EMB_PAD // 4, 1)
             )
-    cap_left = lax.all_to_all(jnp.stack(wanted), "clip", split_axis=0, concat_axis=0, tiled=True)
-    cap_left = cap_left.reshape(n_clip * L_CAP, EMB_PAD // 4)
+    attend_cast = cast_shard(
+        attend_w, jnp.asarray(cast_table(ATTEND_SEGS, CAST_BLOCK))[clip_id], (1, 2, 3), ATTEND_ROWS
+    )
+    space_qkv, space_out, time_qkv, time_out, cross_q, cross_kv, cross_out, early, cap_left = spread_shards(
+        [attend_cast],
+        [(range(N_OWN),) + matrix_plan(ATTEND, ATTEND_SEGS) + (True,)],
+        1,
+        given=[(early, "first"), (jnp.pad(jnp.stack(wanted), ((0, 0), (0, 128 - L_CAP), (0, 0))), "swap")],
+    )
+    early = early[0]
+    cap_left = cap_left[:, :L_CAP].reshape(n_clip * L_CAP, EMB_PAD // 4)
+    pre_one, time_embed = early[:n_clip], early[n_clip : 2 * n_clip]
+    patch_w = early[2 * n_clip :].astype(jnp.bfloat16)
+    act_one = jax.nn.silu(pre_one).astype(jnp.bfloat16)
+    silu_time = jax.nn.silu(time_embed).astype(jnp.bfloat16)
+    local_row = emb_first + jnp.arange(EMB_PAD, dtype=jnp.int32)
+    block_row = local_row - ROW_BLOCK
+    in_block = (block_row >= 0) & (block_row < 6 * D)
+    block_part = jnp.where(in_block, block_row % 6, -1)
+    block_line = jnp.where(in_block, block_row // 6, -1)
+    chooser = jnp.arange(D, dtype=jnp.int32)[:, None] == block_line[None]
+    silu_rows = matmul_low(silu_time, chooser.astype(jnp.bfloat16)).astype(jnp.bfloat16)
+    part_mask = jnp.arange(6, dtype=jnp.int32)[:, None] == block_part[None]
+    block_left = jnp.where(part_mask[None], silu_rows[:, None], 0).reshape(n_clip * 6, EMB_PAD)
+    block_out = sum_clips(matmul_low(block_left, emb_rows)).reshape(n_clip, 6, D)
+    all_mods = table[None] + (block_out + block_b.reshape(6, D))
+    mods = lax.dynamic_slice_in_dim(all_mods, clip_id, 1, 0)
+    my_embed = lax.dynamic_slice_in_dim(time_embed, clip_id, 1, 0)
+
+    keep_part = jnp.sqrt(signal)[:, None, None, None]
+    fade_part = jnp.sqrt(1.0 - signal)[:, None, None, None]
+    noisy = (keep_part * latents + fade_part * noise).astype(jnp.bfloat16)
+    frame_ids = frame_id * frame_dev + jnp.arange(frame_dev)
+    patch_ids = jnp.arange(patches)
+    place = jnp.concatenate(
+        [sincos(patch_ids // PGRID, D // 2), sincos(patch_ids % PGRID, D // 2)], -1
+    )[None, None]
+    hidden_zero = matmul_low(noisy, patch_w) + patch_b + place + sincos(frame_ids, D)[None, :, None]
+
+    def mod_row(number):
+        return mods[:, number][:, None, None, :]
 
     def flat2(value):
         return value.reshape(-1, value.shape[-1])
@@ -1282,10 +1682,6 @@
     grad_pre = pullback(back_low(grad_dense, fc_out))[0].astype(jnp.bfloat16)
     grads["fc_in"] = core_grad(inputs["fc_in"], columns(grad_pre))
     g_fc_in_b = bias_grad(grad_pre)
-    dense_parts = [
-        reduce_pair(pair_chunks(grads, DENSE_SEGS, z), z, z % 2 == 1, x_id, y_id)
-        for z in (3, 2, 1, 0)
-    ][::-1]
     unused, pullback = jax.vjp(modulate, hidden_three, mod_row(3), mod_row(4))
     grad_input, grad_shift_b, grad_scale_b = pullback(back_low(grad_pre, fc_in))
     grad_hidden = grad_hidden + grad_input
@@ -1305,15 +1701,10 @@
     g_cross_bv = bias_grad(grad_cv)
     grad_ckv = grad_ckv + shift(grad_ckv, SWAP_CORE)
     cap_half = pick_columns(cap_rows[0], half_rows(ATTEND_SEGS, "cross_kv"), core_id)
-    grads["cross_kv"] = [weight_split(cap_half, part) for part in columns(grad_ckv)]
+    grads["cross_kv"] = [grad_two_parts(cap_half, part) for part in columns(grad_ckv)]
     grad_ckv = grad_ckv + shift(grad_ckv, SWAP_X)
-    grad_cap_rows = back_split(grad_ckv, cross_kv)
-
-    def reduce_attend(z, x_first):
-        return reduce_pair(pair_chunks(grads, ATTEND_SEGS, z), z, x_first, x_id, y_id)
-
-    attend_parts = [None] * Z_SIZE
-    attend_parts[3] = reduce_attend(3, True)
+    grad_cap_rows = two_parts(lambda part: back_low(part, cross_kv), grad_ckv)
+
     grad_time = (grad_hidden * mod_row(2)).astype(jnp.bfloat16)
     grads["time_out"] = core_grad(inputs["time_out"], [grad_time])
     g_time_bo = bias_grad(grad_time)
@@ -1336,14 +1727,12 @@
     grad_tqkv = lax.all_to_all(
         jnp.swapaxes(jnp.concatenate(grad_tqkv, -1), 1, 2), "frame", split_axis=1, concat_axis=2, tiled=True
     )
-    attend_parts[2] = reduce_attend(2, False)
     grad_gate_a = jnp.sum(grad_hidden * time_res, (1, 2))
     grad_hidden = grad_hidden + back_low(grad_tqkv, time_qkv)
     grad_gate_a = grad_gate_a + jnp.sum(grad_hidden * space_res, (1, 2))
     grad_space = (grad_hidden * mod_row(2)).astype(jnp.bfloat16)
     grads["space_out"] = core_grad(inputs["space_out"], [grad_space])
     g_space_bo = bias_grad(grad_space)
-    attend_parts[1] = reduce_attend(1, True)
     grad_space_o = heads_of(
         back_low(grad_space, space_out).astype(jnp.bfloat16), clip_dev * frame_dev
     )
@@ -1352,7 +1741,6 @@
         for piece in attend_backward(space_q, space_k, space_v, None, space_lse, grad_space_o)
     ]
     grads["space_qkv"] = core_grad(inputs["space_qkv"], grad_sqkv)
-    attend_parts[0] = reduce_attend(0, False)
     g_space_bq = bias_grad(grad_sqkv[0])
     g_space_bv = bias_grad(grad_sqkv[2])
     grad_sqkv = jnp.concatenate(grad_sqkv, -1)
@@ -1375,11 +1763,12 @@
     )
 
     unused, pullback = jax.vjp(gelu_tanh, cap_pre[0])
-    grad_cap_pre = pullback(back_split(grad_cap_rows, cap_last)[:, two_first : two_first + D])[0]
+    grad_cap_act = two_parts(lambda part: back_low(part, cap_last), grad_cap_rows)
+    grad_cap_pre = pullback(grad_cap_act[:, two_first : two_first + D])[0]
     cap_right = lax.all_gather(
         jnp.stack([grad_cap_pre, grad_cap_rows]), "clip", axis=1, tiled=True
     )
-    null_sum = jnp.where(is_null[0], grad_cap_pre, 0.0)
+    null_sum = jnp.sum(jnp.where(all_null[:, None, None], cap_right[0].reshape(n_clip, L_CAP, D), 0.0), 0)
     g_cap_b1 = bias_grad(grad_cap_pre)
     g_cap_b2 = bias_grad(grad_cap_rows)
 
@@ -1405,17 +1794,23 @@
             g_final_b,
         ]
     )
-    vector_grad, gathered_mods, g_patch_w, g_final_w, loss_sum, null_sum = lax.psum(
-        (
-            vector_grad,
-            gathered_mods,
-            g_patch_w,
-            g_final_w,
-            local_loss,
-            jnp.where(once, null_sum, 0.0),
-        ),
-        AXES,
-    )
+    n_vector = vector_grad.shape[0]
+    small = flatten_all([gathered_mods, g_patch_w, g_final_w, vector_grad, local_loss])
+    small_rows = -(-small.shape[0] // (8 * D)) * 8
+    small = jnp.pad(small, (0, small_rows * D - small.shape[0])).reshape(small_rows, D)
+    dense_grad, small = collect_shard(
+        jnp.stack([owner_chunk(grads, DENSE_SEGS, owner) for owner in range(N_OWN)]),
+        144,
+        3,
+        small=small,
+    )
+    dense_grad = dense_grad.reshape(DENSE_ROWS, D)
+    at = 8 * n_clip
+    gathered_mods = small[:at].reshape(n_clip, 8, D)
+    g_patch_w = small[at : at + PATCH_VALUES]
+    g_final_w = small[at + PATCH_VALUES : at + 2 * PATCH_VALUES]
+    rest = small[at + 2 * PATCH_VALUES :].reshape(-1)
+    vector_grad, loss_sum = rest[:n_vector], rest[n_vector]
 
     grad_zero = gathered_mods[:, :6]
     grad_final = gathered_mods[:, 6:]
@@ -1465,29 +1860,26 @@
     small_right = jnp.concatenate([grad_one, grad_embed, zero_rows], 0)
     first_kind = (quarter_row < ROW_CAP_TWO)[None]
     no_left = jnp.zeros_like(cap_left)
+    g_null = from_cap_rows(two_parts(lambda part: back_low(part, cap_weights), null_sum))
+    n_null = -(-null_end // D)
+    n_known = -(-(2 * PATCH_VALUES + n_null) // 16) * 16
+    null_rows = jnp.pad(g_null.reshape(-1), (0, (n_known - 2 * PATCH_VALUES) * D - null_end))
+    known = jnp.concatenate([g_patch_w, g_final_w, null_rows.reshape(-1, D)], 0)
+    known_row = np.concatenate(
+        [np.arange(PATCH_VALUES), ROW_FINAL + np.arange(n_known - PATCH_VALUES)]
+    ).astype(np.int32)
+    known_left = (jnp.asarray(known_row)[:, None] == quarter_row[None]).astype(jnp.bfloat16)
     emb_left = jnp.concatenate(
         [
             small_left,
             jnp.where(first_kind, cap_left, no_left),
             jnp.where(first_kind, no_left, cap_left),
+            known_left,
         ],
         0,
     )
-    emb_right = jnp.concatenate([small_right, cap_right[0], cap_right[1]], 0)
-    emb_grad = two_parts(lambda part: weight_grad(emb_left, part), emb_right)
-    g_null = from_cap_rows(two_parts(lambda part: back_low(part, cap_weights), null_sum))
-    null_rows = jnp.pad(g_null.reshape(-1), (0, (EMB_PAD - (ROW_NULL - EMB_FIRST[last])) * D - null_end))
-    tail_rows = jnp.concatenate(
-        [
-            jnp.zeros((ROW_FINAL - EMB_FIRST[last], D), jnp.float32),
-            g_final_w.reshape(PATCH_VALUES, D),
-            null_rows.reshape(-1, D),
-        ],
-        0,
-    )
-    head_rows = jnp.pad(g_patch_w, ((0, EMB_PAD - PATCH_VALUES), (0, 0)))
-    extra = jnp.where(clip_id == last, tail_rows, jnp.where(at_start, head_rows, 0.0))
-    emb_grad = emb_grad + lax.dynamic_slice_in_dim(extra, frame_id * per, per, 0)
+    emb_right = jnp.concatenate([small_right, cap_right[0], cap_right[1], known], 0)
+    emb_grad = weight_split(emb_left, emb_right)
     unit = (
         LANE_TILES * (frame_id * per + jnp.arange(per, dtype=jnp.int32))[:, None]
         + jnp.arange(D, dtype=jnp.int32)[None] // LANES
@@ -1495,28 +1887,20 @@
     )
     emb_grad = jnp.where((unit >= 0) & (unit < EMB_UNITS), emb_grad, 0.0)
 
-    attend_part = choose_z(attend_parts, z_id).reshape(-1, D)
-    dense_part = choose_z(dense_parts, z_id).reshape(-1, D)
-    local_square = sum(jnp.sum(part * part) for part in (attend_part, dense_part, emb_grad))
-    grad_norm = jnp.sqrt(lax.psum(local_square, AXES) + jnp.sum(vector_sum * vector_sum))
+    attend_grad, emb_whole = collect_shard(
+        jnp.stack([owner_chunk(grads, ATTEND_SEGS, owner) for owner in range(N_OWN)]),
+        176,
+        4,
+        part=emb_grad,
+    )
+    attend_grad = attend_grad.reshape(ATTEND_ROWS, D)
+    local_square = sum(jnp.sum(value * value) for value in (dense_grad, attend_grad, emb_whole))
+    vector_square = jnp.sum(vector_sum * vector_sum)
+    grad_norm = jnp.sqrt(sum_clips(local_square.reshape(1))[0] + vector_square)
     factor = jnp.minimum(1.0, CLIP_LIMIT / (grad_norm + NORM_FLOOR))
-
-    def four_parts(part):
-        over_x = shift(part, SWAP_X)
-        return [part, over_x, shift(part, SWAP_CORE), shift(over_x, SWAP_CORE)]
-
-    spots = jnp.stack(
-        [
-            core_id * 2 + x_id,
-            core_id * 2 + 1 - x_id,
-            (1 - core_id) * 2 + x_id,
-            (1 - core_id) * 2 + 1 - x_id,
-        ]
-    ).astype(jnp.int32)
     scale = factor.reshape(1)
     dense_r = step_shard(
-        four_parts(dense_part),
-        spots,
+        dense_grad,
         jnp.asarray(step_table(DENSE_SEGS, STEP_BLOCK, DENSE_ROWS))[clip_id],
         (1, 4),
         DENSE_ROWS,
@@ -1524,18 +1908,13 @@
         (dense_w, dense_m, dense_v, dense_e),
     )
     attend_r = step_shard(
-        four_parts(attend_part),
-        spots,
+        attend_grad,
         jnp.asarray(step_table(ATTEND_SEGS, STEP_BLOCK, ATTEND_ROWS))[clip_id],
         (1, 2, 3),
         ATTEND_ROWS,
         scale,
         (attend_w, attend_m, attend_v, attend_e),
     )
-    emb_parts = four_parts(emb_grad)
-    emb_whole = jnp.zeros((4, per, D), jnp.float32)
-    for part, flip in zip(emb_parts, (0, 2, 1, 3)):
-        emb_whole = lax.dynamic_update_index_in_dim(emb_whole, part, frame_id ^ flip, 0)
     emb_flat = rows_to_flat(emb_whole.reshape(EMB_PAD, D))
     emb_owned = lax.dynamic_slice_in_dim(emb_flat, emb_shift, EMB_UNITS, 0).reshape(-1)
     embed_r = adam_step(embed_w, emb_owned, embed_m, embed_v, embed_e, factor)

time: 2600 us -> 1820 us (0.70)
  Pallas kernels: 102 us -> 927 us
  waiting for transfers between devices: 862 us -> 42.2 us
  starting transfers between devices: 571 us -> 57.6 us
  other arithmetic: 247 us -> 132 us
  local copies, waits for them, and re-layouts: 350 us -> 261 us
  blocking collectives: 37.8 us -> 0 us
    pallas_call x7 -> x8, Pallas kernels: 99.2 us -> 924 us  [the longest x2 506 us: collect_shard(): pl.pallas_call(kernel, in_specs=[spec] * 2, out_specs=[spec] * 2, out_sha...]
    ppermute x173 -> x37, waiting for transfers between devices: 641 us -> 32 us  [shift(): return lax.ppermute(value, AXES, perm)]
    ppermute x173 -> x37, starting transfers between devices: 546 us -> 39.4 us  [shift(): return lax.ppermute(value, AXES, perm)]
    psum x1 -> x0, waiting for transfers between devices: 210 us -> none  [shards_block(): lax.psum((vector_grad, gathered_mods, g_patch_w, g_final_w, local_loss, j...]
    add x32 -> x3, other arithmetic: 86 us -> 3.49 us  [the longest x2 3.48 us: two_parts(): return both[:value.shape[0]] + both[value.shape[0]:]]
    psum x1 -> x0, blocking collectives: 37.8 us -> none  [shards_block(): lax.psum((vector_grad, gathered_mods, g_patch_w, g_final_w, local_loss, j...]
    dynamic_update_slice x5 -> x0, local copies, waits for them, and re-layouts: 26.2 us -> none  [the longest x1 20.8 us: shards_block(): lax.dynamic_update_slice(jnp.zeros((EMB_PAD * LANE_TILES, LANES), jnp.flo...]
    unnamed x643 -> x373, local copies, waits for them, and re-layouts: 88.2 us -> 67.7 us
  transfers between devices with their start and end apart: 180 -> 42, of which waited for: 40 -> 11; matrix products, arithmetic and copies ran while one was open for 32% -> 29% of each run, Pallas kernels for 4% -> 11%
where the time goes in v2:
time: 1820 us; the launch traced here: 1810 us
  Pallas kernels  927 us (51%)
  matrix products  361 us (20%)
  local copies, waits for them, and re-layouts  261 us (14%)
  other arithmetic  132 us (7%)
  starting transfers between devices  57.6 us (3%)
  waiting for transfers between devices  42.2 us (2%)
  between operations  32.1 us (2%)
    pallas_call x2, Pallas kernels, collect_shard(): pl.pallas_call(kernel, in_specs=[spec] * 2, out_specs=[spec] * 2, out_sha...  506 us
    pallas_call x2, Pallas kernels, spread_shards(): pl.pallas_call(partial(spread_kernel, groups, modes), in_specs=[spec] * (...  367 us
    dot_general x25, matrix products, weight_grad(): lax.dot_general(left, right, (((0,), (0,)), ((), ())), preferred_element_...  112 us
    dot_general x21, matrix products, matmul_low(): lax.dot_general(left, right, (((left.ndim - 1,), (0,)), ((), ())), prefer...  97.8 us
    dot_general x14, matrix products, back_low(): lax.dot_general(grads, weight, (((grads.ndim - 1,), (1,)), ((), ())), pre...  97.2 us
    unnamed x373, local copies, waits for them, and re-layouts  67.7 us
    pallas_call x2, Pallas kernels, step_shard(): pl.pallas_call(partial(step_kernel, widths), grid_spec=pltpu.PrefetchScal...  48.1 us
    ppermute x37, starting transfers between devices, shift(): return lax.ppermute(value, AXES, perm)  39.4 us
  transfers between devices with their start and end apart: 42, of which 11 were waited for; matrix products, arithmetic and copies ran while one was open for 29% of the time, Pallas kernels for 11%

profile of v2, /device:TPU:0, one launch (start us, length us, event | category | flops | bytes accessed | tf_op | source)
XLA Modules:
  0.0 1812.6 jit_solution(4403328219893785458)
XLA Ops:
  19.8 207.8 %shard_map.512 = (bf16[7424,1152]{1,0:T(8,128)(2,1)}, bf16[1152,4608]{1,0:T(8,128)(2,1)}, bf16[4608,1152]{1,0:T(8,128)(2,1)}, f32[8,8,128]{2,1,0:T(8,128)S(1)}) custom-call(bf16[4,464,1152]{2,1,0:T(8,128)(2,1)} %bitcast.543, bf16[6,192,1152]{2,1,0:T(8,128)(2,1)S(1)} %bitcast.555, f32[8,128]{1,0:T(8,128)S(1)} %broadcast_in_dim.116.refs_2_), custom_call_target="tpu_custom_call" | custom-call | bytes 200000000 | tf_op jit(solution)/shard_map/pallas_call | solution.py:938
  236.5 9.4 multiply_convert_fusion.12
  263.8 158.8 %shard_map.514 = (bf16[1152,3456]{1,0:T(8,128)(2,1)}, bf16[1152,1152]{1,0:T(8,128)(2,1)}, bf16[1152,3456]{1,0:T(8,128)(2,1)}, bf16[1152,1152]{1,0:T(8,128)(2,1)}...) custom-call(bf16[6,288,1152]{2,1,0:T(8,128)(2,1)} %bitcast.554, ...), custom_call_target="tpu_custom_call" | custom-call | bytes 200000000 | tf_op jit(solution)/shard_map/pallas_call | solution.py:938
  457.1 15.5 collective-permute-start.1
  480.2 9.8 collective-permute-done.2
  492.2 7.7 fusion.29
  534.2 9.9 all-to-all-done
  550.9 7.7 fusion.32
  655.8 13.8 multiply_convert_fusion
  669.7 8.6 fusion.485
  684.4 16.4 convert_reduce_fusion
  700.9 13.6 multiply_reduce_fusion.11
  757.6 8.1 convert_reduce_fusion.6
  951.3 10.3 convert_reduce_fusion.7
  988.5 9.2 multiply_reduce_fusion.8
  1028.4 7.5 fusion.162
  1078.9 7.8 fusion.71.chunks
  1086.7 202.8 %shard_map.515 = (f32[2,576,1152]{2,1,0:T(8,128)}, f32[120,1152]{1,0:T(8,128)}) custom-call(f32[8,576,1152]{2,1,0:T(8,128)} %fusion.71.chunks, f32[120,1152]{1,0:T(8,128)} %reshape.1204.beside), custom_call_target="tpu_custom_call" | custom-call | bytes 800000000 | tf_op jit(solution)/shard_map/pallas_call | solution.py:1237
  1333.6 19.7 %fusion.338 = f32[240,7424]{1,0:T(8,128)} fusion(bf16[7424,1152]{1,0:T(8,128)(2,1)} %get-tuple-element.45, bf16[120,1152]{1,0:T(8,128)(2,1)S(1)} %subtract_convert_fusion.3, bf16[120,1152]{1,0:T(8,128)(2,1)S(1)} %convert_element_type.582), kind=kOutput, calls=%fused_computation.435 | convolution fusion | flops 4106280960 | bytes 24784896 | tf_op jit(solution)/shard_map/dot_general | solution.py:111
  1378.6 7.8 fusion.35
  1392.0 303.5 %shard_map.516 = (f32[2,864,1152]{2,1,0:T(8,128)}, f32[4,464,1152]{2,1,0:T(8,128)}) custom-call(f32[8,864,1152]{2,1,0:T(8,128)} %fusion.53.chunks, f32[464,1152]{1,0:T(8,128)} %fusion.79.beside), custom_call_target="tpu_custom_call" | custom-call | bytes 800000000 | tf_op jit(solution)/shard_map/pallas_call | solution.py:1237
  1731.2 19.8 %shard_map.519 = (f32[10368,128]{1,0:T(8,128)}, f32[10368,128]{1,0:T(8,128)}, f32[10368,128]{1,0:T(8,128)}, f32[10368,128]{1,0:T(8,128)}) custom-call(s32[4,3]{1,0:T(4,128)S(1)} %fusion.408.table, f32[1]{0:T(128)} %bitcast.155.factor, f32[1152,1152]{1,0:T(8,128)} %bitcast.559, f32[10368,128]{1,0:T(8,128)} %bitcast.552, f32[10368,128]{1,0:T(8,128)} %bitcast.580, ...), custom_call_target="tpu_custom_call" | custom-call | tf_op jit(solution)/shard_map/pallas_call | solution.py:1368
  1751.1 28.3 %shard_map.518 = (f32[15552,128]{1,0:T(8,128)}, f32[15552,128]{1,0:T(8,128)}, f32[15552,128]{1,0:T(8,128)}, f32[15552,128]{1,0:T(8,128)}) custom-call(s32[6,3]{1,0:T(8,128)S(1)} %copy.380.table, f32[1]{0:T(128)} %bitcast.155.factor, f32[1728,1152]{1,0:T(8,128)} %bitcast.558, f32[15552,128]{1,0:T(8,128)} %bitcast.550, f32[15552,128]{1,0:T(8,128)} %bitcast.574, ...), custom_call_target="tpu_custom_call" | custom-call | tf_op jit(solution)/shard_map/pallas_call | solution.py:1368
  1779.3 25.0 %multiply_add_fusion.1 = (f32[2019840]{0:T(1024)}, f32[2019840]{0:T(1024)}, f32[2019840]{0:T(1024)}, f32[2019840]{0:T(1024)}) fusion(f32[2019840]{0:T(1024)} %param.58, f32[2019840]{0:T(1024)S(1)} %bitcast.549, f32[]{:T(128)} %min.7, f32[16704,128]{1,0:T(8,128)} %copy-done.2, s32[]{:T(128)S(6)} %select_n.233, f32[2019840]{0:T(1024)} %param.50, f32[2019840]{0:T(1024)} %param.54), kind=kLoop, calls=%fused_computation.38 | loop fusion | flops 36357120 | bytes 72714248 | tf_op jit(solution)/shard_map/add | solution.py:209
  (827 shorter events, 651.6 us)
Async XLA Ops:
  428.3 27.8 %collective-permute-start = (f32[48,1152]{1,0:T(8,128)}, f32[48,1152]{1,0:T(8,128)}, u32[]{:S(2)}, u32[]{:S(2)}) collective-permute-start(f32[48,1152]{1,0:T(8,128)} %fusion.505), channel_id=1, source_target_pairs={{0,1},{1,0},{2,3},{3,2},{4,5},{5,4},{6,7},{7,6},{8,9},{9,8},{10,11... | collective-permute-start | bytes 663560 | tf_op jit(solution)/shard_map/ppermute | solution.py:573
  457.1 20.7 %collective-permute-start.1 = (f32[48,1152]{1,0:T(8,128)S(1)}, f32[48,1152]{1,0:T(8,128)S(1)}, u32[]{:S(2)}, u32[]{:S(2)}) collective-permute-start(f32[48,1152]{1,0:T(8,128)S(1)} %add.774), channel_id=1, source_target_pairs={{0,2},{1,3},{2,0},{3,1},{4,6},{5,7},{6,4},{7,5},{8,10},{9,11},{10,... | collective-permute-start | bytes 663560 | tf_op jit(solution)/shard_map/ppermute | solution.py:573
  523.7 20.4 %all-to-all-start = ((bf16[1,2,256,1152]{3,1,0,2:T(2,128)(2,1)}), bf16[1,2,256,1152]{3,1,0,2:T(2,128)(2,1)}, u32[]{:S(2)}, u32[]{:S(2)}) async-start(bf16[1,2,256,1152]{3,1,0,2:T(2,128)(2,1)} %copy.328), calls=%async_computation | async-start | bytes 2359296 | tf_op jit(solution)/shard_map/all_to_all | solution.py:1605
  533.7 88.9 %collective-permute-start.12 = (bf16[512,1152]{1,0:T(8,128)(2,1)}, bf16[512,1152]{1,0:T(8,128)(2,1)}, u32[]{:S(2)}, u32[]{:S(2)}) collective-permute-start(bf16[512,1152]{1,0:T(8,128)(2,1)} %bitcast.117), channel_id=1, source_target_pairs={{0,8},{1,9},{2,10},{3,11},{4,12},{5,13},{6,14},{7,15},{8,0},{9,1},... | collective-permute-start | bytes 3538952 | tf_op jit(solution)/shard_map/ppermute | solution.py:573
  597.0 30.0 %all-to-all-start.1 = ((bf16[1,8,64,1152]{3,2,0,1:T(8,128)(2,1)}), bf16[1,8,64,1152]{3,2,0,1:T(8,128)(2,1)}, u32[]{:S(2)}, u32[]{:S(2)}) async-start(bf16[1,8,64,1152]{3,2,0,1:T(8,128)(2,1)} %copy.335), calls=%async_computation.1 | async-start | bytes 2359296 | tf_op jit(solution)/shard_map/all_to_all | solution.py:1616
  621.4 406.9 %collective-permute-start.16 = (bf16[512,1152]{0,1:T(8,128)(2,1)}, bf16[512,1152]{0,1:T(8,128)(2,1)}, u32[]{:S(2)}, u32[]{:S(2)}) collective-permute-start(bf16[512,1152]{0,1:T(8,128)(2,1)} %bitcast.219), channel_id=1, source_target_pairs={{0,8},{1,9},{2,10},{3,11},{4,12},{5,13},{6,14},{7,15},{8,0},{9,1},... | collective-permute-start | bytes 3538952 | tf_op jit(solution)/shard_map/ppermute | solution.py:573
  622.5 161.7 %collective-permute-start.18 = (bf16[512,1152]{1,0:T(8,128)(2,1)}, bf16[512,1152]{1,0:T(8,128)(2,1)}, u32[]{:S(2)}, u32[]{:S(2)}) collective-permute-start(bf16[512,1152]{1,0:T(8,128)(2,1)} %bitcast.121), channel_id=1, source_target_pairs={{0,8},{1,9},{2,10},{3,11},{4,12},{5,13},{6,14},{7,15},{8,0},{9,1},... | collective-permute-start | bytes 3538952 | tf_op jit(solution)/shard_map/ppermute | solution.py:573
  750.9 99.2 %collective-permute-start.10 = (f32[120,2304]{1,0:T(8,128)}, f32[120,2304]{1,0:T(8,128)}, u32[]{:S(2)}, u32[]{:S(2)}) collective-permute-start(f32[120,2304]{1,0:T(8,128)} %maximum_bitcast_fusion.15), channel_id=1, source_target_pairs={{0,8},{1,9},{2,10},{3,11},{4,12},{5,13},{6,14},{7,15},{8,0},{9,1},... | collective-permute-start | bytes 3317768 | tf_op jit(solution)/shard_map/ppermute | solution.py:573
  769.9 19.5 %all-to-all-start.2 = ((bf16[1,2,256,1152]{3,1,0,2:T(2,128)(2,1)}), bf16[1,2,256,1152]{3,1,0,2:T(2,128)(2,1)S(1)}, u32[]{:S(2)}, u32[]{:S(2)}) async-start(bf16[1,2,256,1152]{3,1,0,2:T(2,128)(2,1)} %copy.345), calls=%async_computation.2 | async-start | bytes 2359296 | tf_op jit(solution)/shard_map/all_to_all | solution.py:1711
  783.7 77.5 %collective-permute-start.4 = (bf16[512,1152]{1,0:T(8,128)(2,1)}, bf16[512,1152]{1,0:T(8,128)(2,1)}, u32[]{:S(2)}, u32[]{:S(2)}) collective-permute-start(bf16[512,1152]{1,0:T(8,128)(2,1)} %bitcast.63), channel_id=1, source_target_pairs={{0,8},{1,9},{2,10},{3,11},{4,12},{5,13},{6,14},{7,15},{8,0},{9,1},... | collective-permute-start | bytes 3538952 | tf_op jit(solution)/shard_map/ppermute | solution.py:573
  784.2 72.9 %collective-permute-start.3 = (bf16[512,1152]{1,0:T(8,128)(2,1)}, bf16[512,1152]{1,0:T(8,128)(2,1)}, u32[]{:S(2)}, u32[]{:S(2)}) collective-permute-start(bf16[512,1152]{1,0:T(8,128)(2,1)} %bitcast.52), channel_id=1, source_target_pairs={{0,8},{1,9},{2,10},{3,11},{4,12},{5,13},{6,14},{7,15},{8,0},{9,1},... | collective-permute-start | bytes 3538952 | tf_op jit(solution)/shard_map/ppermute | solution.py:573
  784.2 80.8 %collective-permute-start.5 = (bf16[512,1152]{1,0:T(8,128)(2,1)}, bf16[512,1152]{1,0:T(8,128)(2,1)}, u32[]{:S(2)}, u32[]{:S(2)}) collective-permute-start(bf16[512,1152]{1,0:T(8,128)(2,1)} %bitcast.64), channel_id=1, source_target_pairs={{0,8},{1,9},{2,10},{3,11},{4,12},{5,13},{6,14},{7,15},{8,0},{9,1},... | collective-permute-start | bytes 3538952 | tf_op jit(solution)/shard_map/ppermute | solution.py:573
  844.6 103.9 %all-to-all-start.3 = ((bf16[1,8,64,3456]{3,2,0,1:T(8,128)(2,1)}), bf16[1,8,64,3456]{3,2,0,1:T(8,128)(2,1)}, u32[]{:S(2)}, u32[]{:S(2)}) async-start(bf16[1,8,64,3456]{3,2,0,1:T(8,128)(2,1)} %copy.358), calls=%async_computation.3 | async-start | bytes 7077888 | tf_op jit(solution)/shard_map/all_to_all | solution.py:1727
  849.4 481.4 %all-gather.2.cloned.1.call-start = ((), (), s32[]{:S(2)}) async-start(), calls=%async_computation.4 | async-start | bytes 9953280 | tf_op jit(solution)/shard_map/all_gather | solution.py:1768
  861.2 32.1 %collective-permute-start.27 = (bf16[512,1152]{1,0:T(8,128)(2,1)}, bf16[512,1152]{1,0:T(8,128)(2,1)}, u32[]{:S(2)}, u32[]{:S(2)}) collective-permute-start(bf16[512,1152]{1,0:T(8,128)(2,1)} %bitcast.137), channel_id=1, source_target_pairs={{0,8},{1,9},{2,10},{3,11},{4,12},{5,13},{6,14},{7,15},{8,0},{9,1},... | collective-permute-start | bytes 3538952 | tf_op jit(solution)/shard_map/ppermute | solution.py:573
  865.1 28.3 %collective-permute-start.26 = (bf16[512,1152]{0,1:T(8,128)(2,1)}, bf16[512,1152]{0,1:T(8,128)(2,1)}, u32[]{:S(2)}, u32[]{:S(2)}) collective-permute-start(bf16[512,1152]{0,1:T(8,128)(2,1)} %bitcast.135), channel_id=1, source_target_pairs={{0,8},{1,9},{2,10},{3,11},{4,12},{5,13},{6,14},{7,15},{8,0},{9,1},... | collective-permute-start | bytes 3538952 | tf_op jit(solution)/shard_map/ppermute | solution.py:573
  878.6 26.0 %collective-permute-start.25 = (bf16[512,1152]{0,1:T(8,128)(2,1)}, bf16[512,1152]{0,1:T(8,128)(2,1)}, u32[]{:S(2)}, u32[]{:S(2)}) collective-permute-start(bf16[512,1152]{0,1:T(8,128)(2,1)} %bitcast.130), channel_id=1, source_target_pairs={{0,8},{1,9},{2,10},{3,11},{4,12},{5,13},{6,14},{7,15},{8,0},{9,1},... | collective-permute-start | bytes 3538952 | tf_op jit(solution)/shard_map/ppermute | solution.py:573
  880.7 24.0 %collective-permute-start.24 = (bf16[512,1152]{1,0:T(8,128)(2,1)}, bf16[512,1152]{1,0:T(8,128)(2,1)}, u32[]{:S(2)}, u32[]{:S(2)}) collective-permute-start(bf16[512,1152]{1,0:T(8,128)(2,1)} %bitcast.129), channel_id=1, source_target_pairs={{0,8},{1,9},{2,10},{3,11},{4,12},{5,13},{6,14},{7,15},{8,0},{9,1},... | collective-permute-start | bytes 3538952 | tf_op jit(solution)/shard_map/ppermute | solution.py:573
  893.3 26.6 %collective-permute-start.19 = (bf16[512,1152]{1,0:T(8,128)(2,1)}, bf16[512,1152]{1,0:T(8,128)(2,1)}, u32[]{:S(2)}, u32[]{:S(2)}) collective-permute-start(bf16[512,1152]{1,0:T(8,128)(2,1)} %reshape_reshape.32), channel_id=1, source_target_pairs={{0,8},{1,9},{2,10},{3,11},{4,12},{5,13},{6,14},{7,15},{8,0},{9,1},... | collective-permute-start | bytes 3538952 | tf_op jit(solution)/shard_map/ppermute | solution.py:573
  893.3 33.1 %collective-permute-start.20 = (bf16[512,1152]{1,0:T(8,128)(2,1)}, bf16[512,1152]{1,0:T(8,128)(2,1)}, u32[]{:S(2)}, u32[]{:S(2)}) collective-permute-start(bf16[512,1152]{1,0:T(8,128)(2,1)} %reshape_reshape.33), channel_id=1, source_target_pairs={{0,8},{1,9},{2,10},{3,11},{4,12},{5,13},{6,14},{7,15},{8,0},{9,1},... | collective-permute-start | bytes 3538952 | tf_op jit(solution)/shard_map/ppermute | solution.py:573
  904.6 27.0 %collective-permute-start.21 = (bf16[512,1152]{1,0:T(8,128)(2,1)}, bf16[512,1152]{1,0:T(8,128)(2,1)}, u32[]{:S(2)}, u32[]{:S(2)}) collective-permute-start(bf16[512,1152]{1,0:T(8,128)(2,1)} %reshape_reshape.34), channel_id=1, source_target_pairs={{0,8},{1,9},{2,10},{3,11},{4,12},{5,13},{6,14},{7,15},{8,0},{9,1},... | collective-permute-start | bytes 3538952 | tf_op jit(solution)/shard_map/ppermute | solution.py:573
  904.7 33.0 %collective-permute-start.11 = (f32[120,2304]{1,0:T(8,128)S(1)}, f32[120,2304]{1,0:T(8,128)}, u32[]{:S(2)}, u32[]{:S(2)}) collective-permute-start(f32[120,2304]{1,0:T(8,128)S(1)} %fusion.468), channel_id=1, source_target_pairs={{0,16},{1,17},{2,18},{3,19},{4,20},{5,21},{6,22},{7,23},{8,24},{9,... | collective-permute-start | bytes 3317768 | tf_op jit(solution)/shard_map/ppermute | solution.py:573
  919.9 136.9 %collective-permute-start.9 = (bf16[512,1152]{1,0:T(8,128)(2,1)}, bf16[512,1152]{1,0:T(8,128)(2,1)}, u32[]{:S(2)}, u32[]{:S(2)}) collective-permute-start(bf16[512,1152]{1,0:T(8,128)(2,1)} %bitcast.72), channel_id=1, source_target_pairs={{0,8},{1,9},{2,10},{3,11},{4,12},{5,13},{6,14},{7,15},{8,0},{9,1},... | collective-permute-start | bytes 3538952 | tf_op jit(solution)/shard_map/ppermute | solution.py:573
  926.5 130.3 %collective-permute-start.8 = (bf16[512,4608]{1,0:T(8,128)(2,1)}, bf16[512,4608]{1,0:T(8,128)(2,1)}, u32[]{:S(2)}, u32[]{:S(2)}) collective-permute-start(bf16[512,4608]{1,0:T(8,128)(2,1)} %bitcast.71), channel_id=1, source_target_pairs={{0,8},{1,9},{2,10},{3,11},{4,12},{5,13},{6,14},{7,15},{8,0},{9,1},... | collective-permute-start | bytes 14155784 | tf_op jit(solution)/shard_map/ppermute | solution.py:573
  (211 other events, 1654.3 us)
Sparse Core Ops, SparseCore 0:
  948.6 128.7 all-gather.1

commit v3 on v2

--- a/solution.py
+++ b/solution.py
@@ -1384,6 +1384,141 @@
     return [value.reshape(-1) for value in made]
 
 
+def head_span(head):
+    width = D // HEADS
+    start = head * width // LANES * LANES
+    stop = -(-(head + 1) * width // LANES) * LANES
+    lane = start + lax.broadcasted_iota(jnp.int32, (1, stop - start), 1)
+    ones = (lane >= head * width) & (lane < (head + 1) * width)
+    return slice(start, stop), ones.astype(jnp.float32).astype(jnp.bfloat16)
+
+
+def dot_rows(left, right):
+    return lax.dot_general(left, right, (((1,), (1,)), ((), ())), preferred_element_type=jnp.float32)
+
+
+def dot_down(left, right):
+    return lax.dot_general(left, right, (((0,), (0,)), ((), ())), preferred_element_type=jnp.float32)
+
+
+def live_keys(mode, live, n_queries, n_keys):
+    key = lax.broadcasted_iota(jnp.int32, (n_queries, n_keys), 1)
+    if mode == "cross":
+        return key < live[0]
+    if mode == "all":
+        return None
+    query = lax.broadcasted_iota(jnp.int32, (n_queries, n_keys), 0)
+    return query // mode == key // mode
+
+
+def head_scores(queries, keys, valid):
+    scores = dot_rows(queries, keys) * (D // HEADS) ** (-0.5)
+    return scores if valid is None else jnp.where(valid, scores, MASKED_SCORE)
+
+
+def heads_kernel(mode, live, queries, keys, values, out, log_total, total):
+    n_queries, n_keys = queries.shape[0], keys.shape[0]
+    valid = live_keys(mode, live, n_queries, n_keys)
+    lane = lax.broadcasted_iota(jnp.int32, (1, LANES), 1)
+    total[...] = jnp.zeros_like(total)
+    log_total[...] = jnp.zeros_like(log_total)
+    for head in range(HEADS):
+        span, ones = head_span(head)
+        scores = head_scores(queries[:, span], keys[:, span] * ones, valid)
+        summit = jnp.max(scores, -1, keepdims=True)
+        powers = jnp.exp(scores - summit)
+        sums = jnp.sum(powers, -1, keepdims=True)
+        probs = (powers / sums).astype(jnp.bfloat16)
+        total[:, span] += jnp.dot(
+            probs, values[:, span] * ones, preferred_element_type=jnp.float32
+        )
+        log_total[...] += jnp.where(lane == head, summit + jnp.log(sums), 0.0)
+    out[...] = total[...].astype(jnp.bfloat16)
+
+
+def heads_back_kernel(
+    mode, live, queries, keys, values, log_total, grad_out, grad_q, grad_k, grad_v, sum_q, sum_k, sum_v
+):
+    n_queries, n_keys = queries.shape[0], keys.shape[0]
+    valid = live_keys(mode, live, n_queries, n_keys)
+    scale = (D // HEADS) ** (-0.5)
+    block, last = pl.program_id(0), pl.num_programs(0) - 1
+    sum_q[...] = jnp.zeros_like(sum_q)
+
+    @pl.when((block == 0) | (mode != "cross"))
+    def _():
+        sum_k[...] = jnp.zeros_like(sum_k)
+        sum_v[...] = jnp.zeros_like(sum_v)
+
+    for head in range(HEADS):
+        span, ones = head_span(head)
+        some_keys = keys[:, span] * ones
+        scores = head_scores(queries[:, span], some_keys, valid)
+        probs = jnp.exp(scores - log_total[:, head : head + 1])
+        grad_probs = dot_rows(grad_out[:, span], values[:, span] * ones)
+        row = jnp.sum(probs * grad_probs, -1, keepdims=True)
+        grad_scores = (probs * (grad_probs - row)).astype(jnp.bfloat16)
+        sum_q[:, span] += jnp.dot(grad_scores, some_keys, preferred_element_type=jnp.float32)
+        sum_k[:, span] += dot_down(grad_scores, queries[:, span] * ones)
+        sum_v[:, span] += dot_down(probs.astype(jnp.bfloat16), grad_out[:, span] * ones)
+    grad_q[...] = (sum_q[...] * scale).astype(grad_q.dtype)
+
+    @pl.when((block == last) | (mode != "cross"))
+    def _():
+        grad_k[...] = (sum_k[...] * scale).astype(grad_k.dtype)
+        grad_v[...] = sum_v[...].astype(grad_v.dtype)
+
+
+HEAD_ROWS = 256
+
+
+def heads_specs(mode, keys):
+    own = pl.BlockSpec((HEAD_ROWS, D), lambda b: (b, 0))
+    side = pl.BlockSpec((HEAD_ROWS, LANES), lambda b: (b, 0))
+    shared = pl.BlockSpec(keys.shape, lambda b: (0, 0)) if mode == "cross" else own
+    return own, side, shared
+
+
+def heads_forward(mode, queries, keys, values, live):
+    own, side, shared = heads_specs(mode, keys)
+    n_keys = keys.shape[0] if mode == "cross" else HEAD_ROWS
+    return pl.pallas_call(
+        partial(heads_kernel, mode),
+        grid=(queries.shape[0] // HEAD_ROWS,),
+        in_specs=[pl.BlockSpec(memory_space=pltpu.SMEM), own, shared, shared],
+        out_specs=[own, side],
+        out_shape=[
+            jax.ShapeDtypeStruct(queries.shape, jnp.bfloat16),
+            jax.ShapeDtypeStruct((queries.shape[0], LANES), jnp.float32),
+        ],
+        scratch_shapes=[pltpu.VMEM((HEAD_ROWS, D), jnp.float32)],
+        compiler_params=pltpu.CompilerParams(vmem_limit_bytes=32 * 1024 * 1024),
+    )(live, queries, keys, values)
+
+
+def heads_backward(mode, queries, keys, values, live, log_total, grad_out):
+    own, side, shared = heads_specs(mode, keys)
+    n_keys = keys.shape[0] if mode == "cross" else HEAD_ROWS
+    kind = jnp.float32 if mode == "cross" else jnp.bfloat16
+    return pl.pallas_call(
+        partial(heads_back_kernel, mode),
+        grid=(queries.shape[0] // HEAD_ROWS,),
+        in_specs=[pl.BlockSpec(memory_space=pltpu.SMEM), own, shared, shared, side, own],
+        out_specs=[own, shared, shared],
+        out_shape=[
+            jax.ShapeDtypeStruct(queries.shape, jnp.bfloat16),
+            jax.ShapeDtypeStruct(keys.shape, kind),
+            jax.ShapeDtypeStruct(keys.shape, kind),
+        ],
+        scratch_shapes=[
+            pltpu.VMEM((HEAD_ROWS, D), jnp.float32),
+            pltpu.VMEM((n_keys, D), jnp.float32),
+            pltpu.VMEM((n_keys, D), jnp.float32),
+        ],
+        compiler_params=pltpu.CompilerParams(vmem_limit_bytes=40 * 1024 * 1024),
+    )(live, queries, keys, values, log_total, grad_out)
+
+
 ROW_TIME_ONE = PATCH_VALUES
 ROW_TIME_TWO = ROW_TIME_ONE + TFREQ
 ROW_BLOCK = ROW_TIME_TWO + D
@@ -1536,7 +1671,6 @@
     act_rows = jnp.pad(cap_act[0], ((0, 0), (two_first, EMB_PAD - two_first - D)))
     cap_rows = (matmul_low(act_rows, cap_last) + cap_b2).astype(jnp.bfloat16)[None]
     live_len = jnp.where(is_null, L_CAP, cap_lengths)
-    key_mask = jnp.arange(L_CAP)[None, :] < live_len[:, None]
     cap_wide = jnp.concatenate([cap_in[0], cap_act[0]], -1)
     cap_wide = jnp.pad(cap_wide, ((0, 0), (EMB_PAD, EMB_PAD)))
     wanted = []
@@ -1594,11 +1728,9 @@
         return value.reshape(-1, value.shape[-1])
 
     space_in = modulate(hidden_zero, mod_row(0), mod_row(1)).astype(jnp.bfloat16)
-    space_q, space_k, space_v = (
-        heads_of(piece, clip_dev * frame_dev)
-        for piece in split_qkv(matmul_low(space_in, space_qkv), space_bq, space_bv)
-    )
-    space_o, space_lse = attend_forward(space_q, space_k, space_v, None)
+    live = live_len.astype(jnp.int32)
+    space_q, space_k, space_v = split_qkv(matmul_low(flat2(space_in), space_qkv), space_bq, space_bv)
+    space_o, space_lse = heads_forward("all", space_q, space_k, space_v, live)
     space_flat = space_o.reshape(clip_dev, frame_dev, patches, D)
     space_res = matmul_low(space_flat, space_out) + space_bo
     hidden_one = hidden_zero + mod_row(2) * space_res
@@ -1607,23 +1739,18 @@
     )
     time_in = jnp.swapaxes(time_in, 1, 2)
     frames = time_in.shape[2]
-    time_q, time_k, time_v = (
-        heads_of(piece, clip_dev * local_pos)
-        for piece in split_qkv(matmul_low(time_in, time_qkv), time_bq, time_bv)
-    )
-    time_o, time_lse = attend_forward(time_q, time_k, time_v, None)
+    time_q, time_k, time_v = split_qkv(matmul_low(flat2(time_in), time_qkv), time_bq, time_bv)
+    time_o, time_lse = heads_forward(frames, time_q, time_k, time_v, live)
     time_back = jnp.swapaxes(time_o.reshape(clip_dev, local_pos, frames, D), 1, 2)
     time_flat = lax.all_to_all(time_back, "frame", split_axis=1, concat_axis=2, tiled=True)
     time_res = matmul_low(time_flat, time_out) + time_bo
     hidden_two = hidden_one + mod_row(2) * time_res
     cross_in = hidden_two.astype(jnp.bfloat16)
-    cross_query = heads_of(
-        (matmul_low(cross_in, cross_q) + cross_bq).astype(jnp.bfloat16), clip_dev
-    )
-    cross_merged = matmul_low(cap_rows, cross_kv)
-    cross_k = heads_of(cross_merged[..., :D].astype(jnp.bfloat16), clip_dev)
-    cross_v = heads_of((cross_merged[..., D:] + cross_bv).astype(jnp.bfloat16), clip_dev)
-    cross_o, cross_lse = attend_forward(cross_query, cross_k, cross_v, key_mask)
+    cross_query = (matmul_low(flat2(cross_in), cross_q) + cross_bq).astype(jnp.bfloat16)
+    cross_merged = matmul_low(jnp.pad(cap_rows[0], ((0, -L_CAP % 16), (0, 0))), cross_kv)
+    cross_k = cross_merged[..., :D].astype(jnp.bfloat16)
+    cross_v = (cross_merged[..., D:] + cross_bv).astype(jnp.bfloat16)
+    cross_o, cross_lse = heads_forward("cross", cross_query, cross_k, cross_v, live)
     cross_flat = cross_o.reshape(clip_dev, frame_dev, patches, D)
     hidden_three = hidden_two + matmul_low(cross_flat, cross_out) + cross_bo
     dense_in = modulate(hidden_three, mod_row(3), mod_row(4)).astype(jnp.bfloat16)
@@ -1688,16 +1815,16 @@
     grad_cross = grad_hidden.astype(jnp.bfloat16)
     grads["cross_out"] = core_grad(inputs["cross_out"], [grad_cross])
     g_cross_bo = bias_grad(grad_cross)
-    grad_cross_o = heads_of(back_low(grad_cross, cross_out).astype(jnp.bfloat16), clip_dev)
-    grad_cq, grad_ck, grad_cv = attend_backward(
-        cross_query, cross_k, cross_v, key_mask, cross_lse, grad_cross_o
-    )
-    grad_cq = grad_cq.astype(jnp.bfloat16).reshape(clip_dev, frame_dev, patches, D)
+    grad_cross_o = back_low(flat2(grad_cross), cross_out).astype(jnp.bfloat16)
+    grad_cq, grad_ck, grad_cv = heads_backward(
+        "cross", cross_query, cross_k, cross_v, live, cross_lse, grad_cross_o
+    )
+    grad_cq = grad_cq.reshape(clip_dev, frame_dev, patches, D)
     grads["cross_q"] = core_grad(inputs["cross_q"], [grad_cq])
     g_cross_bq = bias_grad(grad_cq)
     grad_hidden = grad_hidden + back_low(grad_cq, cross_q)
-    grad_cv = grad_cv.reshape(clip_dev, L_CAP, D)
-    grad_ckv = jnp.concatenate([grad_ck.reshape(clip_dev, L_CAP, D), grad_cv], -1)[0]
+    grad_cv = grad_cv[:L_CAP]
+    grad_ckv = jnp.concatenate([grad_ck[:L_CAP], grad_cv], -1)
     g_cross_bv = bias_grad(grad_cv)
     grad_ckv = grad_ckv + shift(grad_ckv, SWAP_CORE)
     cap_half = pick_columns(cap_rows[0], half_rows(ATTEND_SEGS, "cross_kv"), core_id)
@@ -1715,11 +1842,10 @@
         concat_axis=1,
         tiled=True,
     )
-    grad_time_o = heads_of(jnp.swapaxes(grad_time_o, 1, 2), clip_dev * local_pos)
-    grad_tq, grad_tk, grad_tv = attend_backward(time_q, time_k, time_v, None, time_lse, grad_time_o)
+    grad_time_o = flat2(jnp.swapaxes(grad_time_o, 1, 2))
     grad_tqkv = [
-        piece.astype(jnp.bfloat16).reshape(clip_dev, local_pos, frames, D)
-        for piece in (grad_tq, grad_tk, grad_tv)
+        piece.reshape(clip_dev, local_pos, frames, D)
+        for piece in heads_backward(frames, time_q, time_k, time_v, live, time_lse, grad_time_o)
     ]
     grads["time_qkv"] = core_grad(inputs["time_qkv"], grad_tqkv)
     g_time_bq = bias_grad(grad_tqkv[0])
@@ -1733,12 +1859,10 @@
     grad_space = (grad_hidden * mod_row(2)).astype(jnp.bfloat16)
     grads["space_out"] = core_grad(inputs["space_out"], [grad_space])
     g_space_bo = bias_grad(grad_space)
-    grad_space_o = heads_of(
-        back_low(grad_space, space_out).astype(jnp.bfloat16), clip_dev * frame_dev
-    )
+    grad_space_o = back_low(flat2(grad_space), space_out).astype(jnp.bfloat16)
     grad_sqkv = [
-        piece.astype(jnp.bfloat16).reshape(clip_dev, frame_dev, patches, D)
-        for piece in attend_backward(space_q, space_k, space_v, None, space_lse, grad_space_o)
+        piece.reshape(clip_dev, frame_dev, patches, D)
+        for piece in heads_backward("all", space_q, space_k, space_v, live, space_lse, grad_space_o)
     ]
     grads["space_qkv"] = core_grad(inputs["space_qkv"], grad_sqkv)
     g_space_bq = bias_grad(grad_sqkv[0])
@@ -1775,29 +1899,28 @@
     once = frame_id == 0
     gathered_mods = jnp.where(own_clip[:, None, None], grad_mods[None], 0.0)
     zero_d = jnp.zeros((D,), jnp.float32)
-    vector_grad = flatten_all(
-        [
-            g_patch_b,
-            jnp.where(once, g_cap_b1, 0.0),
-            jnp.where(once, g_cap_b2, 0.0),
-            g_space_bq,
-            g_space_bv,
-            g_space_bo,
-            g_time_bq,
-            g_time_bv,
-            g_time_bo,
-            g_cross_bq,
-            g_cross_bv,
-            g_cross_bo,
-            g_fc_in_b,
-            g_fc_out_b,
-            g_final_b,
-        ]
-    )
-    n_vector = vector_grad.shape[0]
-    small = flatten_all([gathered_mods, g_patch_w, g_final_w, vector_grad, local_loss])
-    small_rows = -(-small.shape[0] // (8 * D)) * 8
-    small = jnp.pad(small, (0, small_rows * D - small.shape[0])).reshape(small_rows, D)
+    ends = jnp.concatenate([g_final_b, local_loss.reshape(1)])
+    vector_rows = [
+        g_patch_b,
+        jnp.where(once, g_cap_b1, 0.0),
+        jnp.where(once, g_cap_b2, 0.0),
+        g_space_bq,
+        g_space_bv,
+        g_space_bo,
+        g_time_bq,
+        g_time_bv,
+        g_time_bo,
+        g_cross_bq,
+        g_cross_bv,
+        g_cross_bo,
+        g_fc_in_b.reshape(-1, D),
+        g_fc_out_b,
+        jnp.pad(ends, (0, D - ends.shape[0])),
+    ]
+    small = [gathered_mods.reshape(-1, D), g_patch_w, g_final_w.reshape(PATCH_VALUES, D)]
+    small = small + [value.reshape(-1, D) for value in vector_rows]
+    spare = -sum(value.shape[0] for value in small) % 8
+    small = jnp.concatenate(small + [jnp.zeros((spare, D), jnp.float32)] * (spare > 0), 0)
     dense_grad, small = collect_shard(
         jnp.stack([owner_chunk(grads, DENSE_SEGS, owner) for owner in range(N_OWN)]),
         144,
@@ -1809,8 +1932,10 @@
     gathered_mods = small[:at].reshape(n_clip, 8, D)
     g_patch_w = small[at : at + PATCH_VALUES]
     g_final_w = small[at + PATCH_VALUES : at + 2 * PATCH_VALUES]
-    rest = small[at + 2 * PATCH_VALUES :].reshape(-1)
-    vector_grad, loss_sum = rest[:n_vector], rest[n_vector]
+    rest = small[at + 2 * PATCH_VALUES :]
+    n_whole = 12 + MLP // D + 1
+    loss_sum = rest[n_whole, PATCH_VALUES]
+    vector_grad = jnp.concatenate([rest[:n_whole].reshape(-1), rest[n_whole, :PATCH_VALUES]])
 
     grad_zero = gathered_mods[:, :6]
     grad_final = gathered_mods[:, 6:]

time: 1820 us -> 1750 us (0.962)
  local copies, waits for them, and re-layouts: 261 us -> 183 us
  Pallas kernels: 927 us -> 984 us
  matrix products: 361 us -> 308 us
    pallas_call x0 -> x6, Pallas kernels: none -> 57.5 us  [the longest x3 40.6 us: heads_backward(): pl.pallas_call(partial(heads_back_kernel, mode), grid=(queries.shape[0] /...]
    dot_general x18 -> x0, matrix products: 49.9 us -> none  [the longest x3 15.8 us: attend_backward(): jnp.einsum('bqhe,bkhe->bhqk', grad_out, values, preferred_element_type=jn...]
    reshape x14 -> x18, local copies, waits for them, and re-layouts: 44.3 us -> 15.6 us  [the longest x12 9.91 us: shards_block(): small = small + [value.reshape(-1, D) for value in vector_rows]]
    convert_element_type x14 -> x0, local copies, waits for them, and re-layouts: 26.1 us -> none  [the longest x2 4.53 us: attend_forward(): return (output.astype(jnp.bfloat16), summit + jnp.log(totals))]
    another operation x7 -> x0, local copies, waits for them, and re-layouts: 24.8 us -> none
    unnamed x373 -> x347, local copies, waits for them, and re-layouts: 67.7 us -> 59.3 us
  transfers between devices with their start and end apart: 42 -> 42, of which waited for: 11 -> 11; matrix products, arithmetic and copies ran while one was open for 29% -> 24% of each run, Pallas kernels for 11% -> 15%
where the time goes in v3:
time: 1750 us; the launch traced here: 1740 us
  Pallas kernels  984 us (56%)
  matrix products  308 us (18%)
  local copies, waits for them, and re-layouts  183 us (10%)
  other arithmetic  130 us (7%)
  starting transfers between devices  52.4 us (3%)
  waiting for transfers between devices  49.8 us (3%)
  between operations  31.8 us (2%)
    pallas_call x2, Pallas kernels, collect_shard(): pl.pallas_call(kernel, in_specs=[spec] * 2, out_specs=[spec] * 2, out_sha...  507 us
    pallas_call x2, Pallas kernels, spread_shards(): pl.pallas_call(partial(spread_kernel, groups, modes), in_specs=[spec] * (...  367 us
    dot_general x25, matrix products, weight_grad(): lax.dot_general(left, right, (((0,), (0,)), ((), ())), preferred_element_...  114 us
    dot_general x21, matrix products, matmul_low(): lax.dot_general(left, right, (((left.ndim - 1,), (0,)), ((), ())), prefer...  99.3 us
    dot_general x14, matrix products, back_low(): lax.dot_general(grads, weight, (((grads.ndim - 1,), (1,)), ((), ())), pre...  91.5 us
    unnamed x347, local copies, waits for them, and re-layouts  59.3 us
    pallas_call x2, Pallas kernels, step_shard(): pl.pallas_call(partial(step_kernel, widths), grid_spec=pltpu.PrefetchScal...  48.1 us
    pallas_call x3, Pallas kernels, heads_backward(): pl.pallas_call(partial(heads_back_kernel, mode), grid=(queries.shape[0] /...  40.6 us
  transfers between devices with their start and end apart: 42, of which 11 were waited for; matrix products, arithmetic and copies ran while one was open for 24% of the time, Pallas kernels for 15%

profile of v3, /device:TPU:0, one launch (start us, length us, event | category | flops | bytes accessed | tf_op | source)
XLA Modules:
  0.0 1739.3 jit_solution(2954389192623532177)
XLA Ops:
  20.3 207.8 %shard_map.512 = (bf16[7424,1152]{1,0:T(8,128)(2,1)}, bf16[1152,4608]{1,0:T(8,128)(2,1)}, bf16[4608,1152]{1,0:T(8,128)(2,1)}, f32[8,8,128]{2,1,0:T(8,128)S(1)}) custom-call(bf16[4,464,1152]{2,1,0:T(8,128)(2,1)} %bitcast.412, bf16[6,192,1152]{2,1,0:T(8,128)(2,1)S(1)} %bitcast.424, f32[8,128]{1,0:T(8,128)S(1)} %broadcast_in_dim.108.refs_2_), custom_call_target="tpu_custom_call" | custom-call | bytes 200000000 | tf_op jit(solution)/shard_map/pallas_call | solution.py:938
  237.0 9.5 multiply_convert_fusion.4
  264.3 158.9 %shard_map.514 = (bf16[1152,3456]{1,0:T(8,128)(2,1)}, bf16[1152,1152]{1,0:T(8,128)(2,1)}, bf16[1152,3456]{1,0:T(8,128)(2,1)}, bf16[1152,1152]{1,0:T(8,128)(2,1)}...) custom-call(bf16[6,288,1152]{2,1,0:T(8,128)(2,1)} %bitcast.423, ...), custom_call_target="tpu_custom_call" | custom-call | bytes 200000000 | tf_op jit(solution)/shard_map/pallas_call | solution.py:938
  473.2 15.4 collective-permute-start.1
  496.3 9.7 collective-permute-done.2
  540.4 8.2 all-to-all-done
  548.8 8.1 fusion.408
  607.8 11.8 multiply_convert_fusion
  619.6 12.9 fusion.426
  639.2 17.6 %convert_reduce_fusion = (f32[4608]{0:T(1024)}, bf16[2,256,4608]{2,1,0:T(8,128)(2,1)}) fusion(f32[2,256,4608]{2,1,0:T(8,128)} %get-tuple-element.249, f32[4608]{0:T(1024)S(1)} %copy-done.118, bf16[2,256,1152]{2,1,0:T(8,128)(2,1)} %get-tuple-element.131, bf16[4608,1152]{1,0:T(8,128)(2,1)} %get-tuple-element.73), kind=kOutput, calls=%fused_computation.26 | convolution fusion | flops 5490077184 | bytes 25989120 | tf_op jit(solution)/shard_map/dot_general | solution.py:111
  656.8 13.3 multiply_reduce_fusion.6
  678.1 12.3 shard_map.518
  750.0 14.5 shard_map.519
  880.4 8.8 convert_reduce_fusion.7
  891.7 13.9 shard_map.520
  906.5 8.5 multiply_reduce_fusion.3
  930.5 9.3 concatenate.210.beside
  981.4 7.9 fusion.55
  1011.4 203.8 %shard_map.521 = (f32[2,576,1152]{2,1,0:T(8,128)}, f32[120,1152]{1,0:T(8,128)}) custom-call(f32[8,576,1152]{2,1,0:T(8,128)} %fusion.52.chunks, f32[120,1152]{1,0:T(8,128)} %concatenate.210.beside), custom_call_target="tpu_custom_call" | custom-call | bytes 800000000 | tf_op jit(solution)/shard_map/pallas_call | solution.py:1237
  1261.8 19.8 %fusion.279 = f32[240,7424]{1,0:T(8,128)} fusion(bf16[7424,1152]{1,0:T(8,128)(2,1)} %get-tuple-element.60, bf16[120,1152]{1,0:T(8,128)(2,1)S(1)} %subtract_convert_fusion.3, bf16[120,1152]{1,0:T(8,128)(2,1)S(1)} %convert_element_type.449), kind=kOutput, calls=%fused_computation.364 | convolution fusion | flops 4106280960 | bytes 24784896 | tf_op jit(solution)/shard_map/dot_general | solution.py:111
  1320.2 302.8 %shard_map.522 = (f32[2,864,1152]{2,1,0:T(8,128)}, f32[4,464,1152]{2,1,0:T(8,128)}) custom-call(f32[8,864,1152]{2,1,0:T(8,128)} %fusion.36.chunks, f32[464,1152]{1,0:T(8,128)} %fusion.60.beside), custom_call_target="tpu_custom_call" | custom-call | bytes 800000000 | tf_op jit(solution)/shard_map/pallas_call | solution.py:1237
  1658.0 19.8 %shard_map.525 = (f32[10368,128]{1,0:T(8,128)}, f32[10368,128]{1,0:T(8,128)}, f32[10368,128]{1,0:T(8,128)}, f32[10368,128]{1,0:T(8,128)}) custom-call(s32[4,3]{1,0:T(4,128)S(1)} %fusion.351.table, f32[1]{0:T(128)} %bitcast.126.factor, f32[1152,1152]{1,0:T(8,128)} %bitcast.435, f32[10368,128]{1,0:T(8,128)} %bitcast.421, f32[10368,128]{1,0:T(8,128)} %bitcast.444, ...), custom_call_target="tpu_custom_call" | custom-call | tf_op jit(solution)/shard_map/pallas_call | solution.py:1368
  1677.8 28.3 %shard_map.524 = (f32[15552,128]{1,0:T(8,128)}, f32[15552,128]{1,0:T(8,128)}, f32[15552,128]{1,0:T(8,128)}, f32[15552,128]{1,0:T(8,128)}) custom-call(s32[6,3]{1,0:T(8,128)S(1)} %copy.134.table, f32[1]{0:T(128)} %bitcast.126.factor, f32[1728,1152]{1,0:T(8,128)} %bitcast.434, f32[15552,128]{1,0:T(8,128)} %bitcast.419, f32[15552,128]{1,0:T(8,128)} %bitcast.438, ...), custom_call_target="tpu_custom_call" | custom-call | tf_op jit(solution)/shard_map/pallas_call | solution.py:1368
  1706.1 24.7 %multiply_add_fusion.1 = (f32[2019840]{0:T(1024)}, f32[2019840]{0:T(1024)}, f32[2019840]{0:T(1024)}, f32[2019840]{0:T(1024)}) fusion(f32[2019840]{0:T(1024)} %param.58, f32[2019840]{0:T(1024)S(1)} %bitcast.418, f32[]{:T(128)} %min.7, f32[16704,128]{1,0:T(8,128)} %copy-done.2, s32[]{:T(128)S(6)} %select_n.244, f32[2019840]{0:T(1024)} %param.50, f32[2019840]{0:T(1024)} %param.54), kind=kLoop, calls=%fused_computation.33 | loop fusion | flops 36357120 | bytes 72714248 | tf_op jit(solution)/shard_map/add | solution.py:209
  (762 shorter events, 560.1 us)
Async XLA Ops:
  428.8 43.3 %collective-permute-start = (f32[48,1152]{1,0:T(8,128)}, f32[48,1152]{1,0:T(8,128)}, u32[]{:S(2)}, u32[]{:S(2)}) collective-permute-start(f32[48,1152]{1,0:T(8,128)} %fusion.445), channel_id=1, source_target_pairs={{0,1},{1,0},{2,3},{3,2},{4,5},{5,4},{6,7},{7,6},{8,9},{9,8},{10,11... | collective-permute-start | bytes 663560 | tf_op jit(solution)/shard_map/ppermute | solution.py:573
  539.9 35.5 %collective-permute-start.12 = (bf16[512,1152]{1,0:T(8,128)(2,1)}, bf16[512,1152]{1,0:T(8,128)(2,1)}, u32[]{:S(2)}, u32[]{:S(2)}) collective-permute-start(bf16[512,1152]{1,0:T(8,128)(2,1)} %bitcast.23), channel_id=1, source_target_pairs={{0,8},{1,9},{2,10},{3,11},{4,12},{5,13},{6,14},{7,15},{8,0},{9,1},... | collective-permute-start | bytes 3538952 | tf_op jit(solution)/shard_map/ppermute | solution.py:573
  572.0 381.5 %collective-permute-start.16 = (bf16[512,1152]{1,0:T(8,128)(2,1)}, bf16[512,1152]{1,0:T(8,128)(2,1)}, u32[]{:S(2)}, u32[]{:S(2)}) collective-permute-start(bf16[512,1152]{1,0:T(8,128)(2,1)} %copy-done.27), channel_id=1, source_target_pairs={{0,8},{1,9},{2,10},{3,11},{4,12},{5,13},{6,14},{7,15},{8,0},{9,1},... | collective-permute-start | bytes 3538952 | tf_op jit(solution)/shard_map/ppermute | solution.py:573
  575.4 160.8 %collective-permute-start.18 = (bf16[512,1152]{1,0:T(8,128)(2,1)}, bf16[512,1152]{1,0:T(8,128)(2,1)}, u32[]{:S(2)}, u32[]{:S(2)}) collective-permute-start(bf16[512,1152]{1,0:T(8,128)(2,1)} %bitcast.411), channel_id=1, source_target_pairs={{0,8},{1,9},{2,10},{3,11},{4,12},{5,13},{6,14},{7,15},{8,0},{9,1},... | collective-permute-start | bytes 3538952 | tf_op jit(solution)/shard_map/ppermute | solution.py:573
  692.2 83.5 %collective-permute-start.10 = (f32[120,2304]{1,0:T(8,128)}, f32[120,2304]{1,0:T(8,128)}, u32[]{:S(2)}, u32[]{:S(2)}) collective-permute-start(f32[120,2304]{1,0:T(8,128)} %pad_maximum_fusion.6), channel_id=1, source_target_pairs={{0,8},{1,9},{2,10},{3,11},{4,12},{5,13},{6,14},{7,15},{8,0},{9,1},... | collective-permute-start | bytes 3317768 | tf_op jit(solution)/shard_map/ppermute | solution.py:573
  707.4 33.6 %all-to-all-start.2 = ((bf16[1,2,256,1152]{3,1,0,2:T(2,128)(2,1)}), bf16[1,2,256,1152]{3,1,0,2:T(2,128)(2,1)}, u32[]{:S(2)}, u32[]{:S(2)}) async-start(bf16[1,2,256,1152]{3,1,0,2:T(2,128)(2,1)} %copy.125), calls=%async_computation.2 | async-start | bytes 2359296 | tf_op jit(solution)/shard_map/all_to_all | solution.py:1838
  735.6 54.0 %collective-permute-start.4 = (bf16[512,1152]{1,0:T(8,128)(2,1)}, bf16[512,1152]{1,0:T(8,128)(2,1)}, u32[]{:S(2)}, u32[]{:S(2)}) collective-permute-start(bf16[512,1152]{1,0:T(8,128)(2,1)} %bitcast.52), channel_id=1, source_target_pairs={{0,8},{1,9},{2,10},{3,11},{4,12},{5,13},{6,14},{7,15},{8,0},{9,1},... | collective-permute-start | bytes 3538952 | tf_op jit(solution)/shard_map/ppermute | solution.py:573
  736.1 49.4 %collective-permute-start.3 = (bf16[512,1152]{1,0:T(8,128)(2,1)}, bf16[512,1152]{1,0:T(8,128)(2,1)}, u32[]{:S(2)}, u32[]{:S(2)}) collective-permute-start(bf16[512,1152]{1,0:T(8,128)(2,1)} %bitcast.41), channel_id=1, source_target_pairs={{0,8},{1,9},{2,10},{3,11},{4,12},{5,13},{6,14},{7,15},{8,0},{9,1},... | collective-permute-start | bytes 3538952 | tf_op jit(solution)/shard_map/ppermute | solution.py:573
  736.2 57.3 %collective-permute-start.5 = (bf16[512,1152]{1,0:T(8,128)(2,1)}, bf16[512,1152]{1,0:T(8,128)(2,1)}, u32[]{:S(2)}, u32[]{:S(2)}) collective-permute-start(bf16[512,1152]{1,0:T(8,128)(2,1)} %bitcast.53), channel_id=1, source_target_pairs={{0,8},{1,9},{2,10},{3,11},{4,12},{5,13},{6,14},{7,15},{8,0},{9,1},... | collective-permute-start | bytes 3538952 | tf_op jit(solution)/shard_map/ppermute | solution.py:573
  769.0 108.7 %all-to-all-start.3 = ((bf16[1,8,64,3456]{3,2,0,1:T(8,128)(2,1)}), bf16[1,8,64,3456]{3,2,0,1:T(8,128)(2,1)}, u32[]{:S(2)}, u32[]{:S(2)}) async-start(bf16[1,8,64,3456]{3,2,0,1:T(8,128)(2,1)} %maximum_bitcast_fusion.8), calls=%async_computation.3 | async-start | bytes 7077888 | tf_op jit(solution)/shard_map/all_to_all | solution.py:1853
  773.8 485.2 %all-gather.2.cloned.1.call-start = ((), (), s32[]{:S(2)}) async-start(), calls=%async_computation.4 | async-start | bytes 9953280 | tf_op jit(solution)/shard_map/all_gather | solution.py:1892
  775.7 21.3 %collective-permute-start.6 = (bf16[512,1152]{1,0:T(8,128)(2,1)S(1)}, bf16[512,1152]{1,0:T(8,128)(2,1)S(1)}, u32[]{:S(2)}, u32[]{:S(2)}) collective-permute-start(bf16[512,1152]{1,0:T(8,128)(2,1)S(1)} %bitcast.461), channel_id=1, source_target_pairs={{0,8},{1,9},{2,10},{3,11},{4,12},{5,13},{6,14},{7,15},{8,0},{9,1},... | collective-permute-start | bytes 3538952 | tf_op jit(solution)/shard_map/ppermute | solution.py:573
  789.6 32.9 %collective-permute-start.27 = (bf16[512,1152]{1,0:T(8,128)(2,1)}, bf16[512,1152]{1,0:T(8,128)(2,1)}, u32[]{:S(2)}, u32[]{:S(2)}) collective-permute-start(bf16[512,1152]{1,0:T(8,128)(2,1)} %bitcast.66), channel_id=1, source_target_pairs={{0,8},{1,9},{2,10},{3,11},{4,12},{5,13},{6,14},{7,15},{8,0},{9,1},... | collective-permute-start | bytes 3538952 | tf_op jit(solution)/shard_map/ppermute | solution.py:573
  793.4 29.3 %collective-permute-start.26 = (bf16[512,1152]{1,0:T(8,128)(2,1)}, bf16[512,1152]{1,0:T(8,128)(2,1)}, u32[]{:S(2)}, u32[]{:S(2)}) collective-permute-start(bf16[512,1152]{1,0:T(8,128)(2,1)} %get-tuple-element.70), channel_id=1, source_target_pairs={{0,8},{1,9},{2,10},{3,11},{4,12},{5,13},{6,14},{7,15},{8,0},{9,1},... | collective-permute-start | bytes 3538952 | tf_op jit(solution)/shard_map/ppermute | solution.py:573
  807.6 26.3 %collective-permute-start.25 = (bf16[512,1152]{1,0:T(8,128)(2,1)S(1)}, bf16[512,1152]{1,0:T(8,128)(2,1)}, u32[]{:S(2)}, u32[]{:S(2)}) collective-permute-start(bf16[512,1152]{1,0:T(8,128)(2,1)S(1)} %copy-done.14), channel_id=1, source_target_pairs={{0,8},{1,9},{2,10},{3,11},{4,12},{5,13},{6,14},{7,15},{8,0},{9,1},... | collective-permute-start | bytes 3538952 | tf_op jit(solution)/shard_map/ppermute | solution.py:573
  809.6 24.4 %collective-permute-start.24 = (bf16[512,1152]{1,0:T(8,128)(2,1)}, bf16[512,1152]{1,0:T(8,128)(2,1)}, u32[]{:S(2)}, u32[]{:S(2)}) collective-permute-start(bf16[512,1152]{1,0:T(8,128)(2,1)} %bitcast.38), channel_id=1, source_target_pairs={{0,8},{1,9},{2,10},{3,11},{4,12},{5,13},{6,14},{7,15},{8,0},{9,1},... | collective-permute-start | bytes 3538952 | tf_op jit(solution)/shard_map/ppermute | solution.py:573
  822.6 26.4 %collective-permute-start.19 = (bf16[512,1152]{1,0:T(8,128)(2,1)S(1)}, bf16[512,1152]{1,0:T(8,128)(2,1)}, u32[]{:S(2)}, u32[]{:S(2)}) collective-permute-start(bf16[512,1152]{1,0:T(8,128)(2,1)S(1)} %copy-done.19), channel_id=1, source_target_pairs={{0,8},{1,9},{2,10},{3,11},{4,12},{5,13},{6,14},{7,15},{8,0},{9,1},... | collective-permute-start | bytes 3538952 | tf_op jit(solution)/shard_map/ppermute | solution.py:573
  822.8 31.5 %collective-permute-start.20 = (bf16[512,1152]{1,0:T(8,128)(2,1)}, bf16[512,1152]{1,0:T(8,128)(2,1)}, u32[]{:S(2)}, u32[]{:S(2)}) collective-permute-start(bf16[512,1152]{1,0:T(8,128)(2,1)} %get-tuple-element.79), channel_id=1, source_target_pairs={{0,8},{1,9},{2,10},{3,11},{4,12},{5,13},{6,14},{7,15},{8,0},{9,1},... | collective-permute-start | bytes 3538952 | tf_op jit(solution)/shard_map/ppermute | solution.py:573
  833.8 25.7 %collective-permute-start.21 = (bf16[512,1152]{1,0:T(8,128)(2,1)S(1)}, bf16[512,1152]{1,0:T(8,128)(2,1)}, u32[]{:S(2)}, u32[]{:S(2)}) collective-permute-start(bf16[512,1152]{1,0:T(8,128)(2,1)S(1)} %copy-done.17), channel_id=1, source_target_pairs={{0,8},{1,9},{2,10},{3,11},{4,12},{5,13},{6,14},{7,15},{8,0},{9,1},... | collective-permute-start | bytes 3538952 | tf_op jit(solution)/shard_map/ppermute | solution.py:573
  834.1 31.3 %collective-permute-start.11 = (f32[120,2304]{1,0:T(8,128)}, f32[120,2304]{1,0:T(8,128)}, u32[]{:S(2)}, u32[]{:S(2)}) collective-permute-start(f32[120,2304]{1,0:T(8,128)} %fusion.409), channel_id=1, source_target_pairs={{0,16},{1,17},{2,18},{3,19},{4,20},{5,21},{6,22},{7,23},{8,24},{9,... | collective-permute-start | bytes 3317768 | tf_op jit(solution)/shard_map/ppermute | solution.py:573
  849.0 132.4 %collective-permute-start.9 = (bf16[512,1152]{1,0:T(8,128)(2,1)}, bf16[512,1152]{1,0:T(8,128)(2,1)}, u32[]{:S(2)}, u32[]{:S(2)}) collective-permute-start(bf16[512,1152]{1,0:T(8,128)(2,1)} %bitcast.61), channel_id=1, source_target_pairs={{0,8},{1,9},{2,10},{3,11},{4,12},{5,13},{6,14},{7,15},{8,0},{9,1},... | collective-permute-start | bytes 3538952 | tf_op jit(solution)/shard_map/ppermute | solution.py:573
  854.3 127.1 %collective-permute-start.8 = (bf16[512,4608]{1,0:T(8,128)(2,1)}, bf16[512,4608]{1,0:T(8,128)(2,1)}, u32[]{:S(2)}, u32[]{:S(2)}) collective-permute-start(bf16[512,4608]{1,0:T(8,128)(2,1)} %bitcast.60), channel_id=1, source_target_pairs={{0,8},{1,9},{2,10},{3,11},{4,12},{5,13},{6,14},{7,15},{8,0},{9,1},... | collective-permute-start | bytes 14155784 | tf_op jit(solution)/shard_map/ppermute | solution.py:573
  905.8 34.0 %collective-permute-start.13 = (bf16[512,1152]{1,0:T(8,128)(2,1)S(1)}, bf16[512,1152]{1,0:T(8,128)(2,1)}, u32[]{:S(2)}, u32[]{:S(2)}) collective-permute-start(bf16[512,1152]{1,0:T(8,128)(2,1)S(1)} %get-tuple-element.81), channel_id=1, source_target_pairs={{0,8},{1,9},{2,10},{3,11},{4,12},{5,13},{6,14},{7,15},{8,0},{9,1},... | collective-permute-start | bytes 3538952 | tf_op jit(solution)/shard_map/ppermute | solution.py:573
  906.4 37.2 %collective-permute-start.14 = (bf16[512,1152]{1,0:T(8,128)(2,1)S(1)}, bf16[512,1152]{1,0:T(8,128)(2,1)}, u32[]{:S(2)}, u32[]{:S(2)}) collective-permute-start(bf16[512,1152]{1,0:T(8,128)(2,1)S(1)} %get-tuple-element.82), channel_id=1, source_target_pairs={{0,8},{1,9},{2,10},{3,11},{4,12},{5,13},{6,14},{7,15},{8,0},{9,1},... | collective-permute-start | bytes 3538952 | tf_op jit(solution)/shard_map/ppermute | solution.py:573
  (200 other events, 1770.3 us)
Sparse Core Ops, SparseCore 0:
  877.8 128.7 all-gather.1

commit v4 on v3

--- a/solution.py
+++ b/solution.py
@@ -1280,34 +1280,143 @@
     return shapes, stores
 
 
-def half_rows(segments, name):
-    rows = [[], []]
-    for mine in segments:
-        for label, first, count, wide in mine:
-            if label == name:
-                for core in range(2):
-                    begin = first + core * (count // 2)
-                    rows[core].extend(range(begin, begin + count // 2))
-    return np.array(rows, np.int32)
-
-
-def pick_columns(values, rows, core):
-    wanted = jnp.asarray(rows)[core]
-    chooser = (jnp.arange(values.shape[1], dtype=jnp.int32)[:, None] == wanted[None]).astype(jnp.bfloat16)
-    return matmul_low(values, chooser).astype(jnp.bfloat16)
-
-
-def both_cores(value):
-    return jnp.concatenate([value, shift(value, SWAP_CORE)], 0)
-
-
-def owner_chunk(grads, segments, owner):
-    parts = []
-    for label, first, count, wide in segments[owner]:
-        begin = sum(seg[2] // 2 for mine in segments[:owner] for seg in mine if seg[0] == label)
-        for j in range(wide):
-            parts.append(grads[label][j][begin : begin + count // 2])
-    return jnp.concatenate(parts, 0) if len(parts) > 1 else parts[0]
+GRAD_COLUMNS = 384
+
+
+def grad_plan(matrices, segments, lefts, rights):
+    squares = {}
+    for owner in range(N_OWN):
+        row = 0
+        for name, first, count, wide in segments[owner]:
+            for j in range(wide):
+                block, inner = divmod(first, D)
+                piece = (inner, count // 2, owner, row)
+                squares.setdefault((name, block, j), []).append(piece)
+                row += count // 2
+    plan = []
+    for name, rows, wide in matrices:
+        for block in range(rows // D):
+            for j in range(wide):
+                right, column = rights[name][j]
+                plan.append((lefts[name], block * D, right, column, squares[name, block, j]))
+    return plan
+
+
+def grad_kernel(plan, parts, n_left, core_ref, *refs):
+    n_in = sum(parts)
+    ins, out = refs[:n_in], refs[n_in]
+    left_buf, right_buf, made, left_sem, right_sem, out_sem = refs[n_in + 1 :]
+    core = core_ref[0]
+    place = [sum(parts[:k]) for k in range(len(parts))]
+
+    def left_copies(square, slot):
+        left, row = square[:2]
+        return [
+            pltpu.make_async_copy(
+                ins[place[left] + part].at[pl.ds(row, D)],
+                left_buf.at[slot, part, :, pl.ds(0, ins[place[left]].shape[1])],
+                left_sem.at[slot, part],
+            )
+            for part in range(parts[left])
+        ]
+
+    def right_copies(square, slot):
+        right, column = n_left + square[2], square[3]
+        return [
+            pltpu.make_async_copy(
+                ins[place[right] + part].at[:, pl.ds(column, D)],
+                right_buf.at[slot, part, pl.ds(0, ins[place[right]].shape[0])],
+                right_sem.at[slot, part],
+            )
+            for part in range(parts[right])
+        ]
+
+    def out_copies(number):
+        row, copies = 0, []
+        for k, (first, count, owner, to) in enumerate(plan[number][4]):
+            copies.append(
+                pltpu.make_async_copy(
+                    made.at[number % 2, pl.ds(row, count)],
+                    out.at[owner, pl.ds(to, count)],
+                    out_sem.at[number % 2, k],
+                )
+            )
+            row += count
+        return copies
+
+    slots = []
+    for number, square in enumerate(plan):
+        if number == 0:
+            slots.append((0, True, 0, True))
+            continue
+        left, _, right, _ = slots[-1]
+        new_left = square[:2] != plan[number - 1][:2]
+        new_right = square[2:4] != plan[number - 1][2:4]
+        slots.append((left ^ new_left, new_left, right ^ new_right, new_right))
+
+    def operands(number):
+        left, new_left, right, new_right = slots[number]
+        copies = left_copies(plan[number], left) if new_left else []
+        return copies + (right_copies(plan[number], right) if new_right else [])
+
+    for copy in operands(0):
+        copy.start()
+    for number, square in enumerate(plan):
+        for copy in operands(number):
+            copy.wait()
+        if number + 1 < len(plan):
+            for copy in operands(number + 1):
+                copy.start()
+        if number >= 2:
+            for copy in out_copies(number - 2):
+                copy.wait()
+        left, _, right, _ = slots[number]
+        depth = ins[place[square[0]]].shape[1]
+
+        def some_columns(step, carry):
+            columns = pl.ds(pl.multiple_of(step * GRAD_COLUMNS, LANES), GRAD_COLUMNS)
+            row = 0
+            for first, count, owner, to in square[4]:
+                rows = pl.ds(pl.multiple_of(first + core * count, 16), count)
+                total = 0.0
+                for part in range(parts[square[0]]):
+                    total = total + jnp.dot(
+                        left_buf[left, part, rows, :depth],
+                        right_buf[right, part, :depth, columns],
+                        preferred_element_type=jnp.float32,
+                    )
+                made[number % 2, row : row + count, columns] = total
+                row += count
+            return carry
+
+        lax.fori_loop(0, D // GRAD_COLUMNS, some_columns, 0)
+        for copy in out_copies(number):
+            copy.start()
+    for number in range(max(len(plan) - 2, 0), len(plan)):
+        for copy in out_copies(number):
+            copy.wait()
+
+
+def core_chunks(plan, core, lefts, rights, n_rows):
+    operands = list(lefts) + list(rights)
+    parts = [len(arrays) for arrays in operands]
+    tokens = max(arrays[0].shape[1] for arrays in lefts)
+    spec = pl.BlockSpec(memory_space=pl.ANY)
+    return pl.pallas_call(
+        partial(grad_kernel, plan, parts, len(lefts)),
+        in_specs=[pl.BlockSpec(memory_space=pltpu.SMEM)] + [spec] * sum(parts),
+        out_specs=spec,
+        out_shape=jax.ShapeDtypeStruct((N_OWN, n_rows // 2, D), jnp.float32),
+        scratch_shapes=[
+            pltpu.VMEM((2, 2, D, tokens), jnp.bfloat16),
+            pltpu.VMEM((2, 2, tokens, D), jnp.bfloat16),
+            pltpu.VMEM((2, D // 2, D), jnp.float32),
+            pltpu.SemaphoreType.DMA((2, 2)),
+            pltpu.SemaphoreType.DMA((2, 2)),
+            pltpu.SemaphoreType.DMA((2, N_OWN)),
+        ],
+        compiler_params=pltpu.CompilerParams(vmem_limit_bytes=36 * 1024 * 1024),
+    )(core.astype(jnp.int32).reshape(1), *[array for arrays in operands for array in arrays])
 
 
 def step_values(master, grad, first, second, average):
@@ -1534,10 +1643,6 @@
 def two_parts(product, value):
     both = product(jnp.concatenate(halves(value), 0))
     return both[: value.shape[0]] + both[value.shape[0] :]
-
-
-def grad_two_parts(left, value):
-    return weight_grad(jnp.concatenate([left, left], 0), jnp.concatenate(halves(value), 0))
 
 
 def shards_block(
@@ -1767,28 +1872,35 @@
     clip_error = jnp.sum(jnp.mean(miss * miss, -1), (1, 2))
     local_loss = jnp.sum(loss_weight * clip_error)
 
-    inputs = {}
-    for label, value in (
-        ("space_qkv", space_in),
-        ("space_out", space_flat),
-        ("time_qkv", time_in),
-        ("time_out", time_flat),
-        ("cross_q", cross_in),
-        ("cross_out", cross_flat),
-        ("fc_in", dense_in),
-    ):
-        segments = DENSE_SEGS if label == "fc_in" else ATTEND_SEGS
-        inputs[label] = pick_columns(both_cores(flat2(value)), half_rows(segments, label), core_id)
-    act_both = both_cores(flat2(dense_act))
-    half = half_rows([[("square", 0, D, 1)]], "square")
-    for block in range(MLP // D):
-        inputs["fc_out", block] = pick_columns(act_both[:, block * D : (block + 1) * D], half, core_id)
-
-    def core_grad(left, outs):
-        return [weight_grad(left, both_cores(flat2(out))) for out in outs]
-
-    def columns(value):
-        return [value[..., j * D : (j + 1) * D] for j in range(value.shape[-1] // D)]
+    def two_cores(value):
+        return [value, shift(value, SWAP_CORE)]
+
+    lefts = {
+        label: two_cores(flat2(value).T)
+        for label, value in (
+            ("space_qkv", space_in),
+            ("space_out", space_flat),
+            ("time_qkv", time_in),
+            ("time_out", time_flat),
+            ("cross_q", cross_in),
+            ("cross_out", cross_flat),
+            ("fc_in", dense_in),
+            ("fc_out", dense_act),
+        )
+    }
+
+    def chunks_of(matrices, segments, rights, n_rows):
+        arrays, where = [], {}
+        for label, blocks in rights.items():
+            where[label] = []
+            for value, column in blocks:
+                known = [k for k, other in enumerate(arrays) if other is value]
+                if not known:
+                    arrays.append(value)
+                where[label].append((known[0] if known else len(arrays) - 1, column))
+        order = {label: number for number, (label, rows, wide) in enumerate(matrices)}
+        plan = grad_plan(matrices, segments, order, where)
+        return core_chunks(plan, core_id, [lefts[label] for label in order], arrays, n_rows)
 
     grad_pred = (
         2.0 / miss.shape[-1] * (loss_weight / weight_total)[:, None, None, None] * miss
@@ -1800,40 +1912,47 @@
     grad_fmod = jnp.concatenate([grad_fshift.reshape(1, D), grad_fscale.reshape(1, D)], 0)
     grad_dense = (grad_hidden * mod_row(5)).astype(jnp.bfloat16)
     grad_gate_b = jnp.sum(grad_hidden * dense_res, (1, 2))
-    grads = {}
-    dense_both = both_cores(flat2(grad_dense))
-    g_fc_out = [weight_grad(inputs["fc_out", block], dense_both) for block in range(MLP // D)]
-    grads["fc_out"] = [jnp.concatenate(g_fc_out, 0)]
+    dense_both = two_cores(flat2(grad_dense))
     g_fc_out_b = bias_grad(grad_dense)
     unused, pullback = jax.vjp(gelu_tanh, dense_pre)
     grad_pre = pullback(back_low(grad_dense, fc_out))[0].astype(jnp.bfloat16)
-    grads["fc_in"] = core_grad(inputs["fc_in"], columns(grad_pre))
+    pre_both = two_cores(flat2(grad_pre))
+    dense_chunks = chunks_of(
+        DENSE,
+        DENSE_SEGS,
+        {"fc_in": [(pre_both, j * D) for j in range(MLP // D)], "fc_out": [(dense_both, 0)]},
+        DENSE_ROWS,
+    )
+    rights = {}
     g_fc_in_b = bias_grad(grad_pre)
     unused, pullback = jax.vjp(modulate, hidden_three, mod_row(3), mod_row(4))
     grad_input, grad_shift_b, grad_scale_b = pullback(back_low(grad_pre, fc_in))
     grad_hidden = grad_hidden + grad_input
     grad_cross = grad_hidden.astype(jnp.bfloat16)
-    grads["cross_out"] = core_grad(inputs["cross_out"], [grad_cross])
+    rights["cross_out"] = [(two_cores(flat2(grad_cross)), 0)]
     g_cross_bo = bias_grad(grad_cross)
     grad_cross_o = back_low(flat2(grad_cross), cross_out).astype(jnp.bfloat16)
     grad_cq, grad_ck, grad_cv = heads_backward(
         "cross", cross_query, cross_k, cross_v, live, cross_lse, grad_cross_o
     )
     grad_cq = grad_cq.reshape(clip_dev, frame_dev, patches, D)
-    grads["cross_q"] = core_grad(inputs["cross_q"], [grad_cq])
+    rights["cross_q"] = [(two_cores(flat2(grad_cq)), 0)]
     g_cross_bq = bias_grad(grad_cq)
     grad_hidden = grad_hidden + back_low(grad_cq, cross_q)
     grad_cv = grad_cv[:L_CAP]
     grad_ckv = jnp.concatenate([grad_ck[:L_CAP], grad_cv], -1)
     g_cross_bv = bias_grad(grad_cv)
     grad_ckv = grad_ckv + shift(grad_ckv, SWAP_CORE)
-    cap_half = pick_columns(cap_rows[0], half_rows(ATTEND_SEGS, "cross_kv"), core_id)
-    grads["cross_kv"] = [grad_two_parts(cap_half, part) for part in columns(grad_ckv)]
+    pad_rows = lambda value: jnp.pad(value, ((0, -L_CAP % LANES), (0, 0)))
+    cap_twice = pad_rows(cap_rows[0]).T
+    lefts["cross_kv"] = [jnp.concatenate([cap_twice, cap_twice], 1)]
+    ckv_parts = [jnp.concatenate([pad_rows(part) for part in halves(grad_ckv)], 0)]
+    rights["cross_kv"] = [(ckv_parts, 0), (ckv_parts, D)]
     grad_ckv = grad_ckv + shift(grad_ckv, SWAP_X)
     grad_cap_rows = two_parts(lambda part: back_low(part, cross_kv), grad_ckv)
 
     grad_time = (grad_hidden * mod_row(2)).astype(jnp.bfloat16)
-    grads["time_out"] = core_grad(inputs["time_out"], [grad_time])
+    rights["time_out"] = [(two_cores(flat2(grad_time)), 0)]
     g_time_bo = bias_grad(grad_time)
     grad_time_o = lax.all_to_all(
         back_low(grad_time, time_out).astype(jnp.bfloat16),
@@ -1847,7 +1966,7 @@
         piece.reshape(clip_dev, local_pos, frames, D)
         for piece in heads_backward(frames, time_q, time_k, time_v, live, time_lse, grad_time_o)
     ]
-    grads["time_qkv"] = core_grad(inputs["time_qkv"], grad_tqkv)
+    rights["time_qkv"] = [(two_cores(flat2(part)), 0) for part in grad_tqkv]
     g_time_bq = bias_grad(grad_tqkv[0])
     g_time_bv = bias_grad(grad_tqkv[2])
     grad_tqkv = lax.all_to_all(
@@ -1857,14 +1976,15 @@
     grad_hidden = grad_hidden + back_low(grad_tqkv, time_qkv)
     grad_gate_a = grad_gate_a + jnp.sum(grad_hidden * space_res, (1, 2))
     grad_space = (grad_hidden * mod_row(2)).astype(jnp.bfloat16)
-    grads["space_out"] = core_grad(inputs["space_out"], [grad_space])
+    rights["space_out"] = [(two_cores(flat2(grad_space)), 0)]
     g_space_bo = bias_grad(grad_space)
     grad_space_o = back_low(flat2(grad_space), space_out).astype(jnp.bfloat16)
     grad_sqkv = [
         piece.reshape(clip_dev, frame_dev, patches, D)
         for piece in heads_backward("all", space_q, space_k, space_v, live, space_lse, grad_space_o)
     ]
-    grads["space_qkv"] = core_grad(inputs["space_qkv"], grad_sqkv)
+    rights["space_qkv"] = [(two_cores(flat2(part)), 0) for part in grad_sqkv]
+    attend_chunks = chunks_of(ATTEND, ATTEND_SEGS, rights, ATTEND_ROWS)
     g_space_bq = bias_grad(grad_sqkv[0])
     g_space_bv = bias_grad(grad_sqkv[2])
     grad_sqkv = jnp.concatenate(grad_sqkv, -1)
@@ -1898,7 +2018,6 @@
 
     once = frame_id == 0
     gathered_mods = jnp.where(own_clip[:, None, None], grad_mods[None], 0.0)
-    zero_d = jnp.zeros((D,), jnp.float32)
     ends = jnp.concatenate([g_final_b, local_loss.reshape(1)])
     vector_rows = [
         g_patch_b,
@@ -1922,7 +2041,7 @@
     spare = -sum(value.shape[0] for value in small) % 8
     small = jnp.concatenate(small + [jnp.zeros((spare, D), jnp.float32)] * (spare > 0), 0)
     dense_grad, small = collect_shard(
-        jnp.stack([owner_chunk(grads, DENSE_SEGS, owner) for owner in range(N_OWN)]),
+        dense_chunks,
         144,
         3,
         small=small,
@@ -2013,7 +2132,7 @@
     emb_grad = jnp.where((unit >= 0) & (unit < EMB_UNITS), emb_grad, 0.0)
 
     attend_grad, emb_whole = collect_shard(
-        jnp.stack([owner_chunk(grads, ATTEND_SEGS, owner) for owner in range(N_OWN)]),
+        attend_chunks,
         176,
         4,
         part=emb_grad,

time: 1750 us -> 1680 us (0.960)
  matrix products: 308 us -> 211 us
  Pallas kernels: 984 us -> 1040 us
    dot_general x25 -> x5, matrix products: 114 us -> 21 us  [weight_grad(): lax.dot_general(left, right, (((0,), (0,)), ((), ())), preferred_element_...]
    pallas_call x0 -> x2, Pallas kernels: none -> 58.2 us  [core_chunks(): pl.pallas_call(partial(grad_kernel, plan, parts, len(lefts)), in_specs=[p...]
    slice x36 -> x0, local copies, waits for them, and re-layouts: 20.6 us -> none  [the longest x34 14.6 us: owner_chunk(): parts.append(grads[label][j][begin:begin + count // 2])]
    unnamed x16 -> x3, other arithmetic: 20.9 us -> 0.6 us
    dot_general x21 -> x17, matrix products: 99.3 us -> 86.9 us  [matmul_low(): lax.dot_general(left, right, (((left.ndim - 1,), (0,)), ((), ())), prefer...]
    ppermute x37 -> x34, waiting for transfers between devices: 36.1 us -> 25.2 us  [shift(): return lax.ppermute(value, AXES, perm)]
    ppermute x37 -> x34, starting transfers between devices: 34.5 us -> 42.4 us  [shift(): return lax.ppermute(value, AXES, perm)]
    unnamed x347 -> x365, local copies, waits for them, and re-layouts: 59.3 us -> 58.6 us
  transfers between devices with their start and end apart: 42 -> 39, of which waited for: 11 -> 11; matrix products, arithmetic and copies ran while one was open for 24% -> 12% of each run, Pallas kernels for 15% -> 17%
where the time goes in v4:
time: 1680 us; the launch traced here: 1670 us
  Pallas kernels  1040 us (62%)
  matrix products  211 us (13%)
  local copies, waits for them, and re-layouts  169 us (10%)
  other arithmetic  117 us (7%)
  starting transfers between devices  60.1 us (4%)
  waiting for transfers between devices  43.7 us (3%)
  between operations  31.5 us (2%)
    pallas_call x2, Pallas kernels, collect_shard(): pl.pallas_call(kernel, in_specs=[spec] * 2, out_specs=[spec] * 2, out_sha...  504 us
    pallas_call x2, Pallas kernels, spread_shards(): pl.pallas_call(partial(spread_kernel, groups, modes), in_specs=[spec] * (...  367 us
    dot_general x14, matrix products, back_low(): lax.dot_general(grads, weight, (((grads.ndim - 1,), (1,)), ((), ())), pre...  98.7 us
    dot_general x17, matrix products, matmul_low(): lax.dot_general(left, right, (((left.ndim - 1,), (0,)), ((), ())), prefer...  86.9 us
    unnamed x365, local copies, waits for them, and re-layouts  58.6 us
    pallas_call x2, Pallas kernels, core_chunks(): pl.pallas_call(partial(grad_kernel, plan, parts, len(lefts)), in_specs=[p...  58.2 us
    pallas_call x2, Pallas kernels, step_shard(): pl.pallas_call(partial(step_kernel, widths), grid_spec=pltpu.PrefetchScal...  48.1 us
    ppermute x34, starting transfers between devices, shift(): return lax.ppermute(value, AXES, perm)  42.4 us
  transfers between devices with their start and end apart: 39, of which 11 were waited for; matrix products, arithmetic and copies ran while one was open for 12% of the time, Pallas kernels for 17%

profile of v4, /device:TPU:0, one launch (start us, length us, event | category | flops | bytes accessed | tf_op | source)
XLA Modules:
  0.0 1670.4 jit_solution(16747774534457138703)
XLA Ops:
  20.3 207.8 %shard_map.431 = (bf16[7424,1152]{1,0:T(8,128)(2,1)}, bf16[1152,4608]{1,0:T(8,128)(2,1)}, bf16[4608,1152]{1,0:T(8,128)(2,1)}, f32[8,8,128]{2,1,0:T(8,128)S(1)}) custom-call(bf16[4,464,1152]{2,1,0:T(8,128)(2,1)} %bitcast.343, bf16[6,192,1152]{2,1,0:T(8,128)(2,1)S(1)} %bitcast.355, f32[8,128]{1,0:T(8,128)S(1)} %broadcast_in_dim.120.refs_2_), custom_call_target="tpu_custom_call" | custom-call | bytes 200000000 | tf_op jit(solution)/shard_map/pallas_call | solution.py:938
  237.0 9.5 multiply_convert_fusion.4
  264.3 158.8 %shard_map.433 = (bf16[1152,3456]{1,0:T(8,128)(2,1)}, bf16[1152,1152]{1,0:T(8,128)(2,1)}, bf16[1152,3456]{1,0:T(8,128)(2,1)}, bf16[1152,1152]{1,0:T(8,128)(2,1)}...) custom-call(bf16[6,288,1152]{2,1,0:T(8,128)(2,1)} %bitcast.354, ...), custom_call_target="tpu_custom_call" | custom-call | bytes 200000000 | tf_op jit(solution)/shard_map/pallas_call | solution.py:938
  452.3 15.4 collective-permute-start.1
  476.1 10.3 collective-permute-done.2
  592.1 14.5 multiply_convert_fusion
  606.7 13.7 fusion.217
  626.3 17.9 %convert_reduce_fusion = (f32[4608]{0:T(1024)}, bf16[2,256,4608]{2,1,0:T(8,128)(2,1)}) fusion(f32[2,256,4608]{2,1,0:T(8,128)} %get-tuple-element.220, f32[4608]{0:T(1024)S(1)} %copy-done.142, bf16[2,256,1152]{2,1,0:T(8,128)(2,1)S(1)} %get-tuple-element.133, bf16[4608,1152]{1,0:T(8,128)(2,1)} %get-tuple-element.73), kind=kOutput, calls=%fused_computation.20 | convolution fusion | flops 5490077184 | bytes 25989120 | tf_op jit(solution)/shard_map/dot_general | solution.py:111
  644.2 13.4 multiply_reduce_fusion.6
  666.3 12.7 shard_map.438
  701.1 9.9 all-to-all-done.2
  720.1 13.7 shard_map.439
  803.8 10.0 convert_reduce_fusion.7
  818.6 14.1 shard_map.440
  835.8 10.1 multiply_reduce_fusion.3
  868.5 9.0 concatenate.90.beside
  886.2 34.1 %shard_map.442.chunks = f32[8,864,1152]{2,1,0:T(8,128)} custom-call(s32[1]{0:T(128)} %bitcast.core_ref, bf16[1152,512]{1,0:T(8,128)(2,1)} %bitcast.89.refs_0_, bf16[1152,512]{1,0:T(8,128)(2,1)} %collective-permute-done.9.refs_1_, bf16[1152,512]{1,0:T(8,128)(2,1)} %bitcast.90.refs_2_, bf16[1152,512]{1,0:T(8,128)(2,1)} %collective-permute-done.10.refs_3_, ...), custom_call_target="tpu_custom_call" | custom-call | tf_op jit(solution)/shard_map/pallas_call | solution.py:1405
  920.3 24.1 %shard_map.437.chunks = f32[8,576,1152]{2,1,0:T(8,128)} custom-call(s32[1]{0:T(128)} %bitcast.core_ref, bf16[1152,512]{1,0:T(8,128)(2,1)S(1)} %bitcast.362, bf16[1152,512]{1,0:T(8,128)(2,1)} %collective-permute-done.3.refs_1_, bf16[4608,512]{1,0:T(8,128)(2,1)} %bitcast.46.refs_2_, bf16[4608,512]{1,0:T(8,128)(2,1)} %collective-permute-done.4.refs_3_, ...), custom_call_target="tpu_custom_call" | custom-call | tf_op jit(solution)/shard_map/pallas_call | solution.py:1405
  944.4 202.5 %shard_map.441 = (f32[2,576,1152]{2,1,0:T(8,128)}, f32[120,1152]{1,0:T(8,128)}) custom-call(f32[8,576,1152]{2,1,0:T(8,128)} %shard_map.437.chunks, f32[120,1152]{1,0:T(8,128)} %concatenate.90.beside), custom_call_target="tpu_custom_call" | custom-call | bytes 800000000 | tf_op jit(solution)/shard_map/pallas_call | solution.py:1237
  1193.7 20.0 %fusion.104 = f32[240,7424]{1,0:T(8,128)} fusion(bf16[7424,1152]{1,0:T(8,128)(2,1)} %get-tuple-element.60, bf16[120,1152]{1,0:T(8,128)(2,1)S(1)} %subtract_convert_fusion.4, bf16[120,1152]{1,0:T(8,128)(2,1)S(1)} %convert_element_type.378), kind=kOutput, calls=%fused_computation.201 | convolution fusion | flops 4106280960 | bytes 24784896 | tf_op jit(solution)/shard_map/dot_general | solution.py:111
  1252.3 301.4 %shard_map.443 = (f32[2,864,1152]{2,1,0:T(8,128)}, f32[4,464,1152]{2,1,0:T(8,128)}) custom-call(f32[8,864,1152]{2,1,0:T(8,128)} %shard_map.442.chunks, f32[464,1152]{1,0:T(8,128)} %fusion.48.beside), custom_call_target="tpu_custom_call" | custom-call | bytes 800000000 | tf_op jit(solution)/shard_map/pallas_call | solution.py:1237
  1589.4 19.8 %shard_map.446 = (f32[10368,128]{1,0:T(8,128)}, f32[10368,128]{1,0:T(8,128)}, f32[10368,128]{1,0:T(8,128)}, f32[10368,128]{1,0:T(8,128)}) custom-call(s32[4,3]{1,0:T(4,128)S(1)} %fusion.172.table, f32[1]{0:T(128)} %bitcast.116.factor, f32[1152,1152]{1,0:T(8,128)} %bitcast.378, f32[10368,128]{1,0:T(8,128)} %bitcast.352, f32[10368,128]{1,0:T(8,128)} %bitcast.387, ...), custom_call_target="tpu_custom_call" | custom-call | tf_op jit(solution)/shard_map/pallas_call | solution.py:1477
  1609.2 28.3 %shard_map.445 = (f32[15552,128]{1,0:T(8,128)}, f32[15552,128]{1,0:T(8,128)}, f32[15552,128]{1,0:T(8,128)}, f32[15552,128]{1,0:T(8,128)}) custom-call(s32[6,3]{1,0:T(8,128)S(1)} %copy.204.table, f32[1]{0:T(128)} %bitcast.116.factor, f32[1728,1152]{1,0:T(8,128)} %bitcast.377, f32[15552,128]{1,0:T(8,128)} %bitcast.350, f32[15552,128]{1,0:T(8,128)} %bitcast.383, ...), custom_call_target="tpu_custom_call" | custom-call | tf_op jit(solution)/shard_map/pallas_call | solution.py:1477
  1637.5 24.7 %multiply_add_fusion.1 = (f32[2019840]{0:T(1024)}, f32[2019840]{0:T(1024)}, f32[2019840]{0:T(1024)}, f32[2019840]{0:T(1024)}) fusion(f32[2019840]{0:T(1024)} %param.49, f32[2019840]{0:T(1024)S(1)} %bitcast.349, f32[]{:T(128)} %min.7, f32[16704,128]{1,0:T(8,128)} %copy-done.2, s32[]{:T(128)S(6)} %select_n.229, f32[2019840]{0:T(1024)} %param.41, f32[2019840]{0:T(1024)} %param.45), kind=kLoop, calls=%fused_computation.27 | loop fusion | flops 36357120 | bytes 72714248 | tf_op jit(solution)/shard_map/add | solution.py:209
  (707 shorter events, 443.0 us)
Async XLA Ops:
  429.8 20.2 %collective-permute-start = (f32[48,1152]{1,0:T(8,128)}, f32[48,1152]{1,0:T(8,128)}, u32[]{:S(2)}, u32[]{:S(2)}) collective-permute-start(f32[48,1152]{1,0:T(8,128)} %fusion.226), channel_id=1, source_target_pairs={{0,1},{1,0},{2,3},{3,2},{4,5},{5,4},{6,7},{7,6},{8,9},{9,8},{10,11... | collective-permute-start | bytes 663560 | tf_op jit(solution)/shard_map/ppermute | solution.py:573
  452.3 21.0 %collective-permute-start.1 = (f32[48,1152]{1,0:T(8,128)}, f32[48,1152]{1,0:T(8,128)}, u32[]{:S(2)}, u32[]{:S(2)}) collective-permute-start(f32[48,1152]{1,0:T(8,128)} %add.742), channel_id=1, source_target_pairs={{0,2},{1,3},{2,0},{3,1},{4,6},{5,7},{6,4},{7,5},{8,10},{9,11},{10,... | collective-permute-start | bytes 663560 | tf_op jit(solution)/shard_map/ppermute | solution.py:573
  511.9 19.6 %all-to-all-start = ((bf16[1,2,256,1152]{3,1,0,2:T(2,128)(2,1)}), bf16[1,2,256,1152]{3,1,0,2:T(2,128)(2,1)S(1)}, u32[]{:S(2)}, u32[]{:S(2)}) async-start(bf16[1,2,256,1152]{3,1,0,2:T(2,128)(2,1)} %copy.177), calls=%async_computation | async-start | bytes 2359296 | tf_op jit(solution)/shard_map/all_to_all | solution.py:1842
  547.9 25.9 %all-to-all-start.1 = ((bf16[1,8,64,1152]{3,2,0,1:T(8,128)(2,1)}), bf16[1,8,64,1152]{3,2,0,1:T(8,128)(2,1)}, u32[]{:S(2)}, u32[]{:S(2)}) async-start(bf16[1,8,64,1152]{3,2,0,1:T(8,128)(2,1)} %bitcast.395), calls=%async_computation.1 | async-start | bytes 2359296 | tf_op jit(solution)/shard_map/all_to_all | solution.py:1850
  690.4 20.7 %all-to-all-start.2 = ((bf16[1,2,256,1152]{3,1,0,2:T(2,128)(2,1)}), bf16[1,2,256,1152]{3,1,0,2:T(2,128)(2,1)}, u32[]{:S(2)}, u32[]{:S(2)}) async-start(bf16[1,2,256,1152]{3,1,0,2:T(2,128)(2,1)} %copy.190), calls=%async_computation.2 | async-start | bytes 2359296 | tf_op jit(solution)/shard_map/all_to_all | solution.py:1957
  697.6 45.1 %collective-permute-start.8 = (f32[120,2304]{1,0:T(8,128)}, f32[120,2304]{1,0:T(8,128)}, u32[]{:S(2)}, u32[]{:S(2)}) collective-permute-start(f32[120,2304]{1,0:T(8,128)} %get-tuple-element.129), channel_id=1, source_target_pairs={{0,16},{1,17},{2,18},{3,19},{4,20},{5,21},{6,22},{7,23},{8,24},{9,... | collective-permute-start | bytes 3317768 | tf_op jit(solution)/shard_map/ppermute | solution.py:573
  737.7 62.3 %all-to-all-start.3 = ((bf16[1,8,64,3456]{3,2,0,1:T(8,128)(2,1)}), bf16[1,8,64,3456]{3,2,0,1:T(8,128)(2,1)}, u32[]{:S(2)}, u32[]{:S(2)}) async-start(bf16[1,8,64,3456]{3,2,0,1:T(8,128)(2,1)} %maximum_bitcast_fusion), calls=%async_computation.3 | async-start | bytes 7077888 | tf_op jit(solution)/shard_map/all_to_all | solution.py:1972
  742.5 448.5 %all-gather.2.cloned.1.call-start = ((), (), s32[]{:S(2)}) async-start(), calls=%async_computation.4 | async-start | bytes 9953280 | tf_op jit(solution)/shard_map/all_gather | solution.py:2012
  763.3 35.4 %collective-permute-start.10 = (bf16[1152,512]{1,0:T(8,128)(2,1)}, bf16[1152,512]{1,0:T(8,128)(2,1)}, u32[]{:S(2)}, u32[]{:S(2)}) collective-permute-start(bf16[1152,512]{1,0:T(8,128)(2,1)} %bitcast.90.refs_2_), channel_id=1, source_target_pairs={{0,8},{1,9},{2,10},{3,11},{4,12},{5,13},{6,14},{7,15},{8,0},{9,1},... | collective-permute-start | bytes 3538952 | tf_op jit(solution)/shard_map/ppermute | solution.py:573
  763.7 38.7 %collective-permute-start.9 = (bf16[1152,512]{1,0:T(8,128)(2,1)}, bf16[1152,512]{1,0:T(8,128)(2,1)}, u32[]{:S(2)}, u32[]{:S(2)}) collective-permute-start(bf16[1152,512]{1,0:T(8,128)(2,1)} %bitcast.89.refs_0_), channel_id=1, source_target_pairs={{0,8},{1,9},{2,10},{3,11},{4,12},{5,13},{6,14},{7,15},{8,0},{9,1},... | collective-permute-start | bytes 3538952 | tf_op jit(solution)/shard_map/ppermute | solution.py:573
  765.9 37.1 %collective-permute-start.11 = (bf16[1152,512]{1,0:T(8,128)(2,1)}, bf16[1152,512]{1,0:T(8,128)(2,1)}, u32[]{:S(2)}, u32[]{:S(2)}) collective-permute-start(bf16[1152,512]{1,0:T(8,128)(2,1)} %bitcast.91.refs_4_), channel_id=1, source_target_pairs={{0,8},{1,9},{2,10},{3,11},{4,12},{5,13},{6,14},{7,15},{8,0},{9,1},... | collective-permute-start | bytes 3538952 | tf_op jit(solution)/shard_map/ppermute | solution.py:573
  766.3 47.5 %collective-permute-start.16 = (bf16[512,1152]{1,0:T(8,128)(2,1)S(1)}, bf16[512,1152]{1,0:T(8,128)(2,1)}, u32[]{:S(2)}, u32[]{:S(2)}) collective-permute-start(bf16[512,1152]{1,0:T(8,128)(2,1)S(1)} %copy-done.14), channel_id=1, source_target_pairs={{0,8},{1,9},{2,10},{3,11},{4,12},{5,13},{6,14},{7,15},{8,0},{9,1},... | collective-permute-start | bytes 3538952 | tf_op jit(solution)/shard_map/ppermute | solution.py:573
  769.0 34.1 %collective-permute-start.17 = (bf16[512,1152]{1,0:T(8,128)(2,1)}, bf16[512,1152]{1,0:T(8,128)(2,1)}, u32[]{:S(2)}, u32[]{:S(2)}) collective-permute-start(bf16[512,1152]{1,0:T(8,128)(2,1)} %bitcast.401), channel_id=1, source_target_pairs={{0,8},{1,9},{2,10},{3,11},{4,12},{5,13},{6,14},{7,15},{8,0},{9,1},... | collective-permute-start | bytes 3538952 | tf_op jit(solution)/shard_map/ppermute | solution.py:573
  798.7 15.6 collective-permute-start.15
  802.4 30.3 %collective-permute-start.14 = (bf16[1152,512]{1,0:T(8,128)(2,1)S(1)}, bf16[1152,512]{1,0:T(8,128)(2,1)S(1)}, u32[]{:S(2)}, u32[]{:S(2)}) collective-permute-start(bf16[1152,512]{1,0:T(8,128)(2,1)S(1)} %bitcast.365), channel_id=1, source_target_pairs={{0,8},{1,9},{2,10},{3,11},{4,12},{5,13},{6,14},{7,15},{8,0},{9,1},... | collective-permute-start | bytes 3538952 | tf_op jit(solution)/shard_map/ppermute | solution.py:573
  802.9 31.3 %collective-permute-start.13 = (bf16[1152,512]{1,0:T(8,128)(2,1)S(1)}, bf16[1152,512]{1,0:T(8,128)(2,1)S(1)}, u32[]{:S(2)}, u32[]{:S(2)}) collective-permute-start(bf16[1152,512]{1,0:T(8,128)(2,1)S(1)} %bitcast.367), channel_id=1, source_target_pairs={{0,8},{1,9},{2,10},{3,11},{4,12},{5,13},{6,14},{7,15},{8,0},{9,1},... | collective-permute-start | bytes 3538952 | tf_op jit(solution)/shard_map/ppermute | solution.py:573
  803.1 32.6 %collective-permute-start.12 = (bf16[1152,512]{1,0:T(8,128)(2,1)S(1)}, bf16[1152,512]{1,0:T(8,128)(2,1)S(1)}, u32[]{:S(2)}, u32[]{:S(2)}) collective-permute-start(bf16[1152,512]{1,0:T(8,128)(2,1)S(1)} %bitcast.369), channel_id=1, source_target_pairs={{0,8},{1,9},{2,10},{3,11},{4,12},{5,13},{6,14},{7,15},{8,0},{9,1},... | collective-permute-start | bytes 3538952 | tf_op jit(solution)/shard_map/ppermute | solution.py:573
  813.8 106.5 %collective-permute-start.5 = (bf16[512,4608]{1,0:T(8,128)(2,1)}, bf16[512,4608]{1,0:T(8,128)(2,1)}, u32[]{:S(2)}, u32[]{:S(2)}) collective-permute-start(bf16[512,4608]{1,0:T(8,128)(2,1)} %bitcast.55.refs_4_), channel_id=1, source_target_pairs={{0,8},{1,9},{2,10},{3,11},{4,12},{5,13},{6,14},{7,15},{8,0},{9,1},... | collective-permute-start | bytes 14155784 | tf_op jit(solution)/shard_map/ppermute | solution.py:573
  814.3 106.0 %collective-permute-start.4 = (bf16[4608,512]{1,0:T(8,128)(2,1)}, bf16[4608,512]{1,0:T(8,128)(2,1)}, u32[]{:S(2)}, u32[]{:S(2)}) collective-permute-start(bf16[4608,512]{1,0:T(8,128)(2,1)} %bitcast.46.refs_2_), channel_id=1, source_target_pairs={{0,8},{1,9},{2,10},{3,11},{4,12},{5,13},{6,14},{7,15},{8,0},{9,1},... | collective-permute-start | bytes 14155784 | tf_op jit(solution)/shard_map/ppermute | solution.py:573
  833.8 15.1 collective-permute-start.18
  835.7 13.9 collective-permute-start.20
  854.5 65.7 %collective-permute-start.6 = (bf16[512,1152]{1,0:T(8,128)(2,1)S(1)}, bf16[512,1152]{1,0:T(8,128)(2,1)}, u32[]{:S(2)}, u32[]{:S(2)}) collective-permute-start(bf16[512,1152]{1,0:T(8,128)(2,1)S(1)} %bitcast.359), channel_id=1, source_target_pairs={{0,8},{1,9},{2,10},{3,11},{4,12},{5,13},{6,14},{7,15},{8,0},{9,1},... | collective-permute-start | bytes 3538952 | tf_op jit(solution)/shard_map/ppermute | solution.py:573
  855.7 64.6 %collective-permute-start.3 = (bf16[1152,512]{1,0:T(8,128)(2,1)S(1)}, bf16[1152,512]{1,0:T(8,128)(2,1)}, u32[]{:S(2)}, u32[]{:S(2)}) collective-permute-start(bf16[1152,512]{1,0:T(8,128)(2,1)S(1)} %bitcast.361), channel_id=1, source_target_pairs={{0,8},{1,9},{2,10},{3,11},{4,12},{5,13},{6,14},{7,15},{8,0},{9,1},... | collective-permute-start | bytes 3538952 | tf_op jit(solution)/shard_map/ppermute | solution.py:573
  856.2 21.3 %collective-permute-start.21 = (bf16[512,1152]{1,0:T(8,128)(2,1)}, bf16[512,1152]{1,0:T(8,128)(2,1)}, u32[]{:S(2)}, u32[]{:S(2)}) collective-permute-start(bf16[512,1152]{1,0:T(8,128)(2,1)} %bitcast.73.refs_26_), channel_id=1, source_target_pairs={{0,8},{1,9},{2,10},{3,11},{4,12},{5,13},{6,14},{7,15},{8,0},{9,1},... | collective-permute-start | bytes 3538952 | tf_op jit(solution)/shard_map/ppermute | solution.py:573
  (193 other events, 1725.3 us)
Sparse Core Ops, SparseCore 0:
  757.6 130.0 all-gather.1

commit v5 on v4

--- a/solution.py
+++ b/solution.py
@@ -539,7 +539,7 @@
 AXES = ("frame", "clip")
 LANES = 128
 LANE_TILES = D // LANES
-EMB_PAD = 1856
+EMB_PAD = 1824
 
 
 X_SIZE, CORES, Z_SIZE, Y_SIZE = 2, 2, 4, 2
@@ -700,12 +700,12 @@
 
 
 def flat_to_rows(flat, rows, shift, dtype):
-    block = rows // 4
+    block = rows // 6
     return pl.pallas_call(
         rows_kernel,
         grid_spec=pltpu.PrefetchScalarGridSpec(
             num_scalar_prefetch=1,
-            grid=(4,),
+            grid=(6,),
             in_specs=[pl.BlockSpec(memory_space=pl.ANY)],
             out_specs=pl.BlockSpec((block, D), lambda b, t: (b, 0)),
             scratch_shapes=[
@@ -725,10 +725,10 @@
 
 
 def rows_to_flat(rows):
-    block = rows.shape[0] // 4
+    block = rows.shape[0] // 6
     return pl.pallas_call(
         flat_kernel,
-        grid=(4,),
+        grid=(6,),
         in_specs=[pl.BlockSpec((block, D), lambda b: (b, 0))],
         out_specs=pl.BlockSpec((block * LANE_TILES, LANES), lambda b: (b, 0)),
         out_shape=jax.ShapeDtypeStruct((rows.shape[0] * LANE_TILES, LANES), rows.dtype),
@@ -785,24 +785,37 @@
     def block_of(group, kinds, kind):
         return kinds[kind] + (2 if groups[group][3] and kind % 3 else 0)
 
+    z, y = clip // Y_SIZE, clip % Y_SIZE
+    below, above = {"clip": clip - Y_SIZE}, {"clip": clip + Y_SIZE}
+    across = {"clip": clip + 1 - 2 * y}
+    rings = [group for group in range(n) if len(groups[group][0]) == N_OWN]
+    falls = [group for group in range(n) if group not in rings]
+    first_z = Z_SIZE - 2
+
     def held_at(group, slot):
-        return helds[group].at[owners[slot] - min(groups[group][0])]
-
-    def where_kept(group, slot, action):
-        keep = groups[group][0]
-        if len(keep) == N_OWN:
-            action()
+        if group in rings:
+            return helds[group].at[owners[slot]]
+        return helds[group].at[slot % 2 * Y_SIZE + (y if slot < 2 else 1 - y)]
+
+    def is_own(slot):
+        return z == first_z + slot
+
+    def load(group):
+        to = held_at(group, 0) if group in rings else helds[group].at[(z - first_z) * Y_SIZE + y]
+        return pltpu.make_async_copy(owns[group], to, load_sem.at[group])
+
+    def loading(group, action):
+        if group in rings:
+            action(load(group))
         else:
-            pl.when(owners[slot] >= min(keep))(action)
-
-    def load(group):
-        return pltpu.make_async_copy(owns[group], held_at(group, 0), load_sem.at[group])
-
-    def copy_of(group, slot, block, device, to_slot, kind):
+            pl.when(z >= first_z)(lambda: action(load(group)))
+
+    def copy_of(group, slot, block, device, to_slot, kind, sender=None):
+        row, column = (to_slot, kind) if sender is None else sender
         return pltpu.make_async_remote_copy(
             src_ref=held_at(group, slot).at[block],
             dst_ref=held_at(group, slot).at[block],
-            send_sem=send_sem.at[group, to_slot, kind],
+            send_sem=send_sem.at[group, row, column],
             recv_sem=recv_sem.at[group, to_slot, kind],
             device_id=device,
             device_id_type=pl.DeviceIdType.MESH,
@@ -814,14 +827,14 @@
         if from_kind == 0 and not groups[group][3]:
             return
         args = (group, slot, block_of(group, mine, from_kind), device, to_slot, kind)
-        where_kept(group, slot, lambda: copy_of(*args).start())
+        copy_of(*args).start()
         sent.append(args)
 
     def arrive(group, slot, kind):
         if kind % 3 == 0 and not groups[group][3]:
             return
         block = block_of(group, landing, kind)
-        where_kept(group, slot, lambda: copy_of(group, slot, block, other, slot, kind).wait_recv())
+        copy_of(group, slot, block, other, slot, kind).wait_recv()
 
     def onward(group, slot, kind):
         if slot < half:
@@ -856,14 +869,69 @@
             else:
                 pl.when(clip == (k if arriving else 0))(lambda: action(k))
 
+    fallen = []
+
+    def run(chosen, action):
+        action() if chosen is None else pl.when(chosen)(action)
+
+    def fall(group, slot, kind, device, to_slot, to_kind, sender, chosen):
+        args = (group, slot, block_of(group, mine, kind), device, to_slot, to_kind, sender)
+        run(chosen, lambda: copy_of(*args).start())
+        fallen.append((args, chosen))
+
+    def fall_on(group, slot, kind, chosen):
+        going_down = (z >= 1) & (z <= first_z + slot) & chosen
+        fall(group, slot, kind, below, slot, kind, (slot, kind), going_down)
+        if slot == 0:
+            fall(group, slot, kind, above, slot, kind, (4, 3 + kind), is_own(slot) & chosen)
+        fall(group, slot, kind, across, slot + 2, kind, (4 + slot, kind), chosen)
+
+    def fall_beside(group, slot, kind, chosen):
+        if kind == 1:
+            fall(group, slot, 1, over_x, slot, 2, (slot, 2), chosen)
+        fall(group, slot, kind, other, slot, 3 + kind, (slot, 3 + kind), chosen)
+
+    def fall_arrive(group, slot, kind, chosen):
+        run(chosen, lambda: arrive(group, slot, kind))
+
+    def not_own(slot):
+        return None if slot >= 2 else z != first_z + slot
+
+    def fall_start():
+        for group in falls:
+            for slot in (1, 0):
+                for kind in (1, 0):
+                    fall_on(group, slot, kind, is_own(slot))
+
+    def fall_phase(phase):
+        turns = {
+            1: [(0, (z > 0) & not_own(0))],
+            2: [(0, z == 0), (1, (z > 0) & not_own(1))],
+            3: [(1, z == 0), (2, None)],
+            4: [(3, None)],
+        }[phase]
+        for group in falls:
+            for slot, chosen in turns:
+                for kind in (1, 0):
+                    fall_arrive(group, slot, kind, chosen)
+                    if slot < 2:
+                        fall_on(group, slot, kind, chosen)
+                    fall_beside(group, slot, kind, chosen)
+            if phase == half:
+                for slot in range(4):
+                    fall_arrive(group, slot, 2, not_own(slot))
+                    fall_beside(group, slot, 2, not_own(slot))
+
     for group in range(n):
-        where_kept(group, 0, lambda: load(group).start())
+        loading(group, lambda copy: copy.start())
     for item in range(m):
         peer_load(item).start()
     everyone = tuple({"clip": (clip + k) % N_OWN} for k in range(1, N_OWN)) if m else ()
-    greet((right, left, over_x, other) + everyone)
+    greet((right, left, over_x, other) + everyone + ((across,) if falls else ()))
     for group in range(n):
-        where_kept(group, 0, lambda: load(group).wait())
+        loading(group, lambda copy: copy.wait())
+    fall_start()
+    for group in rings:
         onward(group, 0, 1)
         onward(group, 0, 0)
     for item in range(m):
@@ -873,7 +941,7 @@
     waiting = []
     for step in range(1, half + 1):
         slots = [step] + ([half + step] if step < half else [])
-        pairs_now = [(group, slot) for group in range(n) for slot in slots]
+        pairs_now = [(group, slot) for group in rings for slot in slots]
         for group, slot in pairs_now:
             arrive(group, slot, 1)
             onward(group, slot, 1)
@@ -885,14 +953,19 @@
         for group, slot in waiting:
             arrive(group, slot, 2)
             send(group, slot, 2, other, slot, 5)
+        fall_phase(step)
         waiting = pairs_now
     for group, slot in waiting:
         arrive(group, slot, 2)
         send(group, slot, 2, other, slot, 5)
-    for group in range(n):
+    for group in rings:
         for slot in range(1, N_OWN):
             for kind in (3, 4, 5):
                 arrive(group, slot, kind)
+    for group in falls:
+        for slot in range(4):
+            for kind in (3, 4, 5):
+                fall_arrive(group, slot, kind, not_own(slot))
     done, base = [], 0
     for group, (keep, shapes, stores, common) in enumerate(groups):
         held = helds[group]
@@ -919,7 +992,9 @@
     for item in range(m):
         peers(item, False, lambda k: peer_copy(item, k).wait_send())
     for args in sent:
-        where_kept(args[0], args[1], lambda: copy_of(*args).wait_send())
+        copy_of(*args).wait_send()
+    for args, chosen in fallen:
+        run(chosen, lambda: copy_of(*args).wait_send())
     for copy in done:
         copy.wait()
 
@@ -1696,7 +1771,7 @@
     facts = jnp.broadcast_to(jnp.pad(facts, (0, LANES - 3))[None], (8, LANES))
     cap_weights, fc_in, fc_out, facts = spread_shards(
         [emb_rows, dense_cast],
-        [(cap_owners,) + cap_plan + (False,), (range(N_OWN),) + matrix_plan(DENSE, DENSE_SEGS) + (True,)],
+        [(cap_owners,) + cap_plan + (True,), (range(N_OWN),) + matrix_plan(DENSE, DENSE_SEGS) + (True,)],
         2,
         given=[(facts, "gather")],
     )
@@ -2042,7 +2117,7 @@
     small = jnp.concatenate(small + [jnp.zeros((spare, D), jnp.float32)] * (spare > 0), 0)
     dense_grad, small = collect_shard(
         dense_chunks,
-        144,
+        160,
         3,
         small=small,
     )
@@ -2133,7 +2208,7 @@
 
     attend_grad, emb_whole = collect_shard(
         attend_chunks,
-        176,
+        208,
         4,
         part=emb_grad,
     )

time: 1680 us -> 1650 us (0.982)
  Pallas kernels: 1040 us -> 1010 us
    pallas_call x2, Pallas kernels: 504 us -> 485 us  [collect_shard(): pl.pallas_call(kernel, in_specs=[spec] * 2, out_specs=[spec] * 2, out_sha...]
where the time goes in v5:
time: 1650 us; the launch traced here: 1640 us
  Pallas kernels  1010 us (61%)
  matrix products  210 us (13%)
  local copies, waits for them, and re-layouts  169 us (10%)
  other arithmetic  117 us (7%)
  starting transfers between devices  57.9 us (4%)
  waiting for transfers between devices  46.7 us (3%)
  between operations  31.2 us (2%)
    pallas_call x2, Pallas kernels, collect_shard(): pl.pallas_call(kernel, in_specs=[spec] * 2, out_specs=[spec] * 2, out_sha...  485 us
    pallas_call x2, Pallas kernels, spread_shards(): pl.pallas_call(partial(spread_kernel, groups, modes), in_specs=[spec] * (...  356 us
    dot_general x14, matrix products, back_low(): lax.dot_general(grads, weight, (((grads.ndim - 1,), (1,)), ((), ())), pre...  98.3 us
    dot_general x17, matrix products, matmul_low(): lax.dot_general(left, right, (((left.ndim - 1,), (0,)), ((), ())), prefer...  86.7 us
    unnamed x365, local copies, waits for them, and re-layouts  58.5 us
    pallas_call x2, Pallas kernels, core_chunks(): pl.pallas_call(partial(grad_kernel, plan, parts, len(lefts)), in_specs=[p...  58.2 us
    pallas_call x2, Pallas kernels, step_shard(): pl.pallas_call(partial(step_kernel, widths), grid_spec=pltpu.PrefetchScal...  48.1 us
    pallas_call x3, Pallas kernels, heads_backward(): pl.pallas_call(partial(heads_back_kernel, mode), grid=(queries.shape[0] /...  40.5 us
  transfers between devices with their start and end apart: 39, of which 11 were waited for; matrix products, arithmetic and copies ran while one was open for 12% of the time, Pallas kernels for 17%

profile of v5, /device:TPU:0, one launch (start us, length us, event | category | flops | bytes accessed | tf_op | source)
XLA Modules:
  0.0 1640.2 jit_solution(3814892257841672351)
XLA Ops:
  20.2 199.9 %shard_map.431 = (bf16[7296,1152]{1,0:T(8,128)(2,1)}, bf16[1152,4608]{1,0:T(8,128)(2,1)}, bf16[4608,1152]{1,0:T(8,128)(2,1)}, f32[8,8,128]{2,1,0:T(8,128)S(1)}) custom-call(bf16[6,304,1152]{2,1,0:T(8,128)(2,1)} %bitcast.343, bf16[6,192,1152]{2,1,0:T(8,128)(2,1)S(1)} %bitcast.355, f32[8,128]{1,0:T(8,128)S(1)} %broadcast_in_dim.120.refs_2_), custom_call_target="tpu_custom_call" | custom-call | bytes 200000000 | tf_op jit(solution)/shard_map/pallas_call | solution.py:1013
  229.2 9.4 multiply_convert_fusion.4
  256.4 156.3 %shard_map.433 = (bf16[1152,3456]{1,0:T(8,128)(2,1)}, bf16[1152,1152]{1,0:T(8,128)(2,1)}, bf16[1152,3456]{1,0:T(8,128)(2,1)}, bf16[1152,1152]{1,0:T(8,128)(2,1)}...) custom-call(bf16[6,288,1152]{2,1,0:T(8,128)(2,1)} %bitcast.354, ...), custom_call_target="tpu_custom_call" | custom-call | bytes 200000000 | tf_op jit(solution)/shard_map/pallas_call | solution.py:1013
  441.9 17.2 %collective-permute-start.1 = (f32[48,1152]{1,0:T(8,128)}, f32[48,1152]{1,0:T(8,128)}, u32[]{:S(2)}, u32[]{:S(2)}) collective-permute-start(f32[48,1152]{1,0:T(8,128)} %add.742), channel_id=1, source_target_pairs={{0,2},{1,3},{2,0},{3,1},{4,6},{5,7},{6,4},{7,5},{8,10},{9,11},{10,... | collective-permute-start | bytes 663560 | tf_op jit(solution)/shard_map/ppermute | solution.py:573
  466.8 10.2 collective-permute-done.2
  582.3 14.5 multiply_convert_fusion
  596.9 13.7 fusion.217
  616.6 17.9 %convert_reduce_fusion = (f32[4608]{0:T(1024)}, bf16[2,256,4608]{2,1,0:T(8,128)(2,1)}) fusion(f32[2,256,4608]{2,1,0:T(8,128)} %get-tuple-element.220, f32[4608]{0:T(1024)S(1)} %copy-done.142, bf16[2,256,1152]{2,1,0:T(8,128)(2,1)S(1)} %get-tuple-element.133, bf16[4608,1152]{1,0:T(8,128)(2,1)} %get-tuple-element.73), kind=kOutput, calls=%fused_computation.20 | convolution fusion | flops 5490077184 | bytes 25989120 | tf_op jit(solution)/shard_map/dot_general | solution.py:111
  634.4 13.4 multiply_reduce_fusion.6
  656.6 12.7 shard_map.438
  691.3 10.0 all-to-all-done.2
  710.3 13.7 shard_map.439
  793.9 10.0 convert_reduce_fusion.7
  808.6 14.1 shard_map.440
  825.9 10.0 multiply_reduce_fusion.3
  858.5 9.0 concatenate.90.beside
  876.2 34.1 %shard_map.442.chunks = f32[8,864,1152]{2,1,0:T(8,128)} custom-call(s32[1]{0:T(128)} %bitcast.core_ref, bf16[1152,512]{1,0:T(8,128)(2,1)} %bitcast.89.refs_0_, bf16[1152,512]{1,0:T(8,128)(2,1)} %collective-permute-done.9.refs_1_, bf16[1152,512]{1,0:T(8,128)(2,1)} %bitcast.90.refs_2_, bf16[1152,512]{1,0:T(8,128)(2,1)} %collective-permute-done.10.refs_3_, ...), custom_call_target="tpu_custom_call" | custom-call | tf_op jit(solution)/shard_map/pallas_call | solution.py:1480
  910.4 24.1 %shard_map.437.chunks = f32[8,576,1152]{2,1,0:T(8,128)} custom-call(s32[1]{0:T(128)} %bitcast.core_ref, bf16[1152,512]{1,0:T(8,128)(2,1)S(1)} %bitcast.362, bf16[1152,512]{1,0:T(8,128)(2,1)} %collective-permute-done.3.refs_1_, bf16[4608,512]{1,0:T(8,128)(2,1)} %bitcast.46.refs_2_, bf16[4608,512]{1,0:T(8,128)(2,1)} %collective-permute-done.4.refs_3_, ...), custom_call_target="tpu_custom_call" | custom-call | tf_op jit(solution)/shard_map/pallas_call | solution.py:1480
  934.4 198.3 %shard_map.441 = (f32[2,576,1152]{2,1,0:T(8,128)}, f32[120,1152]{1,0:T(8,128)}) custom-call(f32[8,576,1152]{2,1,0:T(8,128)} %shard_map.437.chunks, f32[120,1152]{1,0:T(8,128)} %concatenate.90.beside), custom_call_target="tpu_custom_call" | custom-call | bytes 800000000 | tf_op jit(solution)/shard_map/pallas_call | solution.py:1312
  1179.7 19.7 %fusion.104 = f32[240,7296]{1,0:T(8,128)} fusion(bf16[7296,1152]{1,0:T(8,128)(2,1)} %get-tuple-element.60, bf16[120,1152]{1,0:T(8,128)(2,1)S(1)} %subtract_convert_fusion.4, bf16[120,1152]{1,0:T(8,128)(2,1)S(1)} %convert_element_type.378), kind=kOutput, calls=%fused_computation.201 | convolution fusion | flops 4035502080 | bytes 24367104 | tf_op jit(solution)/shard_map/dot_general | solution.py:111
  1238.1 286.5 %shard_map.443 = (f32[2,864,1152]{2,1,0:T(8,128)}, f32[4,456,1152]{2,1,0:T(8,128)}) custom-call(f32[8,864,1152]{2,1,0:T(8,128)} %shard_map.442.chunks, f32[456,1152]{1,0:T(8,128)} %fusion.48.beside), custom_call_target="tpu_custom_call" | custom-call | bytes 800000000 | tf_op jit(solution)/shard_map/pallas_call | solution.py:1312
  1559.2 19.8 %shard_map.446 = (f32[10368,128]{1,0:T(8,128)}, f32[10368,128]{1,0:T(8,128)}, f32[10368,128]{1,0:T(8,128)}, f32[10368,128]{1,0:T(8,128)}) custom-call(s32[4,3]{1,0:T(4,128)S(1)} %fusion.172.table, f32[1]{0:T(128)} %bitcast.116.factor, f32[1152,1152]{1,0:T(8,128)} %bitcast.378, f32[10368,128]{1,0:T(8,128)} %bitcast.352, f32[10368,128]{1,0:T(8,128)} %bitcast.387, ...), custom_call_target="tpu_custom_call" | custom-call | tf_op jit(solution)/shard_map/pallas_call | solution.py:1552
  1579.0 28.3 %shard_map.445 = (f32[15552,128]{1,0:T(8,128)}, f32[15552,128]{1,0:T(8,128)}, f32[15552,128]{1,0:T(8,128)}, f32[15552,128]{1,0:T(8,128)}) custom-call(s32[6,3]{1,0:T(8,128)S(1)} %copy.204.table, f32[1]{0:T(128)} %bitcast.116.factor, f32[1728,1152]{1,0:T(8,128)} %bitcast.377, f32[15552,128]{1,0:T(8,128)} %bitcast.350, f32[15552,128]{1,0:T(8,128)} %bitcast.383, ...), custom_call_target="tpu_custom_call" | custom-call | tf_op jit(solution)/shard_map/pallas_call | solution.py:1552
  1607.3 24.7 %multiply_add_fusion.1 = (f32[2019840]{0:T(1024)}, f32[2019840]{0:T(1024)}, f32[2019840]{0:T(1024)}, f32[2019840]{0:T(1024)}) fusion(f32[2019840]{0:T(1024)} %param.49, f32[2019840]{0:T(1024)S(1)} %bitcast.349, f32[]{:T(128)} %min.7, f32[16416,128]{1,0:T(8,128)} %copy-done.2, s32[]{:T(128)S(6)} %select_n.229, f32[2019840]{0:T(1024)} %param.41, f32[2019840]{0:T(1024)} %param.45), kind=kLoop, calls=%fused_computation.27 | loop fusion | flops 36357120 | bytes 72714248 | tf_op jit(solution)/shard_map/add | solution.py:209
  (707 shorter events, 441.6 us)
Async XLA Ops:
  419.3 20.2 %collective-permute-start = (f32[48,1152]{1,0:T(8,128)}, f32[48,1152]{1,0:T(8,128)}, u32[]{:S(2)}, u32[]{:S(2)}) collective-permute-start(f32[48,1152]{1,0:T(8,128)} %fusion.226), channel_id=1, source_target_pairs={{0,1},{1,0},{2,3},{3,2},{4,5},{5,4},{6,7},{7,6},{8,9},{9,8},{10,11... | collective-permute-start | bytes 663560 | tf_op jit(solution)/shard_map/ppermute | solution.py:573
  441.9 22.4 %collective-permute-start.1 = (f32[48,1152]{1,0:T(8,128)}, f32[48,1152]{1,0:T(8,128)}, u32[]{:S(2)}, u32[]{:S(2)}) collective-permute-start(f32[48,1152]{1,0:T(8,128)} %add.742), channel_id=1, source_target_pairs={{0,2},{1,3},{2,0},{3,1},{4,6},{5,7},{6,4},{7,5},{8,10},{9,11},{10,... | collective-permute-start | bytes 663560 | tf_op jit(solution)/shard_map/ppermute | solution.py:573
  502.4 19.6 %all-to-all-start = ((bf16[1,2,256,1152]{3,1,0,2:T(2,128)(2,1)}), bf16[1,2,256,1152]{3,1,0,2:T(2,128)(2,1)S(1)}, u32[]{:S(2)}, u32[]{:S(2)}) async-start(bf16[1,2,256,1152]{3,1,0,2:T(2,128)(2,1)} %copy.177), calls=%async_computation | async-start | bytes 2359296 | tf_op jit(solution)/shard_map/all_to_all | solution.py:1917
  538.4 25.6 %all-to-all-start.1 = ((bf16[1,8,64,1152]{3,2,0,1:T(8,128)(2,1)}), bf16[1,8,64,1152]{3,2,0,1:T(8,128)(2,1)}, u32[]{:S(2)}, u32[]{:S(2)}) async-start(bf16[1,8,64,1152]{3,2,0,1:T(8,128)(2,1)} %bitcast.395), calls=%async_computation.1 | async-start | bytes 2359296 | tf_op jit(solution)/shard_map/all_to_all | solution.py:1925
  680.6 20.7 %all-to-all-start.2 = ((bf16[1,2,256,1152]{3,1,0,2:T(2,128)(2,1)}), bf16[1,2,256,1152]{3,1,0,2:T(2,128)(2,1)}, u32[]{:S(2)}, u32[]{:S(2)}) async-start(bf16[1,2,256,1152]{3,1,0,2:T(2,128)(2,1)} %copy.190), calls=%async_computation.2 | async-start | bytes 2359296 | tf_op jit(solution)/shard_map/all_to_all | solution.py:2032
  687.8 45.1 %collective-permute-start.8 = (f32[120,2304]{1,0:T(8,128)}, f32[120,2304]{1,0:T(8,128)}, u32[]{:S(2)}, u32[]{:S(2)}) collective-permute-start(f32[120,2304]{1,0:T(8,128)} %get-tuple-element.129), channel_id=1, source_target_pairs={{0,16},{1,17},{2,18},{3,19},{4,20},{5,21},{6,22},{7,23},{8,24},{9,... | collective-permute-start | bytes 3317768 | tf_op jit(solution)/shard_map/ppermute | solution.py:573
  727.9 62.2 %all-to-all-start.3 = ((bf16[1,8,64,3456]{3,2,0,1:T(8,128)(2,1)}), bf16[1,8,64,3456]{3,2,0,1:T(8,128)(2,1)}, u32[]{:S(2)}, u32[]{:S(2)}) async-start(bf16[1,8,64,3456]{3,2,0,1:T(8,128)(2,1)} %maximum_bitcast_fusion), calls=%async_computation.3 | async-start | bytes 7077888 | tf_op jit(solution)/shard_map/all_to_all | solution.py:2047
  732.7 444.3 %all-gather.2.cloned.1.call-start = ((), (), s32[]{:S(2)}) async-start(), calls=%async_computation.4 | async-start | bytes 9953280 | tf_op jit(solution)/shard_map/all_gather | solution.py:2087
  753.4 35.4 %collective-permute-start.10 = (bf16[1152,512]{1,0:T(8,128)(2,1)}, bf16[1152,512]{1,0:T(8,128)(2,1)}, u32[]{:S(2)}, u32[]{:S(2)}) collective-permute-start(bf16[1152,512]{1,0:T(8,128)(2,1)} %bitcast.90.refs_2_), channel_id=1, source_target_pairs={{0,8},{1,9},{2,10},{3,11},{4,12},{5,13},{6,14},{7,15},{8,0},{9,1},... | collective-permute-start | bytes 3538952 | tf_op jit(solution)/shard_map/ppermute | solution.py:573
  753.9 38.7 %collective-permute-start.9 = (bf16[1152,512]{1,0:T(8,128)(2,1)}, bf16[1152,512]{1,0:T(8,128)(2,1)}, u32[]{:S(2)}, u32[]{:S(2)}) collective-permute-start(bf16[1152,512]{1,0:T(8,128)(2,1)} %bitcast.89.refs_0_), channel_id=1, source_target_pairs={{0,8},{1,9},{2,10},{3,11},{4,12},{5,13},{6,14},{7,15},{8,0},{9,1},... | collective-permute-start | bytes 3538952 | tf_op jit(solution)/shard_map/ppermute | solution.py:573
  756.1 37.0 %collective-permute-start.11 = (bf16[1152,512]{1,0:T(8,128)(2,1)}, bf16[1152,512]{1,0:T(8,128)(2,1)}, u32[]{:S(2)}, u32[]{:S(2)}) collective-permute-start(bf16[1152,512]{1,0:T(8,128)(2,1)} %bitcast.91.refs_4_), channel_id=1, source_target_pairs={{0,8},{1,9},{2,10},{3,11},{4,12},{5,13},{6,14},{7,15},{8,0},{9,1},... | collective-permute-start | bytes 3538952 | tf_op jit(solution)/shard_map/ppermute | solution.py:573
  756.5 47.4 %collective-permute-start.16 = (bf16[512,1152]{1,0:T(8,128)(2,1)S(1)}, bf16[512,1152]{1,0:T(8,128)(2,1)}, u32[]{:S(2)}, u32[]{:S(2)}) collective-permute-start(bf16[512,1152]{1,0:T(8,128)(2,1)S(1)} %copy-done.14), channel_id=1, source_target_pairs={{0,8},{1,9},{2,10},{3,11},{4,12},{5,13},{6,14},{7,15},{8,0},{9,1},... | collective-permute-start | bytes 3538952 | tf_op jit(solution)/shard_map/ppermute | solution.py:573
  759.1 34.1 %collective-permute-start.17 = (bf16[512,1152]{1,0:T(8,128)(2,1)}, bf16[512,1152]{1,0:T(8,128)(2,1)}, u32[]{:S(2)}, u32[]{:S(2)}) collective-permute-start(bf16[512,1152]{1,0:T(8,128)(2,1)} %bitcast.401), channel_id=1, source_target_pairs={{0,8},{1,9},{2,10},{3,11},{4,12},{5,13},{6,14},{7,15},{8,0},{9,1},... | collective-permute-start | bytes 3538952 | tf_op jit(solution)/shard_map/ppermute | solution.py:573
  788.8 15.6 collective-permute-start.15
  792.5 30.3 %collective-permute-start.14 = (bf16[1152,512]{1,0:T(8,128)(2,1)S(1)}, bf16[1152,512]{1,0:T(8,128)(2,1)S(1)}, u32[]{:S(2)}, u32[]{:S(2)}) collective-permute-start(bf16[1152,512]{1,0:T(8,128)(2,1)S(1)} %bitcast.365), channel_id=1, source_target_pairs={{0,8},{1,9},{2,10},{3,11},{4,12},{5,13},{6,14},{7,15},{8,0},{9,1},... | collective-permute-start | bytes 3538952 | tf_op jit(solution)/shard_map/ppermute | solution.py:573
  793.0 31.4 %collective-permute-start.13 = (bf16[1152,512]{1,0:T(8,128)(2,1)S(1)}, bf16[1152,512]{1,0:T(8,128)(2,1)S(1)}, u32[]{:S(2)}, u32[]{:S(2)}) collective-permute-start(bf16[1152,512]{1,0:T(8,128)(2,1)S(1)} %bitcast.367), channel_id=1, source_target_pairs={{0,8},{1,9},{2,10},{3,11},{4,12},{5,13},{6,14},{7,15},{8,0},{9,1},... | collective-permute-start | bytes 3538952 | tf_op jit(solution)/shard_map/ppermute | solution.py:573
  793.2 32.6 %collective-permute-start.12 = (bf16[1152,512]{1,0:T(8,128)(2,1)S(1)}, bf16[1152,512]{1,0:T(8,128)(2,1)S(1)}, u32[]{:S(2)}, u32[]{:S(2)}) collective-permute-start(bf16[1152,512]{1,0:T(8,128)(2,1)S(1)} %bitcast.369), channel_id=1, source_target_pairs={{0,8},{1,9},{2,10},{3,11},{4,12},{5,13},{6,14},{7,15},{8,0},{9,1},... | collective-permute-start | bytes 3538952 | tf_op jit(solution)/shard_map/ppermute | solution.py:573
  803.9 106.4 %collective-permute-start.5 = (bf16[512,4608]{1,0:T(8,128)(2,1)}, bf16[512,4608]{1,0:T(8,128)(2,1)}, u32[]{:S(2)}, u32[]{:S(2)}) collective-permute-start(bf16[512,4608]{1,0:T(8,128)(2,1)} %bitcast.55.refs_4_), channel_id=1, source_target_pairs={{0,8},{1,9},{2,10},{3,11},{4,12},{5,13},{6,14},{7,15},{8,0},{9,1},... | collective-permute-start | bytes 14155784 | tf_op jit(solution)/shard_map/ppermute | solution.py:573
  804.3 106.0 %collective-permute-start.4 = (bf16[4608,512]{1,0:T(8,128)(2,1)}, bf16[4608,512]{1,0:T(8,128)(2,1)}, u32[]{:S(2)}, u32[]{:S(2)}) collective-permute-start(bf16[4608,512]{1,0:T(8,128)(2,1)} %bitcast.46.refs_2_), channel_id=1, source_target_pairs={{0,8},{1,9},{2,10},{3,11},{4,12},{5,13},{6,14},{7,15},{8,0},{9,1},... | collective-permute-start | bytes 14155784 | tf_op jit(solution)/shard_map/ppermute | solution.py:573
  824.0 15.1 collective-permute-start.18
  825.8 13.9 collective-permute-start.20
  844.6 65.7 %collective-permute-start.6 = (bf16[512,1152]{1,0:T(8,128)(2,1)S(1)}, bf16[512,1152]{1,0:T(8,128)(2,1)}, u32[]{:S(2)}, u32[]{:S(2)}) collective-permute-start(bf16[512,1152]{1,0:T(8,128)(2,1)S(1)} %bitcast.359), channel_id=1, source_target_pairs={{0,8},{1,9},{2,10},{3,11},{4,12},{5,13},{6,14},{7,15},{8,0},{9,1},... | collective-permute-start | bytes 3538952 | tf_op jit(solution)/shard_map/ppermute | solution.py:573
  845.8 64.5 %collective-permute-start.3 = (bf16[1152,512]{1,0:T(8,128)(2,1)S(1)}, bf16[1152,512]{1,0:T(8,128)(2,1)}, u32[]{:S(2)}, u32[]{:S(2)}) collective-permute-start(bf16[1152,512]{1,0:T(8,128)(2,1)S(1)} %bitcast.361), channel_id=1, source_target_pairs={{0,8},{1,9},{2,10},{3,11},{4,12},{5,13},{6,14},{7,15},{8,0},{9,1},... | collective-permute-start | bytes 3538952 | tf_op jit(solution)/shard_map/ppermute | solution.py:573
  846.2 21.3 %collective-permute-start.21 = (bf16[512,1152]{1,0:T(8,128)(2,1)}, bf16[512,1152]{1,0:T(8,128)(2,1)}, u32[]{:S(2)}, u32[]{:S(2)}) collective-permute-start(bf16[512,1152]{1,0:T(8,128)(2,1)} %bitcast.73.refs_26_), channel_id=1, source_target_pairs={{0,8},{1,9},{2,10},{3,11},{4,12},{5,13},{6,14},{7,15},{8,0},{9,1},... | collective-permute-start | bytes 3538952 | tf_op jit(solution)/shard_map/ppermute | solution.py:573
  (193 other events, 1716.1 us)
Sparse Core Ops, SparseCore 0:
  747.8 130.0 all-gather.1

commit v6 on v5

--- a/solution.py
+++ b/solution.py
@@ -864,10 +864,13 @@
 
     def peers(item, arriving, action):
         for k in range(1, N_OWN):
-            if modes[item] != "first":
+            if modes[item] == "gather":
                 action(k)
+            elif modes[item] == "first":
+                pl.when(clip == (k if arriving else 0))(lambda: action(k))
             else:
-                pl.when(clip == (k if arriving else 0))(lambda: action(k))
+                to = clip if arriving else (clip + k) % N_OWN
+                pl.when(to >= N_OWN // 2)(lambda: action(k))
 
     fallen = []
 
@@ -1873,6 +1876,7 @@
     )
     early = early[0]
     cap_left = cap_left[:, :L_CAP].reshape(n_clip * L_CAP, EMB_PAD // 4)
+    cap_left = jnp.where(clip_id >= cap_owners[0], cap_left, jnp.zeros_like(cap_left))
     pre_one, time_embed = early[:n_clip], early[n_clip : 2 * n_clip]
     patch_w = early[2 * n_clip :].astype(jnp.bfloat16)
     act_one = jax.nn.silu(pre_one).astype(jnp.bfloat16)
@@ -2179,7 +2183,8 @@
     small_right = jnp.concatenate([grad_one, grad_embed, zero_rows], 0)
     first_kind = (quarter_row < ROW_CAP_TWO)[None]
     no_left = jnp.zeros_like(cap_left)
-    g_null = from_cap_rows(two_parts(lambda part: back_low(part, cap_weights), null_sum))
+    null_back = back_low(cap_weights, jnp.concatenate(halves(null_sum), 0))
+    g_null = from_cap_rows((null_back[:, :L_CAP] + null_back[:, L_CAP:]).T)
     n_null = -(-null_end // D)
     n_known = -(-(2 * PATCH_VALUES + n_null) // 16) * 16
     null_rows = jnp.pad(g_null.reshape(-1), (0, (n_known - 2 * PATCH_VALUES) * D - null_end))

time: 1650 us -> 1630 us (0.988)
    unnamed x365 -> x361, local copies, waits for them, and re-layouts: 58.5 us -> 58.9 us
  transfers between devices with their start and end apart: 39 -> 39, of which waited for: 11 -> 12; matrix products, arithmetic and copies ran while one was open for 12% -> 12% of each run, Pallas kernels for 17% -> 18%
where the time goes in v6:
time: 1630 us; the launch traced here: 1620 us
  Pallas kernels  1000 us (61%)
  matrix products  198 us (12%)
  local copies, waits for them, and re-layouts  169 us (10%)
  other arithmetic  115 us (7%)
  starting transfers between devices  61.6 us (4%)
  waiting for transfers between devices  38.6 us (2%)
  between operations  31.5 us (2%)
    pallas_call x2, Pallas kernels, collect_shard(): pl.pallas_call(kernel, in_specs=[spec] * 2, out_specs=[spec] * 2, out_sha...  484 us
    pallas_call x2, Pallas kernels, spread_shards(): pl.pallas_call(partial(spread_kernel, groups, modes), in_specs=[spec] * (...  351 us
    dot_general x14, matrix products, back_low(): lax.dot_general(grads, weight, (((grads.ndim - 1,), (1,)), ((), ())), pre...  87.1 us
    dot_general x17, matrix products, matmul_low(): lax.dot_general(left, right, (((left.ndim - 1,), (0,)), ((), ())), prefer...  86.4 us
    unnamed x361, local copies, waits for them, and re-layouts  58.9 us
    pallas_call x2, Pallas kernels, core_chunks(): pl.pallas_call(partial(grad_kernel, plan, parts, len(lefts)), in_specs=[p...  58.2 us
    pallas_call x2, Pallas kernels, step_shard(): pl.pallas_call(partial(step_kernel, widths), grid_spec=pltpu.PrefetchScal...  48.1 us
    ppermute x34, starting transfers between devices, shift(): return lax.ppermute(value, AXES, perm)  43.8 us
  transfers between devices with their start and end apart: 39, of which 12 were waited for; matrix products, arithmetic and copies ran while one was open for 12% of the time, Pallas kernels for 18%

profile of v6, /device:TPU:0, one launch (start us, length us, event | category | flops | bytes accessed | tf_op | source)
XLA Modules:
  0.0 1615.3 jit_solution(2650030640886063543)
XLA Ops:
  20.3 199.8 %shard_map.431 = (bf16[7296,1152]{1,0:T(8,128)(2,1)}, bf16[1152,4608]{1,0:T(8,128)(2,1)}, bf16[4608,1152]{1,0:T(8,128)(2,1)}, f32[8,8,128]{2,1,0:T(8,128)S(1)}) custom-call(bf16[6,304,1152]{2,1,0:T(8,128)(2,1)} %bitcast.345, bf16[6,192,1152]{2,1,0:T(8,128)(2,1)S(1)} %bitcast.357, f32[8,128]{1,0:T(8,128)S(1)} %broadcast_in_dim.117.refs_2_), custom_call_target="tpu_custom_call" | custom-call | bytes 200000000 | tf_op jit(solution)/shard_map/pallas_call | solution.py:1016
  229.2 9.4 multiply_convert_fusion.4
  256.4 150.7 %shard_map.433 = (bf16[1152,3456]{1,0:T(8,128)(2,1)}, bf16[1152,1152]{1,0:T(8,128)(2,1)}, bf16[1152,3456]{1,0:T(8,128)(2,1)}, bf16[1152,1152]{1,0:T(8,128)(2,1)}...) custom-call(bf16[6,288,1152]{2,1,0:T(8,128)(2,1)} %bitcast.356, ...), custom_call_target="tpu_custom_call" | custom-call | bytes 200000000 | tf_op jit(solution)/shard_map/pallas_call | solution.py:1016
  435.9 17.2 %collective-permute-start.1 = (f32[48,1152]{1,0:T(8,128)}, f32[48,1152]{1,0:T(8,128)}, u32[]{:S(2)}, u32[]{:S(2)}) collective-permute-start(f32[48,1152]{1,0:T(8,128)} %add.742), channel_id=1, source_target_pairs={{0,2},{1,3},{2,0},{3,1},{4,6},{5,7},{6,4},{7,5},{8,10},{9,11},{10,... | collective-permute-start | bytes 663560 | tf_op jit(solution)/shard_map/ppermute | solution.py:573
  510.2 8.6 all-to-all-done
  519.0 8.1 fusion.198
  573.4 14.4 multiply_convert_fusion
  587.9 13.6 fusion.218
  607.4 17.8 %convert_reduce_fusion = (f32[4608]{0:T(1024)}, bf16[2,256,4608]{2,1,0:T(8,128)(2,1)}) fusion(f32[2,256,4608]{2,1,0:T(8,128)} %get-tuple-element.220, f32[4608]{0:T(1024)S(1)} %copy-done.140, bf16[2,256,1152]{2,1,0:T(8,128)(2,1)S(1)} %get-tuple-element.133, bf16[4608,1152]{1,0:T(8,128)(2,1)} %get-tuple-element.73), kind=kOutput, calls=%fused_computation.20 | convolution fusion | flops 5490077184 | bytes 25989120 | tf_op jit(solution)/shard_map/dot_general | solution.py:111
  625.2 13.3 multiply_reduce_fusion.6
  646.6 12.6 shard_map.438
  700.2 13.6 shard_map.439
  783.7 10.3 convert_reduce_fusion.7
  797.9 14.1 shard_map.440
  815.2 10.0 multiply_reduce_fusion.3
  847.8 9.0 concatenate.90.beside
  865.5 34.1 %shard_map.442.chunks = f32[8,864,1152]{2,1,0:T(8,128)} custom-call(s32[1]{0:T(128)} %bitcast.core_ref, bf16[1152,512]{1,0:T(8,128)(2,1)} %bitcast.89.refs_0_, bf16[1152,512]{1,0:T(8,128)(2,1)} %collective-permute-done.9.refs_1_, bf16[1152,512]{1,0:T(8,128)(2,1)} %bitcast.90.refs_2_, bf16[1152,512]{1,0:T(8,128)(2,1)} %collective-permute-done.10.refs_3_, ...), custom_call_target="tpu_custom_call" | custom-call | tf_op jit(solution)/shard_map/pallas_call | solution.py:1483
  899.6 24.1 %shard_map.437.chunks = f32[8,576,1152]{2,1,0:T(8,128)} custom-call(s32[1]{0:T(128)} %bitcast.core_ref, bf16[1152,512]{1,0:T(8,128)(2,1)S(1)} %bitcast.364, bf16[1152,512]{1,0:T(8,128)(2,1)} %collective-permute-done.3.refs_1_, bf16[4608,512]{1,0:T(8,128)(2,1)} %bitcast.46.refs_2_, bf16[4608,512]{1,0:T(8,128)(2,1)} %collective-permute-done.4.refs_3_, ...), custom_call_target="tpu_custom_call" | custom-call | tf_op jit(solution)/shard_map/pallas_call | solution.py:1483
  923.7 202.6 %shard_map.441 = (f32[2,576,1152]{2,1,0:T(8,128)}, f32[120,1152]{1,0:T(8,128)}) custom-call(f32[8,576,1152]{2,1,0:T(8,128)} %shard_map.437.chunks, f32[120,1152]{1,0:T(8,128)} %concatenate.90.beside), custom_call_target="tpu_custom_call" | custom-call | bytes 800000000 | tf_op jit(solution)/shard_map/pallas_call | solution.py:1315
  1171.1 9.3 fusion.105
  1216.0 281.8 %shard_map.443 = (f32[2,864,1152]{2,1,0:T(8,128)}, f32[4,456,1152]{2,1,0:T(8,128)}) custom-call(f32[8,864,1152]{2,1,0:T(8,128)} %shard_map.442.chunks, f32[456,1152]{1,0:T(8,128)} %fusion.49.beside), custom_call_target="tpu_custom_call" | custom-call | bytes 800000000 | tf_op jit(solution)/shard_map/pallas_call | solution.py:1315
  1534.1 19.8 %shard_map.446 = (f32[10368,128]{1,0:T(8,128)}, f32[10368,128]{1,0:T(8,128)}, f32[10368,128]{1,0:T(8,128)}, f32[10368,128]{1,0:T(8,128)}) custom-call(s32[4,3]{1,0:T(4,128)S(1)} %fusion.173.table, f32[1]{0:T(128)} %bitcast.117.factor, f32[1152,1152]{1,0:T(8,128)} %bitcast.380, f32[10368,128]{1,0:T(8,128)} %bitcast.354, f32[10368,128]{1,0:T(8,128)} %bitcast.389, ...), custom_call_target="tpu_custom_call" | custom-call | tf_op jit(solution)/shard_map/pallas_call | solution.py:1555
  1553.9 28.3 %shard_map.445 = (f32[15552,128]{1,0:T(8,128)}, f32[15552,128]{1,0:T(8,128)}, f32[15552,128]{1,0:T(8,128)}, f32[15552,128]{1,0:T(8,128)}) custom-call(s32[6,3]{1,0:T(8,128)S(1)} %copy.204.table, f32[1]{0:T(128)} %bitcast.117.factor, f32[1728,1152]{1,0:T(8,128)} %bitcast.379, f32[15552,128]{1,0:T(8,128)} %bitcast.352, f32[15552,128]{1,0:T(8,128)} %bitcast.385, ...), custom_call_target="tpu_custom_call" | custom-call | tf_op jit(solution)/shard_map/pallas_call | solution.py:1555
  1582.2 25.0 %multiply_add_fusion.1 = (f32[2019840]{0:T(1024)}, f32[2019840]{0:T(1024)}, f32[2019840]{0:T(1024)}, f32[2019840]{0:T(1024)}) fusion(f32[2019840]{0:T(1024)} %param.49, f32[2019840]{0:T(1024)S(1)} %bitcast.351, f32[]{:T(128)} %min.7, f32[16416,128]{1,0:T(8,128)} %copy-done.2, s32[]{:T(128)S(6)} %select_n.243, f32[2019840]{0:T(1024)} %param.41, f32[2019840]{0:T(1024)} %param.45), kind=kLoop, calls=%fused_computation.27 | loop fusion | flops 36357120 | bytes 72714248 | tf_op jit(solution)/shard_map/add | solution.py:209
  (703 shorter events, 436.6 us)
Async XLA Ops:
  413.7 19.9 %collective-permute-start = (f32[48,1152]{1,0:T(8,128)}, f32[48,1152]{1,0:T(8,128)}, u32[]{:S(2)}, u32[]{:S(2)}) collective-permute-start(f32[48,1152]{1,0:T(8,128)} %fusion.227), channel_id=1, source_target_pairs={{0,1},{1,0},{2,3},{3,2},{4,5},{5,4},{6,7},{7,6},{8,9},{9,8},{10,11... | collective-permute-start | bytes 663560 | tf_op jit(solution)/shard_map/ppermute | solution.py:573
  435.9 22.4 %collective-permute-start.1 = (f32[48,1152]{1,0:T(8,128)}, f32[48,1152]{1,0:T(8,128)}, u32[]{:S(2)}, u32[]{:S(2)}) collective-permute-start(f32[48,1152]{1,0:T(8,128)} %add.742), channel_id=1, source_target_pairs={{0,2},{1,3},{2,0},{3,1},{4,6},{5,7},{6,4},{7,5},{8,10},{9,11},{10,... | collective-permute-start | bytes 663560 | tf_op jit(solution)/shard_map/ppermute | solution.py:573
  459.3 14.8 collective-permute-start.2
  499.2 19.6 %all-to-all-start = ((bf16[1,2,256,1152]{3,1,0,2:T(2,128)(2,1)}), bf16[1,2,256,1152]{3,1,0,2:T(2,128)(2,1)S(1)}, u32[]{:S(2)}, u32[]{:S(2)}) async-start(bf16[1,2,256,1152]{3,1,0,2:T(2,128)(2,1)} %copy.177), calls=%async_computation | async-start | bytes 2359296 | tf_op jit(solution)/shard_map/all_to_all | solution.py:1921
  534.9 20.6 %all-to-all-start.1 = ((bf16[1,8,64,1152]{3,2,0,1:T(8,128)(2,1)}), bf16[1,8,64,1152]{3,2,0,1:T(8,128)(2,1)}, u32[]{:S(2)}, u32[]{:S(2)}) async-start(bf16[1,8,64,1152]{3,2,0,1:T(8,128)(2,1)} %bitcast.397), calls=%async_computation.1 | async-start | bytes 2359296 | tf_op jit(solution)/shard_map/all_to_all | solution.py:1929
  670.5 20.7 %all-to-all-start.2 = ((bf16[1,2,256,1152]{3,1,0,2:T(2,128)(2,1)}), bf16[1,2,256,1152]{3,1,0,2:T(2,128)(2,1)}, u32[]{:S(2)}, u32[]{:S(2)}) async-start(bf16[1,2,256,1152]{3,1,0,2:T(2,128)(2,1)} %copy.190), calls=%async_computation.2 | async-start | bytes 2359296 | tf_op jit(solution)/shard_map/all_to_all | solution.py:2036
  677.7 45.1 %collective-permute-start.8 = (f32[120,2304]{1,0:T(8,128)}, f32[120,2304]{1,0:T(8,128)}, u32[]{:S(2)}, u32[]{:S(2)}) collective-permute-start(f32[120,2304]{1,0:T(8,128)} %get-tuple-element.129), channel_id=1, source_target_pairs={{0,16},{1,17},{2,18},{3,19},{4,20},{5,21},{6,22},{7,23},{8,24},{9,... | collective-permute-start | bytes 3317768 | tf_op jit(solution)/shard_map/ppermute | solution.py:573
  717.7 62.2 %all-to-all-start.3 = ((bf16[1,8,64,3456]{3,2,0,1:T(8,128)(2,1)}), bf16[1,8,64,3456]{3,2,0,1:T(8,128)(2,1)}, u32[]{:S(2)}, u32[]{:S(2)}) async-start(bf16[1,8,64,3456]{3,2,0,1:T(8,128)(2,1)} %maximum_bitcast_fusion), calls=%async_computation.3 | async-start | bytes 7077888 | tf_op jit(solution)/shard_map/all_to_all | solution.py:2051
  722.6 445.9 %all-gather.2.cloned.1.call-start = ((), (), s32[]{:S(2)}) async-start(), calls=%async_computation.4 | async-start | bytes 9953280 | tf_op jit(solution)/shard_map/all_gather | solution.py:2091
  743.2 35.4 %collective-permute-start.10 = (bf16[1152,512]{1,0:T(8,128)(2,1)}, bf16[1152,512]{1,0:T(8,128)(2,1)}, u32[]{:S(2)}, u32[]{:S(2)}) collective-permute-start(bf16[1152,512]{1,0:T(8,128)(2,1)} %bitcast.90.refs_2_), channel_id=1, source_target_pairs={{0,8},{1,9},{2,10},{3,11},{4,12},{5,13},{6,14},{7,15},{8,0},{9,1},... | collective-permute-start | bytes 3538952 | tf_op jit(solution)/shard_map/ppermute | solution.py:573
  743.6 38.7 %collective-permute-start.9 = (bf16[1152,512]{1,0:T(8,128)(2,1)}, bf16[1152,512]{1,0:T(8,128)(2,1)}, u32[]{:S(2)}, u32[]{:S(2)}) collective-permute-start(bf16[1152,512]{1,0:T(8,128)(2,1)} %bitcast.89.refs_0_), channel_id=1, source_target_pairs={{0,8},{1,9},{2,10},{3,11},{4,12},{5,13},{6,14},{7,15},{8,0},{9,1},... | collective-permute-start | bytes 3538952 | tf_op jit(solution)/shard_map/ppermute | solution.py:573
  745.9 37.0 %collective-permute-start.11 = (bf16[1152,512]{1,0:T(8,128)(2,1)}, bf16[1152,512]{1,0:T(8,128)(2,1)}, u32[]{:S(2)}, u32[]{:S(2)}) collective-permute-start(bf16[1152,512]{1,0:T(8,128)(2,1)} %bitcast.91.refs_4_), channel_id=1, source_target_pairs={{0,8},{1,9},{2,10},{3,11},{4,12},{5,13},{6,14},{7,15},{8,0},{9,1},... | collective-permute-start | bytes 3538952 | tf_op jit(solution)/shard_map/ppermute | solution.py:573
  746.3 47.7 %collective-permute-start.16 = (bf16[512,1152]{1,0:T(8,128)(2,1)S(1)}, bf16[512,1152]{1,0:T(8,128)(2,1)}, u32[]{:S(2)}, u32[]{:S(2)}) collective-permute-start(bf16[512,1152]{1,0:T(8,128)(2,1)S(1)} %copy-done.14), channel_id=1, source_target_pairs={{0,8},{1,9},{2,10},{3,11},{4,12},{5,13},{6,14},{7,15},{8,0},{9,1},... | collective-permute-start | bytes 3538952 | tf_op jit(solution)/shard_map/ppermute | solution.py:573
  749.0 34.0 %collective-permute-start.17 = (bf16[512,1152]{1,0:T(8,128)(2,1)}, bf16[512,1152]{1,0:T(8,128)(2,1)}, u32[]{:S(2)}, u32[]{:S(2)}) collective-permute-start(bf16[512,1152]{1,0:T(8,128)(2,1)} %bitcast.403), channel_id=1, source_target_pairs={{0,8},{1,9},{2,10},{3,11},{4,12},{5,13},{6,14},{7,15},{8,0},{9,1},... | collective-permute-start | bytes 3538952 | tf_op jit(solution)/shard_map/ppermute | solution.py:573
  778.6 15.8 collective-permute-start.15
  782.3 29.7 %collective-permute-start.14 = (bf16[1152,512]{1,0:T(8,128)(2,1)S(1)}, bf16[1152,512]{1,0:T(8,128)(2,1)S(1)}, u32[]{:S(2)}, u32[]{:S(2)}) collective-permute-start(bf16[1152,512]{1,0:T(8,128)(2,1)S(1)} %bitcast.367), channel_id=1, source_target_pairs={{0,8},{1,9},{2,10},{3,11},{4,12},{5,13},{6,14},{7,15},{8,0},{9,1},... | collective-permute-start | bytes 3538952 | tf_op jit(solution)/shard_map/ppermute | solution.py:573
  782.8 30.6 %collective-permute-start.13 = (bf16[1152,512]{1,0:T(8,128)(2,1)S(1)}, bf16[1152,512]{1,0:T(8,128)(2,1)S(1)}, u32[]{:S(2)}, u32[]{:S(2)}) collective-permute-start(bf16[1152,512]{1,0:T(8,128)(2,1)S(1)} %bitcast.369), channel_id=1, source_target_pairs={{0,8},{1,9},{2,10},{3,11},{4,12},{5,13},{6,14},{7,15},{8,0},{9,1},... | collective-permute-start | bytes 3538952 | tf_op jit(solution)/shard_map/ppermute | solution.py:573
  783.0 32.0 %collective-permute-start.12 = (bf16[1152,512]{1,0:T(8,128)(2,1)S(1)}, bf16[1152,512]{1,0:T(8,128)(2,1)S(1)}, u32[]{:S(2)}, u32[]{:S(2)}) collective-permute-start(bf16[1152,512]{1,0:T(8,128)(2,1)S(1)} %bitcast.371), channel_id=1, source_target_pairs={{0,8},{1,9},{2,10},{3,11},{4,12},{5,13},{6,14},{7,15},{8,0},{9,1},... | collective-permute-start | bytes 3538952 | tf_op jit(solution)/shard_map/ppermute | solution.py:573
  794.0 105.6 %collective-permute-start.5 = (bf16[512,4608]{1,0:T(8,128)(2,1)}, bf16[512,4608]{1,0:T(8,128)(2,1)}, u32[]{:S(2)}, u32[]{:S(2)}) collective-permute-start(bf16[512,4608]{1,0:T(8,128)(2,1)} %bitcast.55.refs_4_), channel_id=1, source_target_pairs={{0,8},{1,9},{2,10},{3,11},{4,12},{5,13},{6,14},{7,15},{8,0},{9,1},... | collective-permute-start | bytes 14155784 | tf_op jit(solution)/shard_map/ppermute | solution.py:573
  794.4 105.2 %collective-permute-start.4 = (bf16[4608,512]{1,0:T(8,128)(2,1)}, bf16[4608,512]{1,0:T(8,128)(2,1)}, u32[]{:S(2)}, u32[]{:S(2)}) collective-permute-start(bf16[4608,512]{1,0:T(8,128)(2,1)} %bitcast.46.refs_2_), channel_id=1, source_target_pairs={{0,8},{1,9},{2,10},{3,11},{4,12},{5,13},{6,14},{7,15},{8,0},{9,1},... | collective-permute-start | bytes 14155784 | tf_op jit(solution)/shard_map/ppermute | solution.py:573
  813.1 15.1 collective-permute-start.18
  833.8 65.8 %collective-permute-start.6 = (bf16[512,1152]{1,0:T(8,128)(2,1)S(1)}, bf16[512,1152]{1,0:T(8,128)(2,1)}, u32[]{:S(2)}, u32[]{:S(2)}) collective-permute-start(bf16[512,1152]{1,0:T(8,128)(2,1)S(1)} %bitcast.361), channel_id=1, source_target_pairs={{0,8},{1,9},{2,10},{3,11},{4,12},{5,13},{6,14},{7,15},{8,0},{9,1},... | collective-permute-start | bytes 3538952 | tf_op jit(solution)/shard_map/ppermute | solution.py:573
  834.9 64.7 %collective-permute-start.3 = (bf16[1152,512]{1,0:T(8,128)(2,1)S(1)}, bf16[1152,512]{1,0:T(8,128)(2,1)}, u32[]{:S(2)}, u32[]{:S(2)}) collective-permute-start(bf16[1152,512]{1,0:T(8,128)(2,1)S(1)} %bitcast.363), channel_id=1, source_target_pairs={{0,8},{1,9},{2,10},{3,11},{4,12},{5,13},{6,14},{7,15},{8,0},{9,1},... | collective-permute-start | bytes 3538952 | tf_op jit(solution)/shard_map/ppermute | solution.py:573
  835.4 21.4 %collective-permute-start.21 = (bf16[512,1152]{1,0:T(8,128)(2,1)}, bf16[512,1152]{1,0:T(8,128)(2,1)}, u32[]{:S(2)}, u32[]{:S(2)}) collective-permute-start(bf16[512,1152]{1,0:T(8,128)(2,1)} %bitcast.73.refs_26_), channel_id=1, source_target_pairs={{0,8},{1,9},{2,10},{3,11},{4,12},{5,13},{6,14},{7,15},{8,0},{9,1},... | collective-permute-start | bytes 3538952 | tf_op jit(solution)/shard_map/ppermute | solution.py:573
  (191 other events, 1817.7 us)
Sparse Core Ops, SparseCore 0:
  737.7 131.9 all-gather.1

commit v7 on v6

--- a/solution.py
+++ b/solution.py
@@ -1043,7 +1043,7 @@
     )(*[own.reshape(count, own.shape[0] // count, D) for own, count in zip(owns, blocks)], *values)
 
 
-LAG = 5
+LAG = 4
 
 
 def collect_kernel(first, last, chunks, small, part, out, small_out, part_out, scratch):

time: 1630 us -> 1640 us (level)
  transfers between devices with their start and end apart: 39 -> 39, of which waited for: 12 -> 12; matrix products, arithmetic and copies ran while one was open for 12% -> 12% of each run, Pallas kernels for 18% -> 17%
where the time goes in v7:
time: 1640 us; the launch traced here: 1630 us
  Pallas kernels  1010 us (62%)
  matrix products  198 us (12%)
  local copies, waits for them, and re-layouts  169 us (10%)
  other arithmetic  115 us (7%)
  starting transfers between devices  59.8 us (4%)
  waiting for transfers between devices  40.7 us (2%)
  between operations  31.4 us (2%)
    pallas_call x2, Pallas kernels, collect_shard(): pl.pallas_call(kernel, in_specs=[spec] * 2, out_specs=[spec] * 2, out_sha...  495 us
    pallas_call x2, Pallas kernels, spread_shards(): pl.pallas_call(partial(spread_kernel, groups, modes), in_specs=[spec] * (...  351 us
    dot_general x14, matrix products, back_low(): lax.dot_general(grads, weight, (((grads.ndim - 1,), (1,)), ((), ())), pre...  87.1 us
    dot_general x17, matrix products, matmul_low(): lax.dot_general(left, right, (((left.ndim - 1,), (0,)), ((), ())), prefer...  86.4 us
    unnamed x361, local copies, waits for them, and re-layouts  58.9 us
    pallas_call x2, Pallas kernels, core_chunks(): pl.pallas_call(partial(grad_kernel, plan, parts, len(lefts)), in_specs=[p...  58.2 us
    pallas_call x2, Pallas kernels, step_shard(): pl.pallas_call(partial(step_kernel, widths), grid_spec=pltpu.PrefetchScal...  48.1 us
    ppermute x34, starting transfers between devices, shift(): return lax.ppermute(value, AXES, perm)  42 us
  transfers between devices with their start and end apart: 39, of which 12 were waited for; matrix products, arithmetic and copies ran while one was open for 12% of the time, Pallas kernels for 17%

profile of v7, /device:TPU:0, one launch (start us, length us, event | category | flops | bytes accessed | tf_op | source)
XLA Modules:
  0.0 1626.4 jit_solution(17653086024066157785)
XLA Ops:
  20.3 199.8 %shard_map.431 = (bf16[7296,1152]{1,0:T(8,128)(2,1)}, bf16[1152,4608]{1,0:T(8,128)(2,1)}, bf16[4608,1152]{1,0:T(8,128)(2,1)}, f32[8,8,128]{2,1,0:T(8,128)S(1)}) custom-call(bf16[6,304,1152]{2,1,0:T(8,128)(2,1)} %bitcast.345, bf16[6,192,1152]{2,1,0:T(8,128)(2,1)S(1)} %bitcast.357, f32[8,128]{1,0:T(8,128)S(1)} %broadcast_in_dim.117.refs_2_), custom_call_target="tpu_custom_call" | custom-call | bytes 200000000 | tf_op jit(solution)/shard_map/pallas_call | solution.py:1016
  229.2 9.4 multiply_convert_fusion.4
  256.4 150.7 %shard_map.433 = (bf16[1152,3456]{1,0:T(8,128)(2,1)}, bf16[1152,1152]{1,0:T(8,128)(2,1)}, bf16[1152,3456]{1,0:T(8,128)(2,1)}, bf16[1152,1152]{1,0:T(8,128)(2,1)}...) custom-call(bf16[6,288,1152]{2,1,0:T(8,128)(2,1)} %bitcast.356, ...), custom_call_target="tpu_custom_call" | custom-call | bytes 200000000 | tf_op jit(solution)/shard_map/pallas_call | solution.py:1016
  435.9 17.2 %collective-permute-start.1 = (f32[48,1152]{1,0:T(8,128)}, f32[48,1152]{1,0:T(8,128)}, u32[]{:S(2)}, u32[]{:S(2)}) collective-permute-start(f32[48,1152]{1,0:T(8,128)} %add.742), channel_id=1, source_target_pairs={{0,2},{1,3},{2,0},{3,1},{4,6},{5,7},{6,4},{7,5},{8,10},{9,11},{10,... | collective-permute-start | bytes 663560 | tf_op jit(solution)/shard_map/ppermute | solution.py:573
  510.2 8.6 all-to-all-done
  519.0 8.1 fusion.198
  573.4 14.4 multiply_convert_fusion
  587.9 13.6 fusion.218
  607.4 17.8 %convert_reduce_fusion = (f32[4608]{0:T(1024)}, bf16[2,256,4608]{2,1,0:T(8,128)(2,1)}) fusion(f32[2,256,4608]{2,1,0:T(8,128)} %get-tuple-element.220, f32[4608]{0:T(1024)S(1)} %copy-done.140, bf16[2,256,1152]{2,1,0:T(8,128)(2,1)S(1)} %get-tuple-element.133, bf16[4608,1152]{1,0:T(8,128)(2,1)} %get-tuple-element.73), kind=kOutput, calls=%fused_computation.20 | convolution fusion | flops 5490077184 | bytes 25989120 | tf_op jit(solution)/shard_map/dot_general | solution.py:111
  625.2 13.3 multiply_reduce_fusion.6
  646.6 12.6 shard_map.438
  700.2 13.6 shard_map.439
  783.7 10.3 convert_reduce_fusion.7
  797.9 14.1 shard_map.440
  815.2 10.0 multiply_reduce_fusion.3
  847.8 9.0 concatenate.90.beside
  865.5 34.1 %shard_map.442.chunks = f32[8,864,1152]{2,1,0:T(8,128)} custom-call(s32[1]{0:T(128)} %bitcast.core_ref, bf16[1152,512]{1,0:T(8,128)(2,1)} %bitcast.89.refs_0_, bf16[1152,512]{1,0:T(8,128)(2,1)} %collective-permute-done.9.refs_1_, bf16[1152,512]{1,0:T(8,128)(2,1)} %bitcast.90.refs_2_, bf16[1152,512]{1,0:T(8,128)(2,1)} %collective-permute-done.10.refs_3_, ...), custom_call_target="tpu_custom_call" | custom-call | tf_op jit(solution)/shard_map/pallas_call | solution.py:1483
  899.6 24.1 %shard_map.437.chunks = f32[8,576,1152]{2,1,0:T(8,128)} custom-call(s32[1]{0:T(128)} %bitcast.core_ref, bf16[1152,512]{1,0:T(8,128)(2,1)S(1)} %bitcast.364, bf16[1152,512]{1,0:T(8,128)(2,1)} %collective-permute-done.3.refs_1_, bf16[4608,512]{1,0:T(8,128)(2,1)} %bitcast.46.refs_2_, bf16[4608,512]{1,0:T(8,128)(2,1)} %collective-permute-done.4.refs_3_, ...), custom_call_target="tpu_custom_call" | custom-call | tf_op jit(solution)/shard_map/pallas_call | solution.py:1483
  923.7 197.7 %shard_map.441 = (f32[2,576,1152]{2,1,0:T(8,128)}, f32[120,1152]{1,0:T(8,128)}) custom-call(f32[8,576,1152]{2,1,0:T(8,128)} %shard_map.437.chunks, f32[120,1152]{1,0:T(8,128)} %concatenate.90.beside), custom_call_target="tpu_custom_call" | custom-call | bytes 800000000 | tf_op jit(solution)/shard_map/pallas_call | solution.py:1315
  1168.0 9.3 fusion.105
  1212.9 297.5 %shard_map.443 = (f32[2,864,1152]{2,1,0:T(8,128)}, f32[4,456,1152]{2,1,0:T(8,128)}) custom-call(f32[8,864,1152]{2,1,0:T(8,128)} %shard_map.442.chunks, f32[456,1152]{1,0:T(8,128)} %fusion.49.beside), custom_call_target="tpu_custom_call" | custom-call | bytes 800000000 | tf_op jit(solution)/shard_map/pallas_call | solution.py:1315
  1545.1 19.8 %shard_map.446 = (f32[10368,128]{1,0:T(8,128)}, f32[10368,128]{1,0:T(8,128)}, f32[10368,128]{1,0:T(8,128)}, f32[10368,128]{1,0:T(8,128)}) custom-call(s32[4,3]{1,0:T(4,128)S(1)} %fusion.173.table, f32[1]{0:T(128)} %bitcast.117.factor, f32[1152,1152]{1,0:T(8,128)} %bitcast.380, f32[10368,128]{1,0:T(8,128)} %bitcast.354, f32[10368,128]{1,0:T(8,128)} %bitcast.389, ...), custom_call_target="tpu_custom_call" | custom-call | tf_op jit(solution)/shard_map/pallas_call | solution.py:1555
  1564.9 28.3 %shard_map.445 = (f32[15552,128]{1,0:T(8,128)}, f32[15552,128]{1,0:T(8,128)}, f32[15552,128]{1,0:T(8,128)}, f32[15552,128]{1,0:T(8,128)}) custom-call(s32[6,3]{1,0:T(8,128)S(1)} %copy.204.table, f32[1]{0:T(128)} %bitcast.117.factor, f32[1728,1152]{1,0:T(8,128)} %bitcast.379, f32[15552,128]{1,0:T(8,128)} %bitcast.352, f32[15552,128]{1,0:T(8,128)} %bitcast.385, ...), custom_call_target="tpu_custom_call" | custom-call | tf_op jit(solution)/shard_map/pallas_call | solution.py:1555
  1593.2 25.0 %multiply_add_fusion.1 = (f32[2019840]{0:T(1024)}, f32[2019840]{0:T(1024)}, f32[2019840]{0:T(1024)}, f32[2019840]{0:T(1024)}) fusion(f32[2019840]{0:T(1024)} %param.49, f32[2019840]{0:T(1024)S(1)} %bitcast.351, f32[]{:T(128)} %min.7, f32[16416,128]{1,0:T(8,128)} %copy-done.2, s32[]{:T(128)S(6)} %select_n.243, f32[2019840]{0:T(1024)} %param.41, f32[2019840]{0:T(1024)} %param.45), kind=kLoop, calls=%fused_computation.27 | loop fusion | flops 36357120 | bytes 72714248 | tf_op jit(solution)/shard_map/add | solution.py:209
  (703 shorter events, 436.9 us)
Async XLA Ops:
  413.7 19.9 %collective-permute-start = (f32[48,1152]{1,0:T(8,128)}, f32[48,1152]{1,0:T(8,128)}, u32[]{:S(2)}, u32[]{:S(2)}) collective-permute-start(f32[48,1152]{1,0:T(8,128)} %fusion.227), channel_id=1, source_target_pairs={{0,1},{1,0},{2,3},{3,2},{4,5},{5,4},{6,7},{7,6},{8,9},{9,8},{10,11... | collective-permute-start | bytes 663560 | tf_op jit(solution)/shard_map/ppermute | solution.py:573
  435.9 22.4 %collective-permute-start.1 = (f32[48,1152]{1,0:T(8,128)}, f32[48,1152]{1,0:T(8,128)}, u32[]{:S(2)}, u32[]{:S(2)}) collective-permute-start(f32[48,1152]{1,0:T(8,128)} %add.742), channel_id=1, source_target_pairs={{0,2},{1,3},{2,0},{3,1},{4,6},{5,7},{6,4},{7,5},{8,10},{9,11},{10,... | collective-permute-start | bytes 663560 | tf_op jit(solution)/shard_map/ppermute | solution.py:573
  459.3 14.8 collective-permute-start.2
  499.2 19.6 %all-to-all-start = ((bf16[1,2,256,1152]{3,1,0,2:T(2,128)(2,1)}), bf16[1,2,256,1152]{3,1,0,2:T(2,128)(2,1)S(1)}, u32[]{:S(2)}, u32[]{:S(2)}) async-start(bf16[1,2,256,1152]{3,1,0,2:T(2,128)(2,1)} %copy.177), calls=%async_computation | async-start | bytes 2359296 | tf_op jit(solution)/shard_map/all_to_all | solution.py:1921
  534.9 20.6 %all-to-all-start.1 = ((bf16[1,8,64,1152]{3,2,0,1:T(8,128)(2,1)}), bf16[1,8,64,1152]{3,2,0,1:T(8,128)(2,1)}, u32[]{:S(2)}, u32[]{:S(2)}) async-start(bf16[1,8,64,1152]{3,2,0,1:T(8,128)(2,1)} %bitcast.397), calls=%async_computation.1 | async-start | bytes 2359296 | tf_op jit(solution)/shard_map/all_to_all | solution.py:1929
  670.5 20.7 %all-to-all-start.2 = ((bf16[1,2,256,1152]{3,1,0,2:T(2,128)(2,1)}), bf16[1,2,256,1152]{3,1,0,2:T(2,128)(2,1)}, u32[]{:S(2)}, u32[]{:S(2)}) async-start(bf16[1,2,256,1152]{3,1,0,2:T(2,128)(2,1)} %copy.190), calls=%async_computation.2 | async-start | bytes 2359296 | tf_op jit(solution)/shard_map/all_to_all | solution.py:2036
  677.7 45.1 %collective-permute-start.8 = (f32[120,2304]{1,0:T(8,128)}, f32[120,2304]{1,0:T(8,128)}, u32[]{:S(2)}, u32[]{:S(2)}) collective-permute-start(f32[120,2304]{1,0:T(8,128)} %get-tuple-element.129), channel_id=1, source_target_pairs={{0,16},{1,17},{2,18},{3,19},{4,20},{5,21},{6,22},{7,23},{8,24},{9,... | collective-permute-start | bytes 3317768 | tf_op jit(solution)/shard_map/ppermute | solution.py:573
  717.7 62.2 %all-to-all-start.3 = ((bf16[1,8,64,3456]{3,2,0,1:T(8,128)(2,1)}), bf16[1,8,64,3456]{3,2,0,1:T(8,128)(2,1)}, u32[]{:S(2)}, u32[]{:S(2)}) async-start(bf16[1,8,64,3456]{3,2,0,1:T(8,128)(2,1)} %maximum_bitcast_fusion), calls=%async_computation.3 | async-start | bytes 7077888 | tf_op jit(solution)/shard_map/all_to_all | solution.py:2051
  722.6 442.7 %all-gather.2.cloned.1.call-start = ((), (), s32[]{:S(2)}) async-start(), calls=%async_computation.4 | async-start | bytes 9953280 | tf_op jit(solution)/shard_map/all_gather | solution.py:2091
  743.2 35.4 %collective-permute-start.10 = (bf16[1152,512]{1,0:T(8,128)(2,1)}, bf16[1152,512]{1,0:T(8,128)(2,1)}, u32[]{:S(2)}, u32[]{:S(2)}) collective-permute-start(bf16[1152,512]{1,0:T(8,128)(2,1)} %bitcast.90.refs_2_), channel_id=1, source_target_pairs={{0,8},{1,9},{2,10},{3,11},{4,12},{5,13},{6,14},{7,15},{8,0},{9,1},... | collective-permute-start | bytes 3538952 | tf_op jit(solution)/shard_map/ppermute | solution.py:573
  743.6 38.7 %collective-permute-start.9 = (bf16[1152,512]{1,0:T(8,128)(2,1)}, bf16[1152,512]{1,0:T(8,128)(2,1)}, u32[]{:S(2)}, u32[]{:S(2)}) collective-permute-start(bf16[1152,512]{1,0:T(8,128)(2,1)} %bitcast.89.refs_0_), channel_id=1, source_target_pairs={{0,8},{1,9},{2,10},{3,11},{4,12},{5,13},{6,14},{7,15},{8,0},{9,1},... | collective-permute-start | bytes 3538952 | tf_op jit(solution)/shard_map/ppermute | solution.py:573
  745.9 37.0 %collective-permute-start.11 = (bf16[1152,512]{1,0:T(8,128)(2,1)}, bf16[1152,512]{1,0:T(8,128)(2,1)}, u32[]{:S(2)}, u32[]{:S(2)}) collective-permute-start(bf16[1152,512]{1,0:T(8,128)(2,1)} %bitcast.91.refs_4_), channel_id=1, source_target_pairs={{0,8},{1,9},{2,10},{3,11},{4,12},{5,13},{6,14},{7,15},{8,0},{9,1},... | collective-permute-start | bytes 3538952 | tf_op jit(solution)/shard_map/ppermute | solution.py:573
  746.3 47.7 %collective-permute-start.16 = (bf16[512,1152]{1,0:T(8,128)(2,1)S(1)}, bf16[512,1152]{1,0:T(8,128)(2,1)}, u32[]{:S(2)}, u32[]{:S(2)}) collective-permute-start(bf16[512,1152]{1,0:T(8,128)(2,1)S(1)} %copy-done.14), channel_id=1, source_target_pairs={{0,8},{1,9},{2,10},{3,11},{4,12},{5,13},{6,14},{7,15},{8,0},{9,1},... | collective-permute-start | bytes 3538952 | tf_op jit(solution)/shard_map/ppermute | solution.py:573
  749.0 34.0 %collective-permute-start.17 = (bf16[512,1152]{1,0:T(8,128)(2,1)}, bf16[512,1152]{1,0:T(8,128)(2,1)}, u32[]{:S(2)}, u32[]{:S(2)}) collective-permute-start(bf16[512,1152]{1,0:T(8,128)(2,1)} %bitcast.403), channel_id=1, source_target_pairs={{0,8},{1,9},{2,10},{3,11},{4,12},{5,13},{6,14},{7,15},{8,0},{9,1},... | collective-permute-start | bytes 3538952 | tf_op jit(solution)/shard_map/ppermute | solution.py:573
  778.6 15.8 collective-permute-start.15
  782.3 29.7 %collective-permute-start.14 = (bf16[1152,512]{1,0:T(8,128)(2,1)S(1)}, bf16[1152,512]{1,0:T(8,128)(2,1)S(1)}, u32[]{:S(2)}, u32[]{:S(2)}) collective-permute-start(bf16[1152,512]{1,0:T(8,128)(2,1)S(1)} %bitcast.367), channel_id=1, source_target_pairs={{0,8},{1,9},{2,10},{3,11},{4,12},{5,13},{6,14},{7,15},{8,0},{9,1},... | collective-permute-start | bytes 3538952 | tf_op jit(solution)/shard_map/ppermute | solution.py:573
  782.8 30.6 %collective-permute-start.13 = (bf16[1152,512]{1,0:T(8,128)(2,1)S(1)}, bf16[1152,512]{1,0:T(8,128)(2,1)S(1)}, u32[]{:S(2)}, u32[]{:S(2)}) collective-permute-start(bf16[1152,512]{1,0:T(8,128)(2,1)S(1)} %bitcast.369), channel_id=1, source_target_pairs={{0,8},{1,9},{2,10},{3,11},{4,12},{5,13},{6,14},{7,15},{8,0},{9,1},... | collective-permute-start | bytes 3538952 | tf_op jit(solution)/shard_map/ppermute | solution.py:573
  783.0 32.0 %collective-permute-start.12 = (bf16[1152,512]{1,0:T(8,128)(2,1)S(1)}, bf16[1152,512]{1,0:T(8,128)(2,1)S(1)}, u32[]{:S(2)}, u32[]{:S(2)}) collective-permute-start(bf16[1152,512]{1,0:T(8,128)(2,1)S(1)} %bitcast.371), channel_id=1, source_target_pairs={{0,8},{1,9},{2,10},{3,11},{4,12},{5,13},{6,14},{7,15},{8,0},{9,1},... | collective-permute-start | bytes 3538952 | tf_op jit(solution)/shard_map/ppermute | solution.py:573
  794.0 105.6 %collective-permute-start.5 = (bf16[512,4608]{1,0:T(8,128)(2,1)}, bf16[512,4608]{1,0:T(8,128)(2,1)}, u32[]{:S(2)}, u32[]{:S(2)}) collective-permute-start(bf16[512,4608]{1,0:T(8,128)(2,1)} %bitcast.55.refs_4_), channel_id=1, source_target_pairs={{0,8},{1,9},{2,10},{3,11},{4,12},{5,13},{6,14},{7,15},{8,0},{9,1},... | collective-permute-start | bytes 14155784 | tf_op jit(solution)/shard_map/ppermute | solution.py:573
  794.4 105.2 %collective-permute-start.4 = (bf16[4608,512]{1,0:T(8,128)(2,1)}, bf16[4608,512]{1,0:T(8,128)(2,1)}, u32[]{:S(2)}, u32[]{:S(2)}) collective-permute-start(bf16[4608,512]{1,0:T(8,128)(2,1)} %bitcast.46.refs_2_), channel_id=1, source_target_pairs={{0,8},{1,9},{2,10},{3,11},{4,12},{5,13},{6,14},{7,15},{8,0},{9,1},... | collective-permute-start | bytes 14155784 | tf_op jit(solution)/shard_map/ppermute | solution.py:573
  813.1 15.1 collective-permute-start.18
  833.8 65.8 %collective-permute-start.6 = (bf16[512,1152]{1,0:T(8,128)(2,1)S(1)}, bf16[512,1152]{1,0:T(8,128)(2,1)}, u32[]{:S(2)}, u32[]{:S(2)}) collective-permute-start(bf16[512,1152]{1,0:T(8,128)(2,1)S(1)} %bitcast.361), channel_id=1, source_target_pairs={{0,8},{1,9},{2,10},{3,11},{4,12},{5,13},{6,14},{7,15},{8,0},{9,1},... | collective-permute-start | bytes 3538952 | tf_op jit(solution)/shard_map/ppermute | solution.py:573
  834.9 64.7 %collective-permute-start.3 = (bf16[1152,512]{1,0:T(8,128)(2,1)S(1)}, bf16[1152,512]{1,0:T(8,128)(2,1)}, u32[]{:S(2)}, u32[]{:S(2)}) collective-permute-start(bf16[1152,512]{1,0:T(8,128)(2,1)S(1)} %bitcast.363), channel_id=1, source_target_pairs={{0,8},{1,9},{2,10},{3,11},{4,12},{5,13},{6,14},{7,15},{8,0},{9,1},... | collective-permute-start | bytes 3538952 | tf_op jit(solution)/shard_map/ppermute | solution.py:573
  835.4 21.4 %collective-permute-start.21 = (bf16[512,1152]{1,0:T(8,128)(2,1)}, bf16[512,1152]{1,0:T(8,128)(2,1)}, u32[]{:S(2)}, u32[]{:S(2)}) collective-permute-start(bf16[512,1152]{1,0:T(8,128)(2,1)} %bitcast.73.refs_26_), channel_id=1, source_target_pairs={{0,8},{1,9},{2,10},{3,11},{4,12},{5,13},{6,14},{7,15},{8,0},{9,1},... | collective-permute-start | bytes 3538952 | tf_op jit(solution)/shard_map/ppermute | solution.py:573
  (191 other events, 1819.8 us)
Sparse Core Ops, SparseCore 0:
  737.7 131.9 all-gather.1
